TPU v7x, 32 devices: a whole 2x2x4 slice. The times are simulated.
32 devices in a mesh: lat: 4 (over x, core), lon: 8 (over z, y).
Axes of the slice: x: 2, y: 2, z: 4, core: 2. Of those that a mesh axis runs over, the one named last changes fastest.
Arguments:
- features: float32 [4, 24, 96, 192], P(None, 'lat', 'lon'), may hold values from -460 to 460
- cotangent: float32 [4, 24, 96, 192], P(None, 'lat', 'lon'), may hold values from -6 to 6
- norm_gain: float32 [192], replicated, may hold values from 0.1 to 1.9
- norm_shift: float32 [192], replicated, may hold values from -3 to 3
- qkv_weight: float32 [192, 576], replicated, may hold values from -0.4375 to 0.4375
- out_weight: float32 [192, 192], replicated, may hold values from -0.4375 to 0.4375
- bias_table: float32 [4, 2, 6, 23, 144], P('lat'), may hold values from -6 to 305
Outputs:
- grad_features: float32 [4, 24, 96, 192], P(None, 'lat', 'lon')
- grad_weights: float32 [192, 768], P('lat', 'lon')
- grad_bias: float32 [4, 2, 6, 23, 144], P('lat')
- grad_norm: float32 [2, 192], replicated
All inputs are finite; a program needn't handle non-finite values.
Results may differ from a plain program's by a relative error of at most 0.0003.
Values sent between devices are 32-bit elements; how exact they have to be, the bound alone decides.
No kernel may reach another device: no remote copies, remote signals or barrier semaphores. Data moves between devices by JAX's collectives and lax.ppermute only.
A program may use at most 128 MiB of HBM per device.

v0:
```python
import math

import jax
import jax.numpy as jnp
from jax import lax
from jax.sharding import PartitionSpec as P

D = 192
HEADS = 6
HEAD = 32
ZP = 4
WZ = 2
WLAT = 6
WLON = 12
PW = 2
WIN = 144
LONREL = 23
PAIRS = 144


EPSILON = 1e-05
HIGH = lax.Precision.HIGHEST


def passed_along(value, axis, steps):
    count = lax.axis_size(axis)
    pairs = [(source, (source + steps) % count) for source in range(count)]
    return lax.ppermute(value, axis, pairs)


def offset_table():
    columns = jnp.arange(WLON, dtype=jnp.int32)
    offset = columns[None, :] - columns[:, None] + (WLON - 1)
    return (offset[:, :, None] == jnp.arange(LONREL, dtype=jnp.int32)[None, None, :]).astype(
        jnp.float32
    )


def level_valid():
    level = jnp.arange(WIN, dtype=jnp.int32) // (WLAT * WLON)
    same_level = level[:, None] == level[None, :]
    window_index = jnp.arange(PW, dtype=jnp.int32)[:, None, None]
    return (window_index > 0) | same_level[None, :, :]


def shards(features, cotangent, norm_gain, norm_shift, qkv_weight, out_weight, bias_table):
    half_cols = WLON // 2
    lat_blocks = features.shape[1] // WLAT
    lon_blocks = features.shape[2] // WLON
    onehot = offset_table()
    score_scale = HEAD ** (-0.5)
    average = jnp.mean(features, -1, keepdims=True)
    centred = features - average
    inverse = lax.rsqrt(jnp.mean(centred * centred, -1, keepdims=True) + EPSILON)
    standard = centred * inverse
    normed = standard * norm_gain + norm_shift
    lifted = jnp.roll(normed, 1, 0)
    upstream = jnp.roll(cotangent, 1, 0)
    borrowed, borrowed_grad = passed_along(
        (lifted[:, :, -half_cols:], upstream[:, :, -half_cols:]), "lon", 1
    )
    joined = jnp.concatenate([borrowed, lifted[:, :, :-half_cols]], axis=2)
    joined_grad = jnp.concatenate([borrowed_grad, upstream[:, :, :-half_cols]], axis=2)

    def to_windows(grid_block):
        shaped = grid_block.reshape(PW, WZ, lat_blocks, WLAT, lon_blocks, WLON, D)
        return shaped.transpose(0, 2, 4, 1, 3, 5, 6).reshape(PW, lat_blocks, lon_blocks, WIN, D)

    def split_heads(tensor):
        return tensor.reshape(PW, lat_blocks, lon_blocks, WIN, HEADS, HEAD)

    hidden_win = to_windows(joined)
    grad_win = to_windows(joined_grad)
    projected = jnp.einsum("plnwd,de->plnwe", hidden_win, qkv_weight, precision=HIGH)
    query_heads = split_heads(projected[..., :D])
    key_heads = split_heads(projected[..., D : 2 * D])
    value_heads = split_heads(projected[..., 2 * D :])
    split_table = bias_table.reshape(lat_blocks, PW, HEADS, LONREL, WZ, WZ, WLAT, WLAT)
    bias_full = jnp.einsum("lchrijab,xyr->clhiaxjby", split_table, onehot, precision=HIGH)
    bias_full = bias_full.reshape(PW, lat_blocks, HEADS, WIN, WIN)
    bias_masked = jnp.where(level_valid()[:, None, None], bias_full, -jnp.inf)
    scores = (
        jnp.einsum("plnahe,plnbhe->plnhab", query_heads, key_heads, precision=HIGH) * score_scale
        + bias_masked[:, :, None]
    )
    row_max = jnp.max(scores, axis=-1, keepdims=True)
    exponent = jnp.exp(scores - row_max)
    attention = exponent * (1.0 / jnp.sum(exponent, axis=-1, keepdims=True))
    mixture = jnp.einsum("plnhab,plnbhe->plnahe", attention, value_heads, precision=HIGH).reshape(
        PW, lat_blocks, lon_blocks, WIN, D
    )
    grad_out_w = jnp.einsum("plnwd,plnwe->de", mixture, grad_win, precision=HIGH)
    grad_mixture = split_heads(jnp.einsum("plnwe,de->plnwd", grad_win, out_weight, precision=HIGH))
    grad_attention = jnp.einsum("plnahe,plnbhe->plnhab", grad_mixture, value_heads, precision=HIGH)
    grad_values = jnp.einsum("plnhab,plnahe->plnbhe", attention, grad_mixture, precision=HIGH)
    grad_scores = attention * (
        grad_attention - jnp.sum(attention * grad_attention, axis=-1, keepdims=True)
    )
    grad_queries = (
        jnp.einsum("plnhab,plnbhe->plnahe", grad_scores, key_heads, precision=HIGH) * score_scale
    )
    grad_keys = (
        jnp.einsum("plnhab,plnahe->plnbhe", grad_scores, query_heads, precision=HIGH) * score_scale
    )
    merged_shape = (PW, lat_blocks, lon_blocks, WIN, D)
    grad_projected = jnp.concatenate(
        [
            grad_queries.reshape(merged_shape),
            grad_keys.reshape(merged_shape),
            grad_values.reshape(merged_shape),
        ],
        axis=-1,
    )
    grad_qkv_w = jnp.einsum("plnwd,plnwe->de", hidden_win, grad_projected, precision=HIGH)
    grad_hidden = jnp.einsum("plnwe,de->plnwd", grad_projected, qkv_weight, precision=HIGH)
    score_sum = jnp.sum(grad_scores, axis=2).reshape(
        PW, lat_blocks, HEADS, WZ, WLAT, WLON, WZ, WLAT, WLON
    )
    bias_local = jnp.einsum("clhiaxjby,xyr->lchrijab", score_sum, onehot, precision=HIGH)
    bias_local = bias_local.reshape(lat_blocks, PW, HEADS, LONREL, PAIRS)
    shaped = grad_hidden.reshape(PW, lat_blocks, lon_blocks, WZ, WLAT, WLON, D)
    back_block = shaped.transpose(0, 3, 1, 4, 2, 5, 6).reshape(
        ZP, lat_blocks * WLAT, lon_blocks * WLON, D
    )
    returned = passed_along(back_block[:, :, :half_cols], "lon", -1)
    grad_lifted = jnp.concatenate([back_block[:, :, half_cols:], returned], axis=2)
    grad_normed = jnp.roll(grad_lifted, -1, 0)
    grad_unit = grad_normed * norm_gain
    grad_features = cotangent + inverse * (
        grad_unit
        - jnp.mean(grad_unit, -1, keepdims=True)
        - standard * jnp.mean(grad_unit * standard, -1, keepdims=True)
    )
    token_count = (
        ZP * features.shape[1] * features.shape[2] * lax.axis_size("lat") * lax.axis_size("lon")
    )
    factor = 1.0 / math.sqrt(token_count)
    norm_local = (
        jnp.stack(
            [jnp.sum(grad_normed * standard, axis=(0, 1, 2)), jnp.sum(grad_normed, axis=(0, 1, 2))]
        )
        * factor
    )
    weights_local = jnp.concatenate([grad_qkv_w, grad_out_w], axis=1) * factor
    grad_bias = lax.psum(bias_local, "lon")
    grad_norm = lax.psum(norm_local, ("lat", "lon"))
    column_part = lax.psum_scatter(weights_local, "lon", scatter_dimension=1, tiled=True)
    grad_weights = lax.psum_scatter(column_part, "lat", scatter_dimension=0, tiled=True)
    return (grad_features, grad_weights, grad_bias, grad_norm)


def solution(mesh):
    placed = (
        P(None, "lat", "lon", None),
        P(None, "lat", "lon", None),
        P(),
        P(),
        P(),
        P(),
        P("lat", None, None, None, None),
    )
    return jax.shard_map(
        shards,
        mesh=mesh,
        in_specs=placed,
        out_specs=(
            P(None, "lat", "lon", None),
            P("lat", "lon"),
            P("lat", None, None, None, None),
            P(),
        ),
        check_vma=False,
    )
```

profile of v0, /device:TPU:0, one launch (start us, length us, event | category | flops | bytes accessed | tf_op | source)
XLA Modules:
  0.0 257.8 jit_solution(9279043541099613881)
XLA Ops:
  7.2 1.1 slice.55
  8.3 1.0 fusion.29
  9.4 3.0 %collective-permute-start.1 = (f32[4,6,6,192]{3,0,2,1:T(4,128)S(1)}, f32[4,6,6,192]{3,0,2,1:T(4,128)S(1)}, u32[]{:S(2)}, u32[]{:S(2)}) collective-permute-start(f32[4,6,6,192]{3,0,2,1:T(4,128)S(1)} %fusion.29), channel_id=1, source_target_pairs={{0,1},{1,2},{2,3},{3,4},{4,5},{5,6},{6,7},{7,0},{8,9},{9,10},{10,1... | collective-permute-start | bytes 331784 | tf_op jit(solution)/shard_map/ppermute | solution.py:28
  12.4 1.1 reduce_sum.93
  13.5 0.1 copy.122
  13.6 1.2 fusion.23
  14.9 1.1 multiply_add_fusion
  16.1 1.6 collective-permute-start
  17.7 0.6 copy.128
  18.3 0.1 broadcast_compare_fusion
  18.4 8.9 %convolution_bitcast_fusion = f32[2,1,6,2,6,12,2,6,12]{8,7,4,6,3,2,0,5,1:T(8,128)} fusion(f32[2,6,23,2,2,6,6]{2,0,6,5,4,3,1:T(2,128)S(1)} %bitcast.103, s32[12,12]{1,0:T(8,128)S(1)} %subtract_add_fusion), kind=kOutput, calls=%fused_computation | convolution fusion | flops 68680944 | bytes 1154880 | tf_op jit(solution)/shard_map/lchrijab,xyr->clhiaxjby/dot_general | solution.py:79
  27.3 0.1 broadcast_or_fusion
  27.4 20.7 %copy.165 = f32[2,1,6,2,6,12,2,6,12]{5,4,3,8,7,6,2,0,1:T(8,128)} copy(f32[2,1,6,2,6,12,2,6,12]{8,7,4,6,3,2,0,5,1:T(8,128)} %convolution_bitcast_fusion) | data formatting | bytes 1990656 | tf_op jit(solution)/shard_map/reshape | solution.py:80
  48.0 10.3 %reshape.280 = f32[2,6,144,144]{2,3,1,0:T(8,128)} reshape(f32[2,1,6,2,6,12,2,6,12]{5,4,3,8,7,6,2,0,1:T(8,128)} %copy.165) | data formatting | bytes 1990656 | tf_op jit(solution)/shard_map/reshape | solution.py:80
  58.3 0.1 fusion.25
  58.4 0.1 copy.132
  58.5 0.8 reshape.274
  59.3 0.1 fusion.20
  59.5 0.9 convolution_bitcast_fusion.2
  60.3 0.8 fusion.41
  61.2 0.2 copy.127
  61.4 0.2 copy.126
  61.5 3.4 %fusion.43 = (f32[2,6,144]{2,1,0:T(8,128)S(1)}, f32[2,6,144,144]{2,3,1,0:T(8,128)S(1)}) fusion(f32[2,6,144,144]{2,3,1,0:T(8,128)} %reshape.280, pred[2,144,144]{1,2,0:T(8,128)(4,1)S(1)} %broadcast_or_fusion, f32[2,144,6,32]{1,3,2,0:T(8,128)S(1)} %bitcast.104, f32[2,144,6,32]{1,3,2,0:T(8,128)S(1)} %bitcast.106), kind=kOutput, calls=%fused_computation.82 | convolution fusion | flops 96545088 | bytes 2481408 | tf_op jit(solution)/shard_map/plnahe,plnbhe->plnhab/dot_general | solution.py:83
  65.0 0.3 fusion.1
  65.3 1.1 copy.133
  66.4 1.5 fusion.26
  67.9 2.7 %fusion.12 = f32[2,6,32,144]{3,2,1,0:T(8,128)} fusion(f32[2,144,6,32]{1,3,2,0:T(8,128)S(1)} %fusion.26, f32[2,6,144,144]{2,3,1,0:T(8,128)S(1)} %get-tuple-element.37, f32[2,6,144]{2,1,0:T(8,128)S(1)} %broadcast_divide_fusion, f32[2,6,144]{2,1,0:T(8,128)S(1)} %get-tuple-element.36), kind=kOutput, calls=%fused_computation.22 | convolution fusion | flops 96049152 | bytes 1451520 | tf_op jit(solution)/shard_map/plnhab,plnahe->plnbhe/dot_general | solution.py:95
  70.7 2.0 multiply_reduce_fusion
  72.6 0.5 subtract_multiply_fusion
  73.2 2.5 convolution_multiply_fusion
  75.7 1.8 convolution_multiply_fusion.1
  77.5 2.0 fusion.10
  79.5 1.1 reshape.262
  80.6 0.2 copy.147
  80.8 1.4 copy.146
  82.2 0.2 copy.145
  82.4 0.5 convolution_bitcast_fusion.4
  83.0 1.2 convolution_bitcast_fusion.3
  84.2 1.0 maximum_multiply_fusion
  85.2 2.2 copy.168
  87.5 8.6 %reshape.282 = f32[2,6,2,6,12,2,6,12]{4,3,2,7,6,5,1,0:T(8,128)} reshape(f32[2,6,144,144]{2,3,1,0:T(8,128)S(1)} %copy-done.2) | data formatting | bytes 1990656 | tf_op jit(solution)/shard_map/reshape.58
  96.1 0.5 copy.139
  96.6 0.3 concatenate.41
  96.8 0.2 copy-done.6
  97.1 0.5 copy.137
  97.5 0.3 concatenate.40
  97.8 0.5 copy.135
  98.3 0.3 concatenate.39
  98.6 1.1 fusion.4
  99.8 3.3 %collective-permute-start.2 = (f32[4,6,6,192]{3,2,1,0:T(8,128)S(1)}, f32[4,6,6,192]{3,2,1,0:T(8,128)S(1)}, u32[]{:S(2)}, u32[]{:S(2)}) collective-permute-start(f32[4,6,6,192]{3,2,1,0:T(8,128)S(1)} %get-tuple-element.35), channel_id=1, source_target_pairs={{0,7},{1,0},{2,1},{3,2},{4,3},{5,4},{6,5},{7,6},{8,15},{9,8},{10,9... | collective-permute-start | bytes 331784 | tf_op jit(solution)/shard_map/ppermute | solution.py:28
  103.0 20.1 %copy.151 = f32[2,6,2,6,12,2,6,12]{7,6,4,5,3,2,1,0:T(8,128)} copy(f32[2,6,2,6,12,2,6,12]{4,3,2,7,6,5,1,0:T(8,128)} %reshape.282) | data formatting | bytes 1990656 | tf_op jit(solution)/shard_map/reshape.58
  123.1 13.0 %convolution_bitcast_fusion.1 = f32[1,2,6,23,2,2,6,6]{3,7,5,6,4,2,1,0:T(8,128)S(1)} fusion(f32[2,6,2,6,12,2,6,12]{7,6,4,5,3,2,1,0:T(8,128)} %copy.151, s32[12,12]{1,0:T(8,128)S(1)} %subtract_add_fusion), kind=kOutput, calls=%fused_computation.7 | convolution fusion | flops 68680944 | bytes 1154880 | tf_op jit(solution)/shard_map/clhiaxjby,xyr->lchrijab/dot_general | solution.py:119
  136.1 1.6 copy.152
  137.8 0.0 reduce-scatter.5.cloned.1.call-start
  137.9 0.1 fusion.39
  138.0 0.4 multiply_reduce_fusion.1
  138.4 12.1 %reduce-scatter.7.cloned.1.call-done = f32[96,192]{1,0:T(8,128)} async-done(((f32[768,192]{1,0:T(8,128)}), f32[96,192]{1,0:T(8,128)}) %reduce-scatter.7.cloned.1.call-update) | async-done | bytes 73744
  150.5 1.6 copy.169
  152.2 0.3 copy_add_fusion
  152.5 0.9 copy.153
  153.4 40.2 %psum.15 = f32[2,192]{1,0:T(2,128)} all-reduce(f32[2,192]{1,0:T(2,128)S(1)} %maximum_multiply_fusion.1), channel_id=1, replica_groups=mesh['lat'=4,'lon'=8] {'lat','lon'}, use_global_device_ids=true, to_apply=%region_13.14 | all-reduce | flops 384 | bytes 3072 | tf_op jit(solution)/shard_map/psum | solution.py:146
  193.6 35.7 %all-reduce.2.cloned.1.call-done = f32[1,2,6,23,144]{3,1,4,2,0:T(2,128)} async-done(((f32[1,2,6,23,144]{3,1,4,2,0:T(2,128)}), f32[1,2,6,23,144]{3,1,4,2,0:T(2,128)}) %all-reduce.2.cloned.1.call-update) | async-done | bytes 158992 | tf_op jit(solution)/shard_map/psum | solution.py:145
  229.4 2.2 copy.154
  231.6 19.7 %reduce-scatter.5.cloned.1.call-done = f32[48,96]{1,0:T(8,128)} async-done(((f32[192,96]{1,0:T(8,128)}), f32[48,96]{1,0:T(8,128)}) %reduce-scatter.5.cloned.1.call-update) | async-done | bytes 18448 | tf_op jit(solution)/shard_map/reduce_scatter | solution.py:148
  (52 shorter events, 0.4 us)
Async XLA Ops:
  7.2 52.3 %copy-start = (f32[192,576]{1,0:T(8,128)S(1)}, f32[192,576]{1,0:T(8,128)}, u32[]{:S(2)}) copy-start(f32[192,576]{1,0:T(8,128)} %param.11) | copy-start | bytes 1327108
  7.2 143.3 %reduce-scatter.7.cloned.1.call-start = ((), (), s32[]{:S(2)}) async-start(), calls=%async_computation.4 | async-start | bytes 884736
  8.3 9.4 %copy-start.13 = (f32[1,2,6,23,144]{4,1,3,2,0:T(2,128)S(1)}, f32[1,2,6,23,144]{4,1,3,2,0:T(2,128)}, u32[]{:S(2)}) copy-start(f32[1,2,6,23,144]{4,1,3,2,0:T(2,128)} %param.13) | copy-start | bytes 476932
  9.4 49.0 %collective-permute-start.1 = (f32[4,6,6,192]{3,0,2,1:T(4,128)S(1)}, f32[4,6,6,192]{3,0,2,1:T(4,128)S(1)}, u32[]{:S(2)}, u32[]{:S(2)}) collective-permute-start(f32[4,6,6,192]{3,0,2,1:T(4,128)S(1)} %fusion.29), channel_id=1, source_target_pairs={{0,1},{1,2},{2,3},{3,4},{4,5},{5,6},{6,7},{7,0},{8,9},{9,10},{10,1... | collective-permute-start | bytes 331784 | tf_op jit(solution)/shard_map/ppermute | solution.py:28
  16.1 43.2 %collective-permute-start = (f32[4,6,6,192]{3,2,1,0:T(8,128)S(1)}, f32[4,6,6,192]{3,2,1,0:T(8,128)S(1)}, u32[]{:S(2)}, u32[]{:S(2)}) collective-permute-start(f32[4,6,6,192]{3,2,1,0:T(8,128)S(1)} %fusion.28), channel_id=1, source_target_pairs={{0,1},{1,2},{2,3},{3,4},{4,5},{5,6},{6,7},{7,0},{8,9},{9,10},{10,1... | collective-permute-start | bytes 331784 | tf_op jit(solution)/shard_map/ppermute | solution.py:28
  48.0 10.3 %copy-start.8 = (f32[4,6,12,192]{3,0,2,1:T(4,128)S(1)}, f32[4,6,12,192]{3,0,2,1:T(4,128)}, u32[]{:S(2)}) copy-start(f32[4,6,12,192]{3,0,2,1:T(4,128)} %param.8) | copy-start | bytes 663556
  58.5 1.8 copy-start.7
  59.5 1.9 copy-start.10
  73.1 4.3 %copy-start.1 = (f32[2,6,144,144]{2,3,1,0:T(8,128)}, f32[2,6,144,144]{2,3,1,0:T(8,128)S(1)}, u32[]{:S(2)}) copy-start(f32[2,6,144,144]{2,3,1,0:T(8,128)S(1)} %subtract_multiply_fusion) | copy-start | bytes 2985988
  77.5 3.2 %copy-start.4 = (f32[2,6,32,144]{3,2,1,0:T(8,128)S(1)}, f32[2,6,32,144]{3,2,1,0:T(8,128)}, u32[]{:S(2)}) copy-start(f32[2,6,32,144]{3,2,1,0:T(8,128)} %fusion.12) | copy-start | bytes 663556
  77.5 4.7 %copy-start.5 = (f32[2,6,32,144]{3,2,1,0:T(8,128)S(1)}, f32[2,6,32,144]{3,2,1,0:T(8,128)}, u32[]{:S(2)}) copy-start(f32[2,6,32,144]{3,2,1,0:T(8,128)} %convolution_multiply_fusion.1) | copy-start | bytes 663556
  79.5 2.9 %copy-start.12 = (f32[2,6,32,144]{3,2,1,0:T(8,128)S(1)}, f32[2,6,32,144]{3,2,1,0:T(8,128)}, u32[]{:S(2)}) copy-start(f32[2,6,32,144]{3,2,1,0:T(8,128)} %fusion.10) | copy-start | bytes 663556
  79.5 3.4 %copy-start.11 = (f32[2,144,192]{2,1,0:T(8,128)S(1)}, f32[2,144,192]{2,1,0:T(8,128)}, u32[]{:S(2)}) copy-start(f32[2,144,192]{2,1,0:T(8,128)} %copy-done.10) | copy-start | bytes 663556
  84.2 3.3 %copy-start.2 = (f32[2,6,144,144]{2,3,1,0:T(8,128)S(1)}, f32[2,6,144,144]{2,3,1,0:T(8,128)}, u32[]{:S(2)}) copy-start(f32[2,6,144,144]{2,3,1,0:T(8,128)} %copy-done.1) | copy-start | bytes 2985988
  87.4 142.0 %all-reduce.2.cloned.1.call-start = ((), (), s32[]{:S(2)}) async-start(), calls=%async_computation.3 | async-start | bytes 1769472 | tf_op jit(solution)/shard_map/psum | solution.py:145
  96.1 1.0 copy-start.6
  99.8 38.1 %collective-permute-start.2 = (f32[4,6,6,192]{3,2,1,0:T(8,128)S(1)}, f32[4,6,6,192]{3,2,1,0:T(8,128)S(1)}, u32[]{:S(2)}, u32[]{:S(2)}) collective-permute-start(f32[4,6,6,192]{3,2,1,0:T(8,128)S(1)} %get-tuple-element.35), channel_id=1, source_target_pairs={{0,7},{1,0},{2,1},{3,2},{4,3},{5,4},{6,5},{7,6},{8,15},{9,8},{10,9... | collective-permute-start | bytes 331784 | tf_op jit(solution)/shard_map/ppermute | solution.py:28
  136.1 1.9 copy-start.3
  136.1 1.9 copy-start.14
  137.8 14.4 %copy-start.9 = (f32[4,6,12,192]{3,0,2,1:T(4,128)S(1)}, f32[4,6,12,192]{3,0,2,1:T(4,128)}, u32[]{:S(2)}) copy-start(f32[4,6,12,192]{3,0,2,1:T(4,128)} %param.8) | copy-start | bytes 663556
  137.8 113.5 %reduce-scatter.5.cloned.1.call-start = ((), (), s32[]{:S(2)}) async-start(), calls=%async_computation.2 | async-start | bytes 122880 | tf_op jit(solution)/shard_map/reduce_scatter | solution.py:148
Sparse Core Ops, SparseCore 0:
  87.5 62.9 reduce-scatter.6
  154.4 74.9 all-reduce.1
  232.5 18.7 reduce-scatter.4
where the time goes:
time: 259 us; the launch traced here: 258 us
  local copies, waits for them, and re-layouts  78.7 us (30%)
  waiting for transfers between devices  67.6 us (26%)
  matrix products  41.6 us (16%)
  blocking collectives  40.2 us (16%)
  between operations  14.2 us (5%)
  starting transfers between devices  7.96 us (3%)
  other arithmetic  7.51 us (3%)
    psum x1, blocking collectives, shards(): grad_norm = lax.psum(norm_local, ('lat', 'lon'))  40.2 us
    psum x1, waiting for transfers between devices, shards(): grad_bias = lax.psum(bias_local, 'lon')  35.7 us
    reshape x2, local copies, waits for them, and re-layouts, shards(): bias_full = bias_full.reshape(PW, lat_blocks, HEADS, WIN, WIN)  30.9 us
    another operation x4, local copies, waits for them, and re-layouts  30.6 us
    reduce_scatter x1, waiting for transfers between devices, shards(): lax.psum_scatter(column_part, 'lat', scatter_dimension=0, tiled=True)  19.7 us
    dot_general x1, matrix products, shards(): jnp.einsum('clhiaxjby,xyr->lchrijab', score_sum, onehot, precision=HIGH)  13 us
    unnamed x4, waiting for transfers between devices  12.1 us
    dot_general x1, matrix products, shards(): jnp.einsum('lchrijab,xyr->clhiaxjby', split_table, onehot, precision=HIGH)  8.88 us
  transfers between devices with their start and end apart: 6, of which 3 were waited for; matrix products, arithmetic and copies ran while one was open for 38% of the time, Pallas kernels for 0%

commit v1 on v0

v1 whole, which is shorter than its diff:
```python
import functools
import math

import jax
import jax.numpy as jnp
from jax import lax
from jax.experimental import pallas as pl
from jax.experimental.pallas import tpu as pltpu
from jax.sharding import PartitionSpec as P

D = 192
HEADS = 6
HEAD = 32
ZP = 4
WZ = 2
WLAT = 6
WLON = 12
PW = 2
WIN = 144
LONREL = 23
PAIRS = 144
HALF = WLON // 2
LEVELS = WZ * WLAT
HALF_ROWS = HALF * LEVELS
GROUP = 4
GROUPS = WLON // GROUP
GROUP_ROWS = GROUP * LEVELS
BLOCK = HEADS * GROUP_ROWS
STRIP = LONREL * LEVELS

EPSILON = 1e-05
SCALE = HEAD ** (-0.5)
HIGH = lax.Precision.HIGH
FULL = lax.Precision.HIGHEST


def dot(left, right, precision=HIGH):
    return lax.dot_general(
        left, right, (((1,), (0,)), ((), ())), precision=precision, preferred_element_type=jnp.float32
    )


def dot_right_transposed(left, right, precision=HIGH):
    return lax.dot_general(
        left, right, (((1,), (1,)), ((), ())), precision=precision, preferred_element_type=jnp.float32
    )


def dot_left_transposed(left, right, precision=HIGH):
    return lax.dot_general(
        left, right, (((0,), (0,)), ((), ())), precision=precision, preferred_element_type=jnp.float32
    )


def whole(count):
    return [pl.BlockSpec(memory_space=pltpu.VMEM)] * count


def pack_kernel(features_ref, cotangent_ref, sent_ref, own_ref):
    for c in range(PW):
        for i in range(WZ):
            z = (WZ * c + i - 1) % ZP
            for a in range(WLAT):
                rows = pl.ds(i * WLAT + a, HALF, stride=LEVELS)
                both = jnp.concatenate([features_ref[z, a], cotangent_ref[z, a]], axis=-1)
                for tile in range(3):
                    own_ref[tile, c, rows, :] = both[:HALF, tile * 128 : (tile + 1) * 128]
                    sent_ref[tile, c, rows, :] = both[HALF:, tile * 128 : (tile + 1) * 128]


def unpack_kernel(own_ref, returned_ref, out_ref):
    for c in range(PW):
        for i in range(WZ):
            z = (WZ * c + i - 1) % ZP
            for a in range(WLAT):
                rows = pl.ds(i * WLAT + a, HALF, stride=LEVELS)
                for first, half_ref in ((0, own_ref), (HALF, returned_ref)):
                    out_ref[z, a, first : first + HALF, :128] = half_ref[c, rows, :]
                    out_ref[z, a, first : first + HALF, 128:] = half_ref[2, rows, :][:, c * 64 : (c + 1) * 64]


def block_kernel(
    factor, lat_count, lon_count,
    own_ref, borrowed_ref, gain_ref, shift_ref, qkv_ref, out_w_ref, strip_ref,
    grad_own_ref, grad_borrowed_ref, weights_ref, strip_grad_ref, norm_ref,
    table_ref, table_grad_ref, sums_ref,
):
    gain = gain_ref[...]
    shift = shift_ref[...]
    weight_q = qkv_ref[:, :D]
    weight_k = qkv_ref[:, D : 2 * D]
    weight_v = qkv_ref[:, 2 * D :]
    out_weight = out_w_ref[...]
    head_of_lane = lax.broadcasted_iota(jnp.int32, (GROUP_ROWS, D), 1) // HEAD

    def stacked(value):
        blocks = []
        for g in range(GROUPS):
            rows = value[g * GROUP_ROWS : (g + 1) * GROUP_ROWS]
            for h in range(HEADS):
                blocks.append(jnp.where(head_of_lane == h, rows, 0.0))
        return jnp.concatenate(blocks, axis=0)

    def unstacked(value):
        blocks = []
        for g in range(GROUPS):
            total = None
            for h in range(HEADS):
                first = g * BLOCK + h * GROUP_ROWS
                part = jnp.where(head_of_lane == h, value[first : first + GROUP_ROWS], 0.0)
                total = part if total is None else total + part
            blocks.append(total)
        return jnp.concatenate(blocks, axis=0)

    grad_q_w = grad_k_w = grad_v_w = grad_out_w = None
    gain_sum = shift_sum = None
    results = []
    for c in range(PW):
        for h in range(HEADS):
            strip = strip_ref[c, h * LEVELS : (h + 1) * LEVELS, :]
            if c == 0:
                level = lax.broadcasted_iota(jnp.int32, strip.shape, 0) // WLAT
                key_level = (lax.broadcasted_iota(jnp.int32, strip.shape, 1) % LEVELS) // WLAT
                strip = jnp.where(level == key_level, strip, -jnp.inf)
            for g in range(GROUP):
                first = h * GROUP_ROWS + g * LEVELS
                table_ref[first : first + LEVELS, g * LEVELS : g * LEVELS + STRIP] = strip

        both = jnp.concatenate(
            [jnp.concatenate([borrowed_ref[t, c], own_ref[t, c]], axis=0) for t in range(3)], axis=1
        )
        band = both[:, :D]
        window_grad = both[:, D:]
        average = jnp.mean(band, axis=-1, keepdims=True)
        centred = band - average
        inverse = lax.rsqrt(jnp.mean(centred * centred, axis=-1, keepdims=True) + EPSILON)
        unit = centred * inverse
        tokens = unit * gain + shift
        queries = dot(tokens, weight_q, FULL) * SCALE
        keys = dot(tokens, weight_k, FULL)
        values = dot(tokens, weight_v)
        grad_mixture = dot_right_transposed(window_grad, out_weight)
        query_stack = stacked(queries)
        grad_stack = stacked(grad_mixture)

        scores = dot_right_transposed(query_stack, keys, FULL)
        biased = []
        for g in range(GROUPS):
            start = (WLON - 1 - GROUP * g) * LEVELS
            biased.append(scores[g * BLOCK : (g + 1) * BLOCK] + table_ref[:, start : start + WIN])
        scores = jnp.concatenate(biased, axis=0)
        exponent = jnp.exp(scores - jnp.max(scores, axis=-1, keepdims=True))
        attention = exponent * (1.0 / jnp.sum(exponent, axis=-1, keepdims=True))
        mixture = unstacked(dot(attention, values))
        grad_attention = dot_right_transposed(grad_stack, values)
        weighted = jnp.sum(attention * grad_attention, axis=-1, keepdims=True)
        grad_scores = attention * (grad_attention - weighted)
        grad_values = dot_left_transposed(attention, grad_stack)
        grad_queries = unstacked(dot(grad_scores, keys)) * SCALE
        grad_keys = dot_left_transposed(grad_scores, query_stack)

        table_grad_ref[...] = jnp.zeros_like(table_grad_ref)
        for g in range(GROUPS):
            start = (WLON - 1 - GROUP * g) * LEVELS
            table_grad_ref[:, start : start + WIN] += grad_scores[g * BLOCK : (g + 1) * BLOCK]
        for h in range(HEADS):
            total = None
            for g in range(GROUP):
                first = h * GROUP_ROWS + g * LEVELS
                part = table_grad_ref[first : first + LEVELS, g * LEVELS : g * LEVELS + STRIP]
                total = part if total is None else total + part
            strip_grad_ref[c, h * LEVELS : (h + 1) * LEVELS, :] = total

        parts = (
            dot_left_transposed(tokens, grad_queries),
            dot_left_transposed(tokens, grad_keys),
            dot_left_transposed(tokens, grad_values),
            dot_left_transposed(mixture, window_grad),
        )
        for block, part in enumerate(parts):
            if c == 0:
                sums_ref[block] = part
            else:
                sums_ref[block] += part
        grad_tokens = (
            dot_right_transposed(grad_queries, weight_q)
            + dot_right_transposed(grad_keys, weight_k)
            + dot_right_transposed(grad_values, weight_v)
        )
        gain_part = jnp.sum(grad_tokens * unit, axis=0, keepdims=True)
        shift_part = jnp.sum(grad_tokens, axis=0, keepdims=True)
        gain_sum = gain_part if c == 0 else gain_sum + gain_part
        shift_sum = shift_part if c == 0 else shift_sum + shift_part
        grad_unit = grad_tokens * gain
        result = window_grad + inverse * (
            grad_unit
            - jnp.mean(grad_unit, axis=-1, keepdims=True)
            - unit * jnp.mean(grad_unit * unit, axis=-1, keepdims=True)
        )
        results.append(result)
    for ref, rows in ((grad_borrowed_ref, slice(0, HALF_ROWS)), (grad_own_ref, slice(HALF_ROWS, WIN))):
        for c in range(PW):
            ref[c] = results[c][rows, :128]
        ref[2] = jnp.concatenate([result[rows, 128:] for result in results], axis=1)
    norm_ref[...] = jnp.concatenate([gain_sum, shift_sum], axis=0) * factor
    for block in range(4):
        weights_ref[:, block * D : (block + 1) * D] = sums_ref[block] * factor


def exchanged(value, axis, bit):
    count = lax.axis_size(axis)
    return lax.ppermute(value, axis, [(source, source ^ bit) for source in range(count)])


def bits_of(count):
    return [1 << place for place in range(count.bit_length() - 1)]


def summed_part(value, axis, dimension):
    count = lax.axis_size(axis)
    index = lax.axis_index(axis)
    for bit in reversed(bits_of(count)):
        half = value.shape[dimension] // 2
        high = (index & bit) // bit
        kept = lax.dynamic_slice_in_dim(value, high * half, half, dimension)
        given = lax.dynamic_slice_in_dim(value, (1 - high) * half, half, dimension)
        value = kept + exchanged(given, axis, bit)
    return value


def summed(value, axis):
    for bit in bits_of(lax.axis_size(axis)):
        value = value + exchanged(value, axis, bit)
    return value


def shards(features, cotangent, norm_gain, norm_shift, qkv_weight, out_weight, bias_table):
    lat_count, lon_count = lax.axis_size("lat"), lax.axis_size("lon")
    token_count = ZP * features.shape[1] * features.shape[2] * lat_count * lon_count
    factor = 1.0 / math.sqrt(token_count)
    f32 = jnp.float32
    half_shape = jax.ShapeDtypeStruct((3, PW, HALF_ROWS, 128), f32)
    sent, own = pl.pallas_call(
        pack_kernel, out_shape=(half_shape, half_shape), in_specs=whole(2), out_specs=tuple(whole(2))
    )(features, cotangent)
    borrowed = lax.ppermute(sent, "lon", [(s, (s + 1) % lon_count) for s in range(lon_count)])
    strip = bias_table.reshape(PW, HEADS, LONREL, WZ, WZ, WLAT, WLAT).transpose(0, 1, 3, 5, 2, 4, 6)
    strip = strip.reshape(PW, HEADS * LEVELS, STRIP)
    grad_half = jax.ShapeDtypeStruct((3, HALF_ROWS, 128), f32)
    grad_own, grad_borrowed, weights, strip_grad, norm = pl.pallas_call(
        functools.partial(block_kernel, factor, lat_count, lon_count),
        out_shape=(
            grad_half,
            grad_half,
            jax.ShapeDtypeStruct((D, 4 * D), f32),
            jax.ShapeDtypeStruct((PW, HEADS * LEVELS, STRIP), f32),
            jax.ShapeDtypeStruct((2, D), f32),
        ),
        in_specs=whole(7),
        out_specs=tuple(whole(5)),
        scratch_shapes=[
            pltpu.VMEM((BLOCK, 384), f32),
            pltpu.VMEM((BLOCK, 384), f32),
            pltpu.VMEM((4, D, D), f32),
        ],
        compiler_params=pltpu.CompilerParams(vmem_limit_bytes=48 << 20),
    )(own, borrowed, norm_gain[None], norm_shift[None], qkv_weight, out_weight, strip)
    returned = lax.ppermute(grad_borrowed, "lon", [(s, (s - 1) % lon_count) for s in range(lon_count)])
    grad_features = pl.pallas_call(
        unpack_kernel,
        out_shape=jax.ShapeDtypeStruct(features.shape, f32),
        in_specs=whole(2),
        out_specs=whole(1)[0],
    )(grad_own, returned)
    grad_weights = summed_part(summed_part(weights, "lat", 0), "lon", 1)
    strip_grad = summed(strip_grad, "lon")
    grad_norm = summed(summed(norm, "lat"), "lon")
    grad_bias = strip_grad.reshape(PW, HEADS, WZ, WLAT, LONREL, WZ, WLAT).transpose(0, 1, 4, 2, 5, 3, 6)
    grad_bias = grad_bias.reshape(bias_table.shape)
    return (grad_features, grad_weights, grad_bias, grad_norm)


def solution(mesh):
    placed = (
        P(None, "lat", "lon", None),
        P(None, "lat", "lon", None),
        P(),
        P(),
        P(),
        P(),
        P("lat", None, None, None, None),
    )
    return jax.shard_map(
        shards,
        mesh=mesh,
        in_specs=placed,
        out_specs=(
            P(None, "lat", "lon", None),
            P("lat", "lon"),
            P("lat", None, None, None, None),
            P(),
        ),
        check_vma=False,
    )
```

time: 259 us -> 92 us (0.36)
  local copies, waits for them, and re-layouts: 78.7 us -> 26.3 us
  waiting for transfers between devices: 67.6 us -> 25.3 us
  matrix products: 41.6 us -> 0 us
  blocking collectives: 40.2 us -> 0 us
  Pallas kernels: 0 us -> 14.2 us
  starting transfers between devices: 7.96 us -> 22.1 us
  between operations: 14.2 us -> 0.88 us
  other arithmetic: 7.51 us -> 2.93 us
    dot_general x13 -> x0, matrix products: 41.6 us -> none  [the longest x1 13 us: shards(): jnp.einsum('clhiaxjby,xyr->lchrijab', score_sum, onehot, precision=HIGH)]
    psum x1 -> x0, blocking collectives: 40.2 us -> none  [shards(): grad_norm = lax.psum(norm_local, ('lat', 'lon'))]
    psum x1 -> x0, waiting for transfers between devices: 35.7 us -> none  [shards(): grad_bias = lax.psum(bias_local, 'lon')]
    another operation x4 -> x0, local copies, waits for them, and re-layouts: 30.6 us -> none
    reshape x6 -> x2, local copies, waits for them, and re-layouts: 32.7 us -> 7.18 us  [the longest x1 3.97 us: shards(): strip = strip.reshape(PW, HEADS * LEVELS, STRIP)]
    ppermute x3 -> x15, waiting for transfers between devices: 0.01 us -> 25.3 us  [the longest x13 25.3 us: exchanged(): lax.ppermute(value, axis, [(source, source ^ bit) for source in range(cou...]
    reduce_scatter x1 -> x0, waiting for transfers between devices: 19.7 us -> none  [shards(): lax.psum_scatter(column_part, 'lat', scatter_dimension=0, tiled=True)]
    ppermute x3 -> x15, starting transfers between devices: 7.84 us -> 22.1 us  [the longest x13 15.8 us: exchanged(): lax.ppermute(value, axis, [(source, source ^ bit) for source in range(cou...]
  transfers between devices with their start and end apart: 6 -> 15, of which waited for: 3 -> 8; matrix products, arithmetic and copies ran while one was open for 38% -> 25% of each run, Pallas kernels for 0% -> 2%
where the time goes in v1:
time: 92 us; the launch traced here: 91.6 us
  local copies, waits for them, and re-layouts  26.3 us (29%)
  waiting for transfers between devices  25.3 us (28%)
  starting transfers between devices  22.1 us (24%)
  Pallas kernels  14.2 us (15%)
  other arithmetic  2.93 us (3%)
    ppermute x13, waiting for transfers between devices, exchanged(): lax.ppermute(value, axis, [(source, source ^ bit) for source in range(cou...  25.3 us
    ppermute x13, starting transfers between devices, exchanged(): lax.ppermute(value, axis, [(source, source ^ bit) for source in range(cou...  15.8 us
    unnamed x19, local copies, waits for them, and re-layouts  10.4 us
    pallas_call x1, Pallas kernels, shards(): pl.pallas_call(functools.partial(block_kernel, factor, lat_count, lon_cou...  10.4 us
    transpose x1, local copies, waits for them, and re-layouts, shards(): bias_table.reshape(PW, HEADS, LONREL, WZ, WZ, WLAT, WLAT)  4.14 us
    reshape x1, local copies, waits for them, and re-layouts, shards(): strip = strip.reshape(PW, HEADS * LEVELS, STRIP)  3.97 us
    transpose x1, local copies, waits for them, and re-layouts, shards(): strip_grad.reshape(PW, HEADS, WZ, WLAT, LONREL, WZ, WLAT)  3.69 us
    ppermute x1, starting transfers between devices, shards(): lax.ppermute(grad_borrowed, 'lon', [(s, (s - 1) % lon_count) for s in ran...  3.32 us
  transfers between devices with their start and end apart: 15, of which 8 were waited for; matrix products, arithmetic and copies ran while one was open for 25% of the time, Pallas kernels for 2%

profile of v1, /device:TPU:0, one launch (start us, length us, event | category | flops | bytes accessed | tf_op | source)
XLA Modules:
  0.0 91.6 jit_solution(9558238602078669756)
XLA Ops:
  0.6 1.8 %copy.16.features_ref = f32[4,6,12,192]{3,2,1,0:T(8,128)} copy(f32[4,6,12,192]{3,0,2,1:T(4,128)} %param.7) | data formatting | bytes 442368 | tf_op args[0]
  2.4 1.8 %copy.17.cotangent_ref = f32[4,6,12,192]{3,2,1,0:T(8,128)} copy(f32[4,6,12,192]{3,0,2,1:T(4,128)} %param.8) | data formatting | bytes 442368 | tf_op args[1]
  4.2 2.0 %shard_map.102 = (f32[3,2,72,128]{3,2,1,0:T(8,128)}, f32[3,2,72,128]{3,2,1,0:T(8,128)}) custom-call(f32[4,6,12,192]{3,2,1,0:T(8,128)} %copy.16.features_ref, f32[4,6,12,192]{3,2,1,0:T(8,128)} %copy.17.cotangent_ref), custom_call_target="tpu_custom_call" | custom-call | tf_op jit(solution)/shard_map/pallas_call | solution.py:243
  6.2 3.0 %collective-permute-start = (f32[3,2,72,128]{3,2,1,0:T(8,128)}, f32[3,2,72,128]{3,2,1,0:T(8,128)S(1)}, u32[]{:S(2)}, u32[]{:S(2)}) collective-permute-start(f32[3,2,72,128]{3,2,1,0:T(8,128)} %get-tuple-element.12), channel_id=1, source_target_pairs={{0,1},{1,2},{2,3},{3,4},{4,5},{5,6},{6,7},{7,0},{8,9},{9,10},{10,1... | collective-permute-start | bytes 663560 | tf_op jit(solution)/shard_map/ppermute | solution.py:246
  9.2 1.4 %copy.18 = f32[1,2,6,23,144]{3,1,4,2,0:T(2,128)S(1)} copy(f32[1,2,6,23,144]{4,1,3,2,0:T(2,128)} %param.13) | data formatting | bytes 317952 | tf_op args[6]
  10.6 0.0 copy-start
  10.6 0.0 copy-start.1
  10.7 0.0 copy-start.2
  10.7 0.0 copy-start.4
  10.7 0.0 copy-start.5
  10.7 4.1 %copy.19 = f32[2,6,2,6,23,2,6]{6,5,4,3,2,1,0:T(2,128)} copy(f32[2,6,2,6,23,2,6]{4,0,6,3,5,2,1:T(2,128)S(1)} %bitcast.11) | data formatting | bytes 317952 | tf_op jit(solution)/shard_map/transpose | solution.py:247
  14.8 4.0 %reshape.21.strip_ref = f32[2,72,276]{2,1,0:T(8,128)S(1)} reshape(f32[2,6,2,6,23,2,6]{6,5,4,3,2,1,0:T(2,128)} %copy.19) | data formatting | bytes 317952 | tf_op jit(solution)/shard_map/reshape | solution.py:248
  18.8 0.0 collective-permute-done.borrowed_ref
  18.8 0.0 copy-done
  18.8 0.0 copy-done.1
  18.9 0.0 copy-done.2
  18.9 0.0 copy-done.4
  18.9 0.0 copy-done.5
  18.9 10.4 %shard_map.103 = (f32[3,72,128]{2,1,0:T(8,128)S(1)}, f32[3,72,128]{2,1,0:T(8,128)S(1)}, f32[192,768]{1,0:T(8,128)S(1)}, f32[2,72,276]{2,1,0:T(8,128)S(1)}, f32[2,192]{1,0:T(2,128)S(1)}) custom-call(f32[3,2,72,128]{3,2,1,0:T(8,128)S(1)} %copy-done.1, f32[3,2,72,128]{3,2,1,0:T(8,128)S(1)} %collective-permute-done.borrowed_ref, f32[1,192]{1,0:T(1,128)S(1)} %bitcast.7, ...), custom_call_target="tpu_custom_call" | custom-call | tf_op jit(solution)/shard_map/pallas_call | solution.py:250
  29.3 0.0 copy-start.3
  29.3 0.6 copy-done.3
  29.9 1.6 %collective-permute-start.2 = (f32[96,768]{1,0:T(8,128)S(1)}, f32[96,768]{1,0:T(8,128)S(1)}, u32[]{:S(2)}, u32[]{:S(2)}) collective-permute-start(f32[96,768]{1,0:T(8,128)S(1)} %constant_dynamic-slice_fusion.4), channel_id=1, source_target_pairs={{0,16},{8,24},{16,0},{24,8},{1,17},{9,25},{17,1},{25,9},{2,18},{10... | collective-permute-start | bytes 884744 | tf_op jit(solution)/shard_map/ppermute | solution.py:212
  31.5 7.0 %collective-permute-done.2 = f32[96,768]{1,0:T(8,128)S(1)} collective-permute-done((f32[96,768]{1,0:T(8,128)S(1)}, f32[96,768]{1,0:T(8,128)S(1)}, u32[]{:S(2)}, u32[]{:S(2)}) %collective-permute-start.2) | collective-permute-done | bytes 294944 | tf_op jit(solution)/shard_map/ppermute | solution.py:212
  38.5 0.1 collective-permute-start.3
  38.6 1.6 %collective-permute-start.7 = (f32[2,72,276]{2,1,0:T(8,128)S(1)}, f32[2,72,276]{2,1,0:T(8,128)S(1)}, u32[]{:S(2)}, u32[]{:S(2)}) collective-permute-start(f32[2,72,276]{2,1,0:T(8,128)S(1)} %get-tuple-element.16), channel_id=1, source_target_pairs={{0,1},{1,0},{2,3},{3,2},{4,5},{5,4},{6,7},{7,6},{8,9},{9,8},{10,11... | collective-permute-start | bytes 476936 | tf_op jit(solution)/shard_map/ppermute | solution.py:212
  40.2 0.0 collective-permute-done.3
  40.3 2.6 %collective-permute-start.4 = (f32[48,384]{1,0:T(8,128)S(1)}, f32[48,384]{1,0:T(8,128)S(1)}, u32[]{:S(2)}, u32[]{:S(2)}) collective-permute-start(f32[48,384]{1,0:T(8,128)S(1)} %constant_dynamic-slice_fusion.2), channel_id=1, source_target_pairs={{0,4},{1,5},{2,6},{3,7},{4,0},{5,1},{6,2},{7,3},{8,12},{9,13},{10,... | collective-permute-start | bytes 221192 | tf_op jit(solution)/shard_map/ppermute | solution.py:212
  42.9 3.5 %collective-permute-done.7 = f32[2,72,276]{2,1,0:T(8,128)S(1)} collective-permute-done((f32[2,72,276]{2,1,0:T(8,128)S(1)}, f32[2,72,276]{2,1,0:T(8,128)S(1)}, u32[]{:S(2)}, u32[]{:S(2)}) %collective-permute-start.7) | collective-permute-done | bytes 159008 | tf_op jit(solution)/shard_map/ppermute | solution.py:212
  46.5 1.6 %collective-permute-start.8 = (f32[2,72,276]{2,1,0:T(8,128)S(1)}, f32[2,72,276]{2,1,0:T(8,128)S(1)}, u32[]{:S(2)}, u32[]{:S(2)}) collective-permute-start(f32[2,72,276]{2,1,0:T(8,128)S(1)} %add.89), channel_id=1, source_target_pairs={{0,2},{1,3},{2,0},{3,1},{4,6},{5,7},{6,4},{7,5},{8,10},{9,11},{10,... | collective-permute-start | bytes 476936 | tf_op jit(solution)/shard_map/ppermute | solution.py:212
  48.1 0.0 collective-permute-done.4
  48.1 0.1 constant_dynamic-slice_fusion.1
  48.2 0.5 collective-permute-start.5
  48.8 3.3 %collective-permute-start.1 = (f32[3,72,128]{2,1,0:T(8,128)S(1)}, f32[3,72,128]{2,1,0:T(8,128)S(1)}, u32[]{:S(2)}, u32[]{:S(2)}) collective-permute-start(f32[3,72,128]{2,1,0:T(8,128)S(1)} %get-tuple-element.14), channel_id=1, source_target_pairs={{0,7},{1,0},{2,1},{3,2},{4,3},{5,4},{6,5},{7,6},{8,15},{9,8},{10,9... | collective-permute-start | bytes 331784 | tf_op jit(solution)/shard_map/ppermute | solution.py:268
  52.1 2.8 %collective-permute-done.8 = f32[2,72,276]{2,1,0:T(8,128)S(1)} collective-permute-done((f32[2,72,276]{2,1,0:T(8,128)S(1)}, f32[2,72,276]{2,1,0:T(8,128)S(1)}, u32[]{:S(2)}, u32[]{:S(2)}) %collective-permute-start.8) | collective-permute-done | bytes 159008 | tf_op jit(solution)/shard_map/ppermute | solution.py:212
  54.9 2.7 %collective-permute-start.9 = (f32[2,72,276]{2,1,0:T(8,128)S(1)}, f32[2,72,276]{2,1,0:T(8,128)S(1)}, u32[]{:S(2)}, u32[]{:S(2)}) collective-permute-start(f32[2,72,276]{2,1,0:T(8,128)S(1)} %add.90), channel_id=1, source_target_pairs={{0,4},{1,5},{2,6},{3,7},{4,0},{5,1},{6,2},{7,3},{8,12},{9,13},{10,... | collective-permute-start | bytes 476936 | tf_op jit(solution)/shard_map/ppermute | solution.py:212
  57.6 0.0 collective-permute-done.5
  57.6 0.1 dynamic-slice_add_fusion.3
  57.7 0.7 constant_dynamic-slice_fusion
  58.4 0.7 collective-permute-start.6
  59.0 0.0 collective-permute-start.10
  59.0 1.2 %collective-permute-done.10 = f32[2,192]{1,0:T(2,128)S(1)} collective-permute-done((f32[2,192]{1,0:T(2,128)S(1)}, f32[2,192]{1,0:T(2,128)S(1)}, u32[]{:S(2)}, u32[]{:S(2)}) %collective-permute-start.10) | collective-permute-done | bytes 1568 | tf_op jit(solution)/shard_map/ppermute | solution.py:212
  60.2 1.5 %collective-permute-start.11 = (f32[2,192]{1,0:T(2,128)S(1)}, f32[2,192]{1,0:T(2,128)S(1)}, u32[]{:S(2)}, u32[]{:S(2)}) collective-permute-start(f32[2,192]{1,0:T(2,128)S(1)} %add.92), channel_id=1, source_target_pairs={{0,16},{8,24},{16,0},{24,8},{1,17},{9,25},{17,1},{25,9},{2,18},{10... | collective-permute-start | bytes 4616 | tf_op jit(solution)/shard_map/ppermute | solution.py:212
  61.7 2.1 %collective-permute-done.11 = f32[2,192]{1,0:T(2,128)S(1)} collective-permute-done((f32[2,192]{1,0:T(2,128)S(1)}, f32[2,192]{1,0:T(2,128)S(1)}, u32[]{:S(2)}, u32[]{:S(2)}) %collective-permute-start.11) | collective-permute-done | bytes 1568 | tf_op jit(solution)/shard_map/ppermute | solution.py:212
  63.8 1.4 %collective-permute-start.12 = (f32[2,192]{1,0:T(2,128)S(1)}, f32[2,192]{1,0:T(2,128)S(1)}, u32[]{:S(2)}, u32[]{:S(2)}) collective-permute-start(f32[2,192]{1,0:T(2,128)S(1)} %add.93), channel_id=1, source_target_pairs={{0,1},{1,0},{2,3},{3,2},{4,5},{5,4},{6,7},{7,6},{8,9},{9,8},{10,11... | collective-permute-start | bytes 4616 | tf_op jit(solution)/shard_map/ppermute | solution.py:212
  65.2 2.2 %collective-permute-done.12 = f32[2,192]{1,0:T(2,128)S(1)} collective-permute-done((f32[2,192]{1,0:T(2,128)S(1)}, f32[2,192]{1,0:T(2,128)S(1)}, u32[]{:S(2)}, u32[]{:S(2)}) %collective-permute-start.12) | collective-permute-done | bytes 1568 | tf_op jit(solution)/shard_map/ppermute | solution.py:212
  67.4 1.1 %collective-permute-start.13 = (f32[2,192]{1,0:T(2,128)S(1)}, f32[2,192]{1,0:T(2,128)S(1)}, u32[]{:S(2)}, u32[]{:S(2)}) collective-permute-start(f32[2,192]{1,0:T(2,128)S(1)} %add.94), channel_id=1, source_target_pairs={{0,2},{1,3},{2,0},{3,1},{4,6},{5,7},{6,4},{7,5},{8,10},{9,11},{10,... | collective-permute-start | bytes 4616 | tf_op jit(solution)/shard_map/ppermute | solution.py:212
  68.5 2.4 %collective-permute-done.13 = f32[2,192]{1,0:T(2,128)S(1)} collective-permute-done((f32[2,192]{1,0:T(2,128)S(1)}, f32[2,192]{1,0:T(2,128)S(1)}, u32[]{:S(2)}, u32[]{:S(2)}) %collective-permute-start.13) | collective-permute-done | bytes 1568 | tf_op jit(solution)/shard_map/ppermute | solution.py:212
  71.0 0.4 collective-permute-start.14
  71.4 4.1 %collective-permute-done.14 = f32[2,192]{1,0:T(2,128)S(1)} collective-permute-done((f32[2,192]{1,0:T(2,128)S(1)}, f32[2,192]{1,0:T(2,128)S(1)}, u32[]{:S(2)}, u32[]{:S(2)}) %collective-permute-start.14) | collective-permute-done | bytes 1568 | tf_op jit(solution)/shard_map/ppermute | solution.py:212
  75.5 0.6 add.96
  76.0 0.0 collective-permute-done.1.returned_ref
  76.0 0.0 copy-start.6
  76.0 0.6 copy-done.6
  76.7 1.8 %shard_map.104 = f32[4,6,12,192]{3,2,1,0:T(8,128)} custom-call(f32[3,72,128]{2,1,0:T(8,128)} %copy-done.3, f32[3,72,128]{2,1,0:T(8,128)} %copy-done.6), custom_call_target="tpu_custom_call" | custom-call | tf_op jit(solution)/shard_map/pallas_call | solution.py:269
  78.5 1.9 %copy.21 = f32[4,6,12,192]{3,0,2,1:T(4,128)} copy(f32[4,6,12,192]{3,2,1,0:T(8,128)} %shard_map.104) | data formatting | bytes 442368
  80.4 0.0 collective-permute-done.9
  80.4 0.7 add.91
  81.1 3.2 %reshape.22 = f32[2,6,2,6,23,2,6]{6,5,4,3,2,1,0:T(2,128)S(1)} reshape(f32[2,72,276]{2,1,0:T(8,128)} %add.91) | data formatting | bytes 317952 | tf_op jit(solution)/shard_map/reshape | solution.py:278
  84.3 3.7 %copy.20 = f32[2,6,23,2,2,6,6]{2,0,6,5,4,3,1:T(2,128)} copy(f32[2,6,23,2,2,6,6]{6,4,2,5,3,1,0:T(2,128)S(1)} %bitcast.9) | data formatting | bytes 317952 | tf_op jit(solution)/shard_map/transpose | solution.py:278
  88.0 2.2 %copy.22 = f32[1,2,6,23,144]{4,1,3,2,0:T(2,128)} copy(f32[1,2,6,23,144]{3,1,4,2,0:T(2,128)} %bitcast.10) | data formatting | bytes 317952
  90.2 0.0 collective-permute-done.6
  90.2 1.4 %dynamic-slice_add_fusion.4 = f32[48,96]{1,0:T(8,128)} fusion(f32[48,96]{1,0:T(8,128)} %collective-permute-done.6, f32[48,192]{1,0:T(8,128)S(1)} %dynamic-slice_add_fusion.3, s32[]{:T(128)S(6)} %select_n.54), kind=kLoop, calls=%fused_computation.4 | loop fusion | flops 4608 | bytes 55300 | tf_op jit(solution)/shard_map/add | solution.py:227
  (12 shorter events, 0.2 us)
Async XLA Ops:
  6.2 12.6 %collective-permute-start = (f32[3,2,72,128]{3,2,1,0:T(8,128)}, f32[3,2,72,128]{3,2,1,0:T(8,128)S(1)}, u32[]{:S(2)}, u32[]{:S(2)}) collective-permute-start(f32[3,2,72,128]{3,2,1,0:T(8,128)} %get-tuple-element.12), channel_id=1, source_target_pairs={{0,1},{1,2},{2,3},{3,4},{4,5},{5,6},{6,7},{7,0},{8,9},{9,10},{10,1... | collective-permute-start | bytes 663560 | tf_op jit(solution)/shard_map/ppermute | solution.py:246
  10.6 8.2 %copy-start = (f32[192,576]{1,0:T(8,128)S(1)}, f32[192,576]{1,0:T(8,128)}, u32[]{:S(2)}) copy-start(f32[192,576]{1,0:T(8,128)} %qkv_ref.1) | copy-start | bytes 1327108
  10.6 8.2 %copy-start.1 = (f32[3,2,72,128]{3,2,1,0:T(8,128)S(1)}, f32[3,2,72,128]{3,2,1,0:T(8,128)}, u32[]{:S(2)}) copy-start(f32[3,2,72,128]{3,2,1,0:T(8,128)} %get-tuple-element.11.own_ref) | copy-start | bytes 663556
  10.7 8.2 %copy-start.2 = (f32[192,192]{1,0:T(8,128)S(1)}, f32[192,192]{1,0:T(8,128)}, u32[]{:S(2)}) copy-start(f32[192,192]{1,0:T(8,128)} %out_w_ref.1) | copy-start | bytes 442372
  10.7 8.2 %copy-start.4 = (f32[192]{0:T(256)S(1)}, f32[192]{0:T(256)}, u32[]{:S(2)}) copy-start(f32[192]{0:T(256)} %param.9) | copy-start | bytes 2308
  10.7 8.2 %copy-start.5 = (f32[192]{0:T(256)S(1)}, f32[192]{0:T(256)}, u32[]{:S(2)}) copy-start(f32[192]{0:T(256)} %param.10) | copy-start | bytes 2308
  29.3 0.6 copy-start.3
  29.9 8.5 %collective-permute-start.2 = (f32[96,768]{1,0:T(8,128)S(1)}, f32[96,768]{1,0:T(8,128)S(1)}, u32[]{:S(2)}, u32[]{:S(2)}) collective-permute-start(f32[96,768]{1,0:T(8,128)S(1)} %constant_dynamic-slice_fusion.4), channel_id=1, source_target_pairs={{0,16},{8,24},{16,0},{24,8},{1,17},{9,25},{17,1},{25,9},{2,18},{10... | collective-permute-start | bytes 884744 | tf_op jit(solution)/shard_map/ppermute | solution.py:212
  38.5 1.7 %collective-permute-start.3 = (f32[48,768]{1,0:T(8,128)S(1)}, f32[48,768]{1,0:T(8,128)S(1)}, u32[]{:S(2)}, u32[]{:S(2)}) collective-permute-start(f32[48,768]{1,0:T(8,128)S(1)} %constant_dynamic-slice_fusion.3), channel_id=1, source_target_pairs={{0,8},{8,0},{16,24},{24,16},{1,9},{9,1},{17,25},{25,17},{2,10},{10... | collective-permute-start | bytes 442376 | tf_op jit(solution)/shard_map/ppermute | solution.py:212
  38.6 7.8 %collective-permute-start.7 = (f32[2,72,276]{2,1,0:T(8,128)S(1)}, f32[2,72,276]{2,1,0:T(8,128)S(1)}, u32[]{:S(2)}, u32[]{:S(2)}) collective-permute-start(f32[2,72,276]{2,1,0:T(8,128)S(1)} %get-tuple-element.16), channel_id=1, source_target_pairs={{0,1},{1,0},{2,3},{3,2},{4,5},{5,4},{6,7},{7,6},{8,9},{9,8},{10,11... | collective-permute-start | bytes 476936 | tf_op jit(solution)/shard_map/ppermute | solution.py:212
  40.3 7.9 %collective-permute-start.4 = (f32[48,384]{1,0:T(8,128)S(1)}, f32[48,384]{1,0:T(8,128)S(1)}, u32[]{:S(2)}, u32[]{:S(2)}) collective-permute-start(f32[48,384]{1,0:T(8,128)S(1)} %constant_dynamic-slice_fusion.2), channel_id=1, source_target_pairs={{0,4},{1,5},{2,6},{3,7},{4,0},{5,1},{6,2},{7,3},{8,12},{9,13},{10,... | collective-permute-start | bytes 221192 | tf_op jit(solution)/shard_map/ppermute | solution.py:212
  46.5 8.4 %collective-permute-start.8 = (f32[2,72,276]{2,1,0:T(8,128)S(1)}, f32[2,72,276]{2,1,0:T(8,128)S(1)}, u32[]{:S(2)}, u32[]{:S(2)}) collective-permute-start(f32[2,72,276]{2,1,0:T(8,128)S(1)} %add.89), channel_id=1, source_target_pairs={{0,2},{1,3},{2,0},{3,1},{4,6},{5,7},{6,4},{7,5},{8,10},{9,11},{10,... | collective-permute-start | bytes 476936 | tf_op jit(solution)/shard_map/ppermute | solution.py:212
  48.2 9.4 %collective-permute-start.5 = (f32[48,192]{1,0:T(8,128)S(1)}, f32[48,192]{1,0:T(8,128)S(1)}, u32[]{:S(2)}, u32[]{:S(2)}) collective-permute-start(f32[48,192]{1,0:T(8,128)S(1)} %constant_dynamic-slice_fusion.1), channel_id=1, source_target_pairs={{0,2},{1,3},{2,0},{3,1},{4,6},{5,7},{6,4},{7,5},{8,10},{9,11},{10,... | collective-permute-start | bytes 110600 | tf_op jit(solution)/shard_map/ppermute | solution.py:212
  48.8 27.3 %collective-permute-start.1 = (f32[3,72,128]{2,1,0:T(8,128)S(1)}, f32[3,72,128]{2,1,0:T(8,128)S(1)}, u32[]{:S(2)}, u32[]{:S(2)}) collective-permute-start(f32[3,72,128]{2,1,0:T(8,128)S(1)} %get-tuple-element.14), channel_id=1, source_target_pairs={{0,7},{1,0},{2,1},{3,2},{4,3},{5,4},{6,5},{7,6},{8,15},{9,8},{10,9... | collective-permute-start | bytes 331784 | tf_op jit(solution)/shard_map/ppermute | solution.py:268
  54.9 25.4 %collective-permute-start.9 = (f32[2,72,276]{2,1,0:T(8,128)S(1)}, f32[2,72,276]{2,1,0:T(8,128)S(1)}, u32[]{:S(2)}, u32[]{:S(2)}) collective-permute-start(f32[2,72,276]{2,1,0:T(8,128)S(1)} %add.90), channel_id=1, source_target_pairs={{0,4},{1,5},{2,6},{3,7},{4,0},{5,1},{6,2},{7,3},{8,12},{9,13},{10,... | collective-permute-start | bytes 476936 | tf_op jit(solution)/shard_map/ppermute | solution.py:212
  58.4 31.8 %collective-permute-start.6 = (f32[48,96]{1,0:T(8,128)}, f32[48,96]{1,0:T(8,128)}, u32[]{:S(2)}, u32[]{:S(2)}) collective-permute-start(f32[48,96]{1,0:T(8,128)} %constant_dynamic-slice_fusion), channel_id=1, source_target_pairs={{0,1},{1,0},{2,3},{3,2},{4,5},{5,4},{6,7},{7,6},{8,9},{9,8},{10,11... | collective-permute-start | bytes 55304 | tf_op jit(solution)/shard_map/ppermute | solution.py:212
  59.0 1.2 %collective-permute-start.10 = (f32[2,192]{1,0:T(2,128)S(1)}, f32[2,192]{1,0:T(2,128)S(1)}, u32[]{:S(2)}, u32[]{:S(2)}) collective-permute-start(f32[2,192]{1,0:T(2,128)S(1)} %get-tuple-element.17), channel_id=1, source_target_pairs={{0,8},{8,0},{16,24},{24,16},{1,9},{9,1},{17,25},{25,17},{2,10},{10... | collective-permute-start | bytes 4616 | tf_op jit(solution)/shard_map/ppermute | solution.py:212
  60.2 3.6 %collective-permute-start.11 = (f32[2,192]{1,0:T(2,128)S(1)}, f32[2,192]{1,0:T(2,128)S(1)}, u32[]{:S(2)}, u32[]{:S(2)}) collective-permute-start(f32[2,192]{1,0:T(2,128)S(1)} %add.92), channel_id=1, source_target_pairs={{0,16},{8,24},{16,0},{24,8},{1,17},{9,25},{17,1},{25,9},{2,18},{10... | collective-permute-start | bytes 4616 | tf_op jit(solution)/shard_map/ppermute | solution.py:212
  63.8 3.6 %collective-permute-start.12 = (f32[2,192]{1,0:T(2,128)S(1)}, f32[2,192]{1,0:T(2,128)S(1)}, u32[]{:S(2)}, u32[]{:S(2)}) collective-permute-start(f32[2,192]{1,0:T(2,128)S(1)} %add.93), channel_id=1, source_target_pairs={{0,1},{1,0},{2,3},{3,2},{4,5},{5,4},{6,7},{7,6},{8,9},{9,8},{10,11... | collective-permute-start | bytes 4616 | tf_op jit(solution)/shard_map/ppermute | solution.py:212
  67.4 3.6 %collective-permute-start.13 = (f32[2,192]{1,0:T(2,128)S(1)}, f32[2,192]{1,0:T(2,128)S(1)}, u32[]{:S(2)}, u32[]{:S(2)}) collective-permute-start(f32[2,192]{1,0:T(2,128)S(1)} %add.94), channel_id=1, source_target_pairs={{0,2},{1,3},{2,0},{3,1},{4,6},{5,7},{6,4},{7,5},{8,10},{9,11},{10,... | collective-permute-start | bytes 4616 | tf_op jit(solution)/shard_map/ppermute | solution.py:212
  71.0 4.5 %collective-permute-start.14 = (f32[2,192]{1,0:T(2,128)S(1)}, f32[2,192]{1,0:T(2,128)S(1)}, u32[]{:S(2)}, u32[]{:S(2)}) collective-permute-start(f32[2,192]{1,0:T(2,128)S(1)} %add.95), channel_id=1, source_target_pairs={{0,4},{1,5},{2,6},{3,7},{4,0},{5,1},{6,2},{7,3},{8,12},{9,13},{10,... | collective-permute-start | bytes 4616 | tf_op jit(solution)/shard_map/ppermute | solution.py:212
  76.0 0.6 copy-start.6

commit v2 on v1

v2 whole, which is shorter than its diff:
```python
import functools
import math

import jax
import jax.numpy as jnp
from jax import lax
from jax.experimental import pallas as pl
from jax.experimental.pallas import tpu as pltpu
from jax.sharding import PartitionSpec as P

D = 192
HEADS = 6
HEAD = 32
ZP = 4
WZ = 2
WLAT = 6
WLON = 12
PW = 2
WIN = 144
LONREL = 23
PAIRS = 144
HALF = WLON // 2
LEVELS = WZ * WLAT
HALF_ROWS = HALF * LEVELS
GROUP = 4
GROUPS = WLON // GROUP
GROUP_ROWS = GROUP * LEVELS
BLOCK = HEADS * GROUP_ROWS
STRIP = LONREL * LEVELS
PADDED = 16
OFFSETS = 24

EPSILON = 1e-05
SCALE = HEAD ** (-0.5)
HIGH = lax.Precision.HIGH
FULL = lax.Precision.HIGHEST


def dot(left, right, precision=HIGH):
    return lax.dot_general(
        left, right, (((1,), (0,)), ((), ())), precision=precision, preferred_element_type=jnp.float32
    )


def dot_right_transposed(left, right, precision=HIGH):
    return lax.dot_general(
        left, right, (((1,), (1,)), ((), ())), precision=precision, preferred_element_type=jnp.float32
    )


def dot_left_transposed(left, right, precision=HIGH):
    return lax.dot_general(
        left, right, (((0,), (0,)), ((), ())), precision=precision, preferred_element_type=jnp.float32
    )


def whole(count):
    return [pl.BlockSpec(memory_space=pltpu.VMEM)] * count


def pack_kernel(features_ref, cotangent_ref, sent_ref, own_ref):
    for a in range(WLAT):
        for x in range(WLON):
            target_ref = own_ref if x < HALF else sent_ref
            band = features_ref[a, x]
            grad = cotangent_ref[a, x]
            tiles = (band[:, :128], jnp.concatenate([band[:, 128:], grad[:, 128:]], axis=1), grad[:, :128])
            for z in range(ZP):
                c, i = divmod((z + 1) % ZP, WZ)
                row = (x % HALF) * LEVELS + i * WLAT + a
                for tile in range(3):
                    target_ref[tile, c, row : row + 1, :] = tiles[tile][z : z + 1]


def unpack_kernel(own_ref, returned_ref, out_ref):
    for a in range(WLAT):
        for x in range(WLON):
            source_ref = own_ref if x < HALF else returned_ref
            for z in range(ZP):
                c, i = divmod((z + 1) % ZP, WZ)
                row = (x % HALF) * LEVELS + i * WLAT + a
                out_ref[a, x, z : z + 1, :128] = source_ref[c, row : row + 1, :]
                out_ref[a, x, z : z + 1, 128:] = source_ref[2, row : row + 1, c * 64 : (c + 1) * 64]


def pair_order():
    row = lax.broadcasted_iota(jnp.int32, (LEVELS * PADDED, 1), 0)
    key, query = row // PADDED, row % PADDED
    place = (query // WLAT) * 72 + (key // WLAT) * 36 + (query % WLAT) * WLAT + key % WLAT
    place = jnp.where(query < LEVELS, place, -1)
    return (place == lax.broadcasted_iota(jnp.int32, (LEVELS * PADDED, PAIRS), 1)).astype(jnp.float32)


def offset_order():
    row = lax.broadcasted_iota(jnp.int32, (LEVELS * OFFSETS, 1), 0)
    place = (row % OFFSETS) * LEVELS + row // OFFSETS
    columns = lax.broadcasted_iota(jnp.int32, (LEVELS * OFFSETS, LEVELS * OFFSETS), 1)
    return (place == columns).astype(jnp.float32)


def table_kernel(bias_ref, table_ref, turned_ref, strip_ref):
    pairs, offsets = pair_order(), offset_order()
    strip_ref[...] = jnp.zeros_like(strip_ref)
    for c in range(PW):
        rows = jnp.concatenate([bias_ref[h, :, c, :] for h in range(HEADS)], axis=0)
        turned_ref[...] = dot_right_transposed(pairs, rows, FULL)
        for h in range(HEADS):
            for key in range(LEVELS):
                strip_ref[h * PADDED : (h + 1) * PADDED, key * OFFSETS : key * OFFSETS + LONREL] = turned_ref[
                    key * PADDED : (key + 1) * PADDED, h * LONREL : (h + 1) * LONREL
                ]
        strips = dot(strip_ref[...], offsets, FULL)
        if c == 0:
            level = (lax.broadcasted_iota(jnp.int32, strips.shape, 0) % PADDED) // WLAT
            key_level = (lax.broadcasted_iota(jnp.int32, strips.shape, 1) % LEVELS) // WLAT
            strips = jnp.where(level == key_level, strips, -jnp.inf)
        for h in range(HEADS):
            strip = strips[h * PADDED : h * PADDED + LEVELS, :STRIP]
            for g in range(GROUP):
                first = h * GROUP_ROWS + g * LEVELS
                table_ref[c, first : first + LEVELS, g * LEVELS : g * LEVELS + STRIP] = strip


def finish_kernel(parity_ref, mine_ref, other_ref, weights_ref, norm_ref, bias_ref, weights_out_ref, norm_out_ref,
                  strip_ref, turned_ref):
    pairs, offsets = pair_order(), offset_order()
    low = parity_ref[0] == 0
    mine, other = mine_ref[...], other_ref[...]
    halves = (jnp.where(low, mine, other), jnp.where(low, other, mine))
    strip_ref[...] = jnp.zeros_like(strip_ref)
    strips = []
    for half in halves:
        tail = half[112:130]
        last = jnp.concatenate([tail[:, :20], tail[:, 20:40], tail[:, 40:60]], axis=0)
        strips.append(jnp.concatenate([half[:54], half[56:110], last], axis=1))
    for c in range(PW):
        for h in range(HEADS):
            strip = strips[h // 3]
            if c == 1:
                first = (h % 3) * LEVELS
                part = strip[first : first + LEVELS]
            else:
                first = 3 * LEVELS + (h % 3) * WLAT
                part = strip[first : first + WLAT]
                key_level = (lax.broadcasted_iota(jnp.int32, part.shape, 1) % LEVELS) // WLAT
                part = jnp.concatenate([jnp.where(key_level == i, part, 0.0) for i in range(WZ)], axis=0)
            strip_ref[h * PADDED : h * PADDED + LEVELS, :STRIP] = part
        by_level = dot_right_transposed(strip_ref[...], offsets, FULL)
        for h in range(HEADS):
            for key in range(LEVELS):
                turned_ref[key * PADDED : (key + 1) * PADDED, h * LONREL : (h + 1) * LONREL] = by_level[
                    h * PADDED : (h + 1) * PADDED, key * OFFSETS : key * OFFSETS + LONREL
                ]
        rows = dot_left_transposed(turned_ref[...], pairs, FULL)
        for h in range(HEADS):
            bias_ref[h, :, c, :] = rows[h * LONREL : (h + 1) * LONREL]
    weights_out_ref[...] = unpacked_chunk(weights_ref[...])
    norm_out_ref[:, :128] = norm_ref[:2]
    norm_out_ref[0:1, 128:] = norm_ref[2:3, :64]
    norm_out_ref[1:2, 128:] = norm_ref[2:3, 64:]


def packed_chunk(chunk):
    beside = jnp.concatenate([chunk[40:, 32 * piece : 32 * (piece + 1)] for piece in range(3)], axis=0)
    beside = jnp.concatenate([beside, jnp.zeros((16, 32), chunk.dtype)], axis=0)
    return jnp.concatenate([chunk[:40], beside], axis=1)


def unpacked_chunk(packed):
    last = jnp.concatenate([packed[8 * piece : 8 * (piece + 1), 96:] for piece in range(3)], axis=1)
    return jnp.concatenate([packed[:, :96], last], axis=0)


def block_kernel(
    factor, packed,
    own_ref, borrowed_ref, gain_ref, shift_ref, qkv_ref, out_w_ref, table_ref,
    grad_own_ref, grad_borrowed_ref, weights_ref, strip_grad_ref, norm_ref,
    table_grad_ref, sums_ref,
):
    gain = gain_ref[...]
    shift = shift_ref[...]
    weight_q = qkv_ref[:, :D]
    weight_k = qkv_ref[:, D : 2 * D]
    weight_v = qkv_ref[:, 2 * D :]
    out_weight = out_w_ref[...]
    head_of_lane = lax.broadcasted_iota(jnp.int32, (GROUP_ROWS, D), 1) // HEAD

    def stacked(value):
        blocks = []
        for g in range(GROUPS):
            rows = value[g * GROUP_ROWS : (g + 1) * GROUP_ROWS]
            for h in range(HEADS):
                blocks.append(jnp.where(head_of_lane == h, rows, 0.0))
        return jnp.concatenate(blocks, axis=0)

    def unstacked(value):
        blocks = []
        for g in range(GROUPS):
            total = None
            for h in range(HEADS):
                first = g * BLOCK + h * GROUP_ROWS
                part = jnp.where(head_of_lane == h, value[first : first + GROUP_ROWS], 0.0)
                total = part if total is None else total + part
            blocks.append(total)
        return jnp.concatenate(blocks, axis=0)

    grad_q_w = grad_k_w = grad_v_w = grad_out_w = None
    gain_sum = shift_sum = None
    results = []
    strip_parts = ([], [])
    for c in range(PW):
        both = jnp.concatenate(
            [jnp.concatenate([borrowed_ref[t, c], own_ref[t, c]], axis=0) for t in range(3)], axis=1
        )
        band = both[:, :D]
        window_grad = jnp.concatenate([both[:, 256:], both[:, D:256]], axis=1)
        average = jnp.mean(band, axis=-1, keepdims=True)
        centred = band - average
        inverse = lax.rsqrt(jnp.mean(centred * centred, axis=-1, keepdims=True) + EPSILON)
        unit = centred * inverse
        tokens = unit * gain + shift
        queries = dot(tokens, weight_q, FULL) * SCALE
        keys = dot(tokens, weight_k, FULL)
        values = dot(tokens, weight_v)
        grad_mixture = dot_right_transposed(window_grad, out_weight)
        query_stack = stacked(queries)
        grad_stack = stacked(grad_mixture)

        scores = dot_right_transposed(query_stack, keys, FULL)
        biased = []
        for g in range(GROUPS):
            start = (WLON - 1 - GROUP * g) * LEVELS
            biased.append(scores[g * BLOCK : (g + 1) * BLOCK] + table_ref[c, :, start : start + WIN])
        scores = jnp.concatenate(biased, axis=0)
        exponent = jnp.exp(scores - jnp.max(scores, axis=-1, keepdims=True))
        attention = exponent * (1.0 / jnp.sum(exponent, axis=-1, keepdims=True))
        mixture = unstacked(dot(attention, values))
        grad_attention = dot_right_transposed(grad_stack, values)
        weighted = jnp.sum(attention * grad_attention, axis=-1, keepdims=True)
        grad_scores = attention * (grad_attention - weighted)
        grad_values = dot_left_transposed(attention, grad_stack)
        grad_queries = unstacked(dot(grad_scores, keys)) * SCALE
        grad_keys = dot_left_transposed(grad_scores, query_stack)

        table_grad_ref[...] = jnp.zeros_like(table_grad_ref)
        for g in range(GROUPS):
            start = (WLON - 1 - GROUP * g) * LEVELS
            table_grad_ref[:, start : start + WIN] += grad_scores[g * BLOCK : (g + 1) * BLOCK]
        for half in range(2):
            strips = []
            for h in range(3 * half, 3 * half + 3):
                total = None
                for g in range(GROUP):
                    first = h * GROUP_ROWS + g * LEVELS
                    part = table_grad_ref[first : first + LEVELS, g * LEVELS : g * LEVELS + STRIP]
                    total = part if total is None else total + part
                strips.append(total if c == 1 else total[:WLAT] + total[WLAT:])
            strip_parts[half].insert(0, jnp.concatenate(strips, axis=0))

        parts = (
            dot_left_transposed(tokens, grad_queries),
            dot_left_transposed(tokens, grad_keys),
            dot_left_transposed(tokens, grad_values),
            dot_left_transposed(mixture, window_grad),
        )
        for block, part in enumerate(parts):
            if c == 0:
                sums_ref[block] = part
            else:
                sums_ref[block] += part
        grad_tokens = (
            dot_right_transposed(grad_queries, weight_q)
            + dot_right_transposed(grad_keys, weight_k)
            + dot_right_transposed(grad_values, weight_v)
        )
        gain_part = jnp.sum(grad_tokens * unit, axis=0, keepdims=True)
        shift_part = jnp.sum(grad_tokens, axis=0, keepdims=True)
        gain_sum = gain_part if c == 0 else gain_sum + gain_part
        shift_sum = shift_part if c == 0 else shift_sum + shift_part
        grad_unit = grad_tokens * gain
        result = window_grad + inverse * (
            grad_unit
            - jnp.mean(grad_unit, axis=-1, keepdims=True)
            - unit * jnp.mean(grad_unit * unit, axis=-1, keepdims=True)
        )
        results.append(result)
    for ref, rows in ((grad_borrowed_ref, slice(0, HALF_ROWS)), (grad_own_ref, slice(HALF_ROWS, WIN))):
        for c in range(PW):
            ref[c] = results[c][rows, :128]
        ref[2] = jnp.concatenate([result[rows, 128:] for result in results], axis=1)
    for half in range(2):
        strip = jnp.concatenate(strip_parts[half], axis=0)
        strip_grad_ref[half] = jnp.zeros_like(strip_grad_ref[half])
        strip_grad_ref[half, :54, :] = strip[:, :128]
        strip_grad_ref[half, 56:110, :] = strip[:, 128:256]
        for piece in range(3):
            strip_grad_ref[half, 112:130, 20 * piece : 20 * (piece + 1)] = strip[18 * piece : 18 * (piece + 1), 256:]
    gain_sum, shift_sum = gain_sum * factor, shift_sum * factor
    norm_ref[...] = jnp.zeros_like(norm_ref)
    norm_ref[:3] = jnp.concatenate(
        [gain_sum[:, :128], shift_sum[:, :128], jnp.concatenate([gain_sum[:, 128:], shift_sum[:, 128:]], axis=1)], axis=0
    )
    for block in range(4):
        part = sums_ref[block] * factor
        if not packed:
            weights_ref[:, block * D : (block + 1) * D] = part
            continue
        for y in range(2):
            for lat in range(4):
                chunk = part[48 * lat : 48 * (lat + 1), 96 * y : 96 * (y + 1)]
                weights_ref[lat % 2, y, block % 2, block // 2, lat // 2] = packed_chunk(chunk)


def exchanged(value, axis, bit):
    count = lax.axis_size(axis)
    return lax.ppermute(value, axis, [(source, source ^ bit) for source in range(count)])


def bits_of(count):
    return [1 << place for place in range(count.bit_length() - 1)]


def kept_and_given(value, axis, bit):
    high = (lax.axis_index(axis) // bit) % 2
    return (
        lax.dynamic_index_in_dim(value, high, 0, keepdims=False),
        lax.dynamic_index_in_dim(value, 1 - high, 0, keepdims=False),
    )


def exchange_all(values, axis, bit):
    flat = [value.reshape(-1, 128) for value in values]
    arrived = exchanged(jnp.concatenate(flat, axis=0), axis, bit)
    results, first = [], 0
    for value, rows in zip(values, flat):
        results.append(arrived[first : first + rows.shape[0]].reshape(value.shape))
        first += rows.shape[0]
    return results


def chunk_order(lat_count, lon_count):
    lat_bits, lon_bits = bits_of(lat_count), bits_of(lon_count)
    return [("lat", lat_bits[0])] + [("lon", bit) for bit in lon_bits] + [("lat", bit) for bit in lat_bits[1:]]


def chunks_by_bit(weights, lat_count, lon_count):
    rows, columns = weights.shape[0] // lat_count, weights.shape[1] // lon_count
    lat_places, lon_places = len(bits_of(lat_count)), len(bits_of(lon_count))
    split = weights.reshape((2,) * lat_places + (rows,) + (2,) * lon_places + (columns,))
    lat_dims = list(range(lat_places))[::-1]
    lon_dims = list(range(lat_places + 1, lat_places + 1 + lon_places))[::-1]
    order = lat_dims[:1] + lon_dims + lat_dims[1:] + [lat_places, lat_places + 1 + lon_places]
    places = lat_places + lon_places
    split = split.transpose(order).reshape((2,) * places + (rows * columns,))
    words = -(-rows * columns // 1024) * 1024
    split = jnp.pad(split, [(0, 0)] * places + [(0, words - rows * columns)])
    return split.reshape((2,) * places + (words // 128, 128))


def shards(features, cotangent, norm_gain, norm_shift, qkv_weight, out_weight, bias_table):
    lat_count, lon_count = lax.axis_size("lat"), lax.axis_size("lon")
    token_count = ZP * features.shape[1] * features.shape[2] * lat_count * lon_count
    factor = 1.0 / math.sqrt(token_count)
    packed = (lat_count, lon_count) == (4, 8)
    f32 = jnp.float32
    shape = jax.ShapeDtypeStruct
    params = pltpu.CompilerParams(vmem_limit_bytes=48 << 20)
    half_shape = shape((3, PW, HALF_ROWS, 128), f32)
    sent, own = pl.pallas_call(
        pack_kernel, out_shape=(half_shape, half_shape), in_specs=whole(2), out_specs=tuple(whole(2)),
        compiler_params=params,
    )(features.transpose(1, 2, 0, 3), cotangent.transpose(1, 2, 0, 3))
    borrowed = lax.ppermute(sent, "lon", [(s, (s + 1) % lon_count) for s in range(lon_count)])
    table = pl.pallas_call(
        table_kernel,
        out_shape=shape((PW, GROUP_ROWS * HEADS, 384), f32),
        in_specs=whole(1),
        out_specs=whole(1)[0],
        scratch_shapes=[
            pltpu.VMEM((LEVELS * PADDED, HEADS * LONREL), f32),
            pltpu.VMEM((HEADS * PADDED, LEVELS * OFFSETS), f32),
        ],
        compiler_params=params,
    )(bias_table[0].transpose(1, 2, 0, 3))
    grad_half = shape((3, HALF_ROWS, 128), f32)
    grad_own, grad_borrowed, weights, strip_grad, norm = pl.pallas_call(
        functools.partial(block_kernel, factor, packed),
        out_shape=(
            grad_half,
            grad_half,
            shape((2, 2, 2, 2, 2, 40, 128) if packed else (D, 4 * D), f32),
            shape((2, 136, 128), f32),
            shape((8, 128), f32),
        ),
        in_specs=whole(7),
        out_specs=tuple(whole(5)),
        scratch_shapes=[pltpu.VMEM((BLOCK, 384), f32), pltpu.VMEM((4, D, D), f32)],
        compiler_params=params,
    )(own, borrowed, norm_gain[None], norm_shift[None], qkv_weight, out_weight, table)
    if not packed:
        weights = chunks_by_bit(weights, lat_count, lon_count)
    returned = lax.ppermute(grad_borrowed, "lon", [(s, (s - 1) % lon_count) for s in range(lon_count)])
    grad_features = pl.pallas_call(
        unpack_kernel,
        out_shape=shape((WLAT, WLON, ZP, D), f32),
        in_specs=whole(2),
        out_specs=whole(1)[0],
        compiler_params=params,
    )(grad_own, returned).transpose(2, 0, 1, 3)
    other_strip = None
    for axis, bit in chunk_order(lat_count, lon_count):
        kept, given = kept_and_given(weights, axis, bit)
        if axis == "lon" and bit == 1:
            kept_strip, given_strip = kept_and_given(strip_grad, axis, bit)
            more, more_strip, more_norm = exchange_all([given, given_strip, norm], axis, bit)
            strip_grad = kept_strip + more_strip
        elif axis == "lon":
            more, more_strip, more_norm = exchange_all([given, strip_grad, norm], axis, bit)
            strip_grad = strip_grad + more_strip
        else:
            if bit > 1 and other_strip is None:
                other_strip = exchanged(strip_grad, "lon", 1)
            more, more_norm = exchange_all([given, norm], axis, bit)
        weights, norm = kept + more, norm + more_norm
    if packed:
        chunk = weights
    else:
        chunk = jnp.zeros((40, 128), f32)
    parity = (lax.axis_index("lon") % 2).astype(jnp.int32)[None]
    grad_bias, grad_weights, grad_norm = pl.pallas_call(
        finish_kernel,
        out_shape=(shape((HEADS, LONREL, PW, PAIRS), f32), shape((48, 96), f32), shape((2, D), f32)),
        in_specs=[pl.BlockSpec(memory_space=pltpu.SMEM)] + whole(4),
        out_specs=tuple(whole(3)),
        scratch_shapes=[
            pltpu.VMEM((HEADS * PADDED, LEVELS * OFFSETS), f32),
            pltpu.VMEM((LEVELS * PADDED, HEADS * LONREL), f32),
        ],
        compiler_params=params,
    )(parity, strip_grad, other_strip, chunk, norm)
    grad_bias = grad_bias.transpose(2, 0, 1, 3)[None]
    if not packed:
        rows, columns = D // lat_count, 4 * D // lon_count
        grad_weights = weights.reshape(-1)[: rows * columns].reshape(rows, columns)
    return (grad_features, grad_weights, grad_bias, grad_norm)


def solution(mesh):
    placed = (
        P(None, "lat", "lon", None),
        P(None, "lat", "lon", None),
        P(),
        P(),
        P(),
        P(),
        P("lat", None, None, None, None),
    )
    return jax.shard_map(
        shards,
        mesh=mesh,
        in_specs=placed,
        out_specs=(
            P(None, "lat", "lon", None),
            P("lat", "lon"),
            P("lat", None, None, None, None),
            P(),
        ),
        check_vma=False,
    )
```

time: 92 us -> 58.2 us (0.63)
  local copies, waits for them, and re-layouts: 26.3 us -> 2.75 us
  starting transfers between devices: 22.1 us -> 7.95 us
  waiting for transfers between devices: 25.3 us -> 28.8 us
  Pallas kernels: 14.2 us -> 17.3 us
  other arithmetic: 2.93 us -> 0.22 us
    ppermute x13 -> x6, starting transfers between devices: 15.8 us -> 2.92 us  [exchanged(): lax.ppermute(value, axis, [(source, source ^ bit) for source in range(cou...]
    transpose x2 -> x0, local copies, waits for them, and re-layouts: 7.84 us -> none  [the longest x1 4.14 us: shards(): bias_table.reshape(PW, HEADS, LONREL, WZ, WZ, WLAT, WLAT)]
    unnamed x19 -> x14, local copies, waits for them, and re-layouts: 10.4 us -> 2.6 us
    reshape x2 -> x0, local copies, waits for them, and re-layouts: 7.18 us -> none  [the longest x1 3.97 us: shards(): strip = strip.reshape(PW, HEADS * LEVELS, STRIP)]
    ppermute x1, waiting for transfers between devices: 0.01 us -> 6.25 us  [shards(): lax.ppermute(sent, 'lon', [(s, (s + 1) % lon_count) for s in range(lon_co...]
    ppermute x13 -> x6, waiting for transfers between devices: 25.3 us -> 19.8 us  [exchanged(): lax.ppermute(value, axis, [(source, source ^ bit) for source in range(cou...]
    pallas_call x2 -> x4, Pallas kernels: 12.2 us -> 17.1 us  [the longest x1 10.4 us: shards(): pl.pallas_call(functools.partial(block_kernel, factor, packed), out_shape...]
    add x13, other arithmetic: 2.93 us -> 0.15 us  [the longest x10 0.11 us: shards(): weights, norm = (kept + more, norm + more_norm)]
  transfers between devices with their start and end apart: 15 -> 8, of which waited for: 8 -> 8; matrix products, arithmetic and copies ran while one was open for 25% -> 0% of each run, Pallas kernels for 2% -> 5%
where the time goes in v2:
time: 58.2 us; the launch traced here: 58 us
  waiting for transfers between devices  28.8 us (49%)
  Pallas kernels  17.3 us (30%)
  starting transfers between devices  7.95 us (14%)
  local copies, waits for them, and re-layouts  2.75 us (5%)
  between operations  0.99 us (2%)
    ppermute x6, waiting for transfers between devices, exchanged(): lax.ppermute(value, axis, [(source, source ^ bit) for source in range(cou...  19.8 us
    pallas_call x1, Pallas kernels, shards(): pl.pallas_call(functools.partial(block_kernel, factor, packed), out_shape...  10.4 us
    ppermute x1, waiting for transfers between devices, shards(): lax.ppermute(sent, 'lon', [(s, (s + 1) % lon_count) for s in range(lon_co...  6.25 us
    pallas_call x1, Pallas kernels, shards(): pl.pallas_call(finish_kernel, out_shape=(shape((HEADS, LONREL, PW, PAIRS)...  3.49 us
    ppermute x1, starting transfers between devices, shards(): lax.ppermute(sent, 'lon', [(s, (s + 1) % lon_count) for s in range(lon_co...  3.02 us
    ppermute x6, starting transfers between devices, exchanged(): lax.ppermute(value, axis, [(source, source ^ bit) for source in range(cou...  2.92 us
    ppermute x1, waiting for transfers between devices, shards(): lax.ppermute(grad_borrowed, 'lon', [(s, (s - 1) % lon_count) for s in ran...  2.73 us
    unnamed x14, local copies, waits for them, and re-layouts  2.6 us
  transfers between devices with their start and end apart: 8, of which 8 were waited for; matrix products, arithmetic and copies ran while one was open for 0% of the time, Pallas kernels for 5%

profile of v2, /device:TPU:0, one launch (start us, length us, event | category | flops | bytes accessed | tf_op | source)
XLA Modules:
  0.0 58.0 jit_solution(11965945490387930429)
XLA Ops:
  0.6 0.0 copy-start.1
  0.6 1.0 %copy-done.1 = f32[4,6,12,192]{3,0,2,1:T(4,128)S(1)} copy-done((f32[4,6,12,192]{3,0,2,1:T(4,128)S(1)}, f32[4,6,12,192]{3,0,2,1:T(4,128)}, u32[]{:S(2)}) %copy-start.1) | copy-done | bytes 221208
  1.6 0.0 copy-start.2
  1.6 1.0 %copy-done.2 = f32[4,6,12,192]{3,0,2,1:T(4,128)S(1)} copy-done((f32[4,6,12,192]{3,0,2,1:T(4,128)S(1)}, f32[4,6,12,192]{3,0,2,1:T(4,128)}, u32[]{:S(2)}) %copy-start.2) | copy-done | bytes 221208
  2.6 0.0 copy-start.3
  2.6 0.2 shard_map.102
  2.8 3.0 %collective-permute-start = (f32[3,2,72,128]{3,2,1,0:T(8,128)S(1)}, f32[3,2,72,128]{3,2,1,0:T(8,128)S(1)}, u32[]{:S(2)}, u32[]{:S(2)}) collective-permute-start(f32[3,2,72,128]{3,2,1,0:T(8,128)S(1)} %get-tuple-element.15), channel_id=1, source_target_pairs={{0,1},{1,2},{2,3},{3,4},{4,5},{5,6},{6,7},{7,0},{8,9},{9,10},{10,1... | collective-permute-start | bytes 663560 | tf_op jit(solution)/shard_map/ppermute | solution.py:373
  5.8 0.0 copy-done.3
  5.8 0.0 copy-start
  5.8 0.0 copy-start.4
  5.8 0.0 copy-start.6
  5.8 2.2 %shard_map.103.table_ref = f32[2,288,384]{2,1,0:T(8,128)S(1)} custom-call(f32[6,23,2,144]{3,2,1,0:T(2,128)S(1)} %bitcast.38), custom_call_target="tpu_custom_call" | custom-call | tf_op jit(solution)/shard_map/pallas_call | solution.py:374
  8.0 6.3 %collective-permute-done.borrowed_ref = f32[3,2,72,128]{3,2,1,0:T(8,128)S(1)} collective-permute-done((f32[3,2,72,128]{3,2,1,0:T(8,128)S(1)}, f32[3,2,72,128]{3,2,1,0:T(8,128)S(1)}, u32[]{:S(2)}, u32[]{:S(2)}) %collective-permute-start) | collective-permute-done | bytes 221216 | tf_op jit(solution)/shard_map/ppermute | solution.py:373
  14.3 0.0 copy-start.5
  14.3 0.0 copy-done
  14.3 0.0 copy-done.4
  14.3 0.0 copy-done.6
  14.3 0.7 %copy-done.5 = f32[192]{0:T(256)S(1)} copy-done((f32[192]{0:T(256)S(1)}, f32[192]{0:T(256)}, u32[]{:S(2)}) %copy-start.5) | copy-done | bytes 792
  15.0 10.4 %shard_map.104 = (f32[3,72,128]{2,1,0:T(8,128)S(1)}, f32[3,72,128]{2,1,0:T(8,128)S(1)}, f32[2,2,2,2,2,40,128]{6,5,4,3,2,1,0:T(8,128)S(1)}, f32[2,136,128]{2,1,0:T(8,128)S(1)}, f32[8,128]{1,0:T(8,128)S(1)}) custom-call(f32[3,2,72,128]{3,2,1,0:T(8,128)S(1)} %get-tuple-element.14.own_ref, f32[3,2,72,128]{3,2,1,0:T(8,128)S(1)} %collective-permute-done.borrowed_ref, ...), custom_call_target="tpu_custom_call" | custom-call | tf_op jit(solution)/shard_map/pallas_call | solution.py:386
  25.5 0.1 collective-permute-start.2
  25.6 1.6 %collective-permute-done.2 = f32[648,128]{1,0:T(8,128)S(1)} collective-permute-done((f32[648,128]{1,0:T(8,128)S(1)}, f32[648,128]{1,0:T(8,128)S(1)}, u32[]{:S(2)}, u32[]{:S(2)}) %collective-permute-start.2) | collective-permute-done | bytes 331808 | tf_op jit(solution)/shard_map/ppermute | solution.py:316
  27.3 0.1 collective-permute-start.3
  27.4 7.8 %collective-permute-done.3 = f32[464,128]{1,0:T(8,128)S(1)} collective-permute-done((f32[464,128]{1,0:T(8,128)S(1)}, f32[464,128]{1,0:T(8,128)S(1)}, u32[]{:S(2)}, u32[]{:S(2)}) %collective-permute-start.3) | collective-permute-done | bytes 237600 | tf_op jit(solution)/shard_map/ppermute | solution.py:316
  35.3 0.1 collective-permute-start.4
  35.4 5.2 %collective-permute-done.4 = f32[304,128]{1,0:T(8,128)S(1)} collective-permute-done((f32[304,128]{1,0:T(8,128)S(1)}, f32[304,128]{1,0:T(8,128)S(1)}, u32[]{:S(2)}, u32[]{:S(2)}) %collective-permute-start.4) | collective-permute-done | bytes 155680 | tf_op jit(solution)/shard_map/ppermute | solution.py:316
  40.7 0.7 %collective-permute-start.5 = (f32[224,128]{1,0:T(8,128)S(1)}, f32[224,128]{1,0:T(8,128)S(1)}, u32[]{:S(2)}, u32[]{:S(2)}) collective-permute-start(f32[224,128]{1,0:T(8,128)S(1)} %pad_maximum_fusion.3), channel_id=1, source_target_pairs={{0,4},{1,5},{2,6},{3,7},{4,0},{5,1},{6,2},{7,3},{8,12},{9,13},{10,... | collective-permute-start | bytes 344072 | tf_op jit(solution)/shard_map/ppermute | solution.py:316
  41.4 2.0 %collective-permute-start.1 = (f32[3,72,128]{2,1,0:T(8,128)S(1)}, f32[3,72,128]{2,1,0:T(8,128)S(1)}, u32[]{:S(2)}, u32[]{:S(2)}) collective-permute-start(f32[3,72,128]{2,1,0:T(8,128)S(1)} %get-tuple-element.17), channel_id=1, source_target_pairs={{0,7},{1,0},{2,1},{3,2},{4,3},{5,4},{6,5},{7,6},{8,15},{9,8},{10,9... | collective-permute-start | bytes 331784 | tf_op jit(solution)/shard_map/ppermute | solution.py:402
  43.5 2.7 %collective-permute-done.1.returned_ref = f32[3,72,128]{2,1,0:T(8,128)S(1)} collective-permute-done((f32[3,72,128]{2,1,0:T(8,128)S(1)}, f32[3,72,128]{2,1,0:T(8,128)S(1)}, u32[]{:S(2)}, u32[]{:S(2)}) %collective-permute-start.1) | collective-permute-done | bytes 110624 | tf_op jit(solution)/shard_map/ppermute | solution.py:402
  46.2 1.0 %shard_map.105 = f32[6,12,4,192]{3,2,1,0:T(4,128)} custom-call(f32[3,72,128]{2,1,0:T(8,128)S(1)} %get-tuple-element.16.own_ref, f32[3,72,128]{2,1,0:T(8,128)S(1)} %collective-permute-done.1.returned_ref), custom_call_target="tpu_custom_call" | custom-call | tf_op jit(solution)/shard_map/pallas_call | solution.py:403
  47.2 1.3 %collective-permute-done.5 = f32[224,128]{1,0:T(8,128)S(1)} collective-permute-done((f32[224,128]{1,0:T(8,128)S(1)}, f32[224,128]{1,0:T(8,128)S(1)}, u32[]{:S(2)}, u32[]{:S(2)}) %collective-permute-start.5) | collective-permute-done | bytes 114720 | tf_op jit(solution)/shard_map/ppermute | solution.py:316
  48.6 1.6 %collective-permute-start.7 = (f32[48,128]{1,0:T(8,128)S(1)}, f32[48,128]{1,0:T(8,128)S(1)}, u32[]{:S(2)}, u32[]{:S(2)}) collective-permute-start(f32[48,128]{1,0:T(8,128)S(1)} %pad_maximum_fusion.4), channel_id=1, source_target_pairs={{0,16},{8,24},{16,0},{24,8},{1,17},{9,25},{17,1},{25,9},{2,18},{10... | collective-permute-start | bytes 73736 | tf_op jit(solution)/shard_map/ppermute | solution.py:316
  50.2 0.4 collective-permute-start.6
  50.6 1.9 %collective-permute-done.7 = f32[48,128]{1,0:T(8,128)S(1)} collective-permute-done((f32[48,128]{1,0:T(8,128)S(1)}, f32[48,128]{1,0:T(8,128)S(1)}, u32[]{:S(2)}, u32[]{:S(2)}) %collective-permute-start.7) | collective-permute-done | bytes 24608 | tf_op jit(solution)/shard_map/ppermute | solution.py:316
  52.5 2.0 %collective-permute-done.6.other_ref = f32[136,128]{1,0:T(8,128)S(1)} collective-permute-done((f32[136,128]{1,0:T(8,128)S(1)}, f32[136,128]{1,0:T(8,128)S(1)}, u32[]{:S(2)}, u32[]{:S(2)}) %collective-permute-start.6) | collective-permute-done | bytes 69664 | tf_op jit(solution)/shard_map/ppermute | solution.py:316
  54.5 3.5 %shard_map.106 = (f32[6,23,2,144]{3,2,1,0:T(2,128)}, f32[48,96]{1,0:T(8,128)}, f32[2,192]{1,0:T(2,128)}) custom-call(s32[1]{0:T(128)} %bitcast.7.parity_ref, f32[136,128]{1,0:T(8,128)S(1)} %slice_add_fusion.mine_ref, f32[136,128]{1,0:T(8,128)S(1)} %collective-permute-done.6.other_ref, f32[40,128]{1,0:T(8,128)S(1)} %slice_add_fusion.3.weights_ref, ...), custom_call_target="tpu_custom_call" | custom-call | tf_op jit(solution)/shard_map/pallas_call | solution.py:430
  (28 shorter events, 0.4 us)
Async XLA Ops:
  0.6 1.0 %copy-start.1 = (f32[4,6,12,192]{3,0,2,1:T(4,128)S(1)}, f32[4,6,12,192]{3,0,2,1:T(4,128)}, u32[]{:S(2)}) copy-start(f32[4,6,12,192]{3,0,2,1:T(4,128)} %param.7) | copy-start | bytes 663556
  1.6 1.0 %copy-start.2 = (f32[4,6,12,192]{3,0,2,1:T(4,128)S(1)}, f32[4,6,12,192]{3,0,2,1:T(4,128)}, u32[]{:S(2)}) copy-start(f32[4,6,12,192]{3,0,2,1:T(4,128)} %param.8) | copy-start | bytes 663556
  2.6 3.3 %copy-start.3 = (f32[1,2,6,23,144]{4,1,3,2,0:T(2,128)S(1)}, f32[1,2,6,23,144]{4,1,3,2,0:T(2,128)}, u32[]{:S(2)}) copy-start(f32[1,2,6,23,144]{4,1,3,2,0:T(2,128)} %param.13) | copy-start | bytes 476932
  2.8 11.5 %collective-permute-start = (f32[3,2,72,128]{3,2,1,0:T(8,128)S(1)}, f32[3,2,72,128]{3,2,1,0:T(8,128)S(1)}, u32[]{:S(2)}, u32[]{:S(2)}) collective-permute-start(f32[3,2,72,128]{3,2,1,0:T(8,128)S(1)} %get-tuple-element.15), channel_id=1, source_target_pairs={{0,1},{1,2},{2,3},{3,4},{4,5},{5,6},{6,7},{7,0},{8,9},{9,10},{10,1... | collective-permute-start | bytes 663560 | tf_op jit(solution)/shard_map/ppermute | solution.py:373
  5.8 8.5 %copy-start = (f32[192,576]{1,0:T(8,128)S(1)}, f32[192,576]{1,0:T(8,128)}, u32[]{:S(2)}) copy-start(f32[192,576]{1,0:T(8,128)} %qkv_ref.1) | copy-start | bytes 1327108
  5.8 8.5 %copy-start.4 = (f32[192,192]{1,0:T(8,128)S(1)}, f32[192,192]{1,0:T(8,128)}, u32[]{:S(2)}) copy-start(f32[192,192]{1,0:T(8,128)} %out_w_ref.1) | copy-start | bytes 442372
  5.8 8.5 %copy-start.6 = (f32[192]{0:T(256)S(1)}, f32[192]{0:T(256)}, u32[]{:S(2)}) copy-start(f32[192]{0:T(256)} %param.10) | copy-start | bytes 2308
  14.3 0.7 %copy-start.5 = (f32[192]{0:T(256)S(1)}, f32[192]{0:T(256)}, u32[]{:S(2)}) copy-start(f32[192]{0:T(256)} %param.9) | copy-start | bytes 2308
  25.5 1.7 %collective-permute-start.2 = (f32[648,128]{1,0:T(8,128)S(1)}, f32[648,128]{1,0:T(8,128)S(1)}, u32[]{:S(2)}, u32[]{:S(2)}) collective-permute-start(f32[648,128]{1,0:T(8,128)S(1)} %pad_maximum_fusion), channel_id=1, source_target_pairs={{0,8},{8,0},{16,24},{24,16},{1,9},{9,1},{17,25},{25,17},{2,10},{10... | collective-permute-start | bytes 995336 | tf_op jit(solution)/shard_map/ppermute | solution.py:316
  27.3 7.9 %collective-permute-start.3 = (f32[464,128]{1,0:T(8,128)S(1)}, f32[464,128]{1,0:T(8,128)S(1)}, u32[]{:S(2)}, u32[]{:S(2)}) collective-permute-start(f32[464,128]{1,0:T(8,128)S(1)} %pad_maximum_fusion.1), channel_id=1, source_target_pairs={{0,1},{1,0},{2,3},{3,2},{4,5},{5,4},{6,7},{7,6},{8,9},{9,8},{10,11... | collective-permute-start | bytes 712712 | tf_op jit(solution)/shard_map/ppermute | solution.py:316
  35.3 5.3 %collective-permute-start.4 = (f32[304,128]{1,0:T(8,128)S(1)}, f32[304,128]{1,0:T(8,128)S(1)}, u32[]{:S(2)}, u32[]{:S(2)}) collective-permute-start(f32[304,128]{1,0:T(8,128)S(1)} %pad_maximum_fusion.2), channel_id=1, source_target_pairs={{0,2},{1,3},{2,0},{3,1},{4,6},{5,7},{6,4},{7,5},{8,10},{9,11},{10,... | collective-permute-start | bytes 466952 | tf_op jit(solution)/shard_map/ppermute | solution.py:316
  40.7 7.8 %collective-permute-start.5 = (f32[224,128]{1,0:T(8,128)S(1)}, f32[224,128]{1,0:T(8,128)S(1)}, u32[]{:S(2)}, u32[]{:S(2)}) collective-permute-start(f32[224,128]{1,0:T(8,128)S(1)} %pad_maximum_fusion.3), channel_id=1, source_target_pairs={{0,4},{1,5},{2,6},{3,7},{4,0},{5,1},{6,2},{7,3},{8,12},{9,13},{10,... | collective-permute-start | bytes 344072 | tf_op jit(solution)/shard_map/ppermute | solution.py:316
  41.4 4.7 %collective-permute-start.1 = (f32[3,72,128]{2,1,0:T(8,128)S(1)}, f32[3,72,128]{2,1,0:T(8,128)S(1)}, u32[]{:S(2)}, u32[]{:S(2)}) collective-permute-start(f32[3,72,128]{2,1,0:T(8,128)S(1)} %get-tuple-element.17), channel_id=1, source_target_pairs={{0,7},{1,0},{2,1},{3,2},{4,3},{5,4},{6,5},{7,6},{8,15},{9,8},{10,9... | collective-permute-start | bytes 331784 | tf_op jit(solution)/shard_map/ppermute | solution.py:402
  48.6 3.9 %collective-permute-start.7 = (f32[48,128]{1,0:T(8,128)S(1)}, f32[48,128]{1,0:T(8,128)S(1)}, u32[]{:S(2)}, u32[]{:S(2)}) collective-permute-start(f32[48,128]{1,0:T(8,128)S(1)} %pad_maximum_fusion.4), channel_id=1, source_target_pairs={{0,16},{8,24},{16,0},{24,8},{1,17},{9,25},{17,1},{25,9},{2,18},{10... | collective-permute-start | bytes 73736 | tf_op jit(solution)/shard_map/ppermute | solution.py:316
  50.2 4.4 %collective-permute-start.6 = (f32[136,128]{1,0:T(8,128)S(1)}, f32[136,128]{1,0:T(8,128)S(1)}, u32[]{:S(2)}, u32[]{:S(2)}) collective-permute-start(f32[136,128]{1,0:T(8,128)S(1)} %slice_add_fusion.mine_ref), channel_id=1, source_target_pairs={{0,1},{1,0},{2,3},{3,2},{4,5},{5,4},{6,7},{7,6},{8,9},{9,8},{10,11... | collective-permute-start | bytes 208904 | tf_op jit(solution)/shard_map/ppermute | solution.py:316

commit v3 on v2

v3 whole, which is shorter than its diff:
```python
import functools
import math

import jax
import jax.numpy as jnp
from jax import lax
from jax.experimental import pallas as pl
from jax.experimental.pallas import tpu as pltpu
from jax.sharding import PartitionSpec as P

D = 192
HEADS = 6
HEAD = 32
ZP = 4
WZ = 2
WLAT = 6
WLON = 12
PW = 2
WIN = 144
LONREL = 23
PAIRS = 144
HALF = WLON // 2
LEVELS = WZ * WLAT
HALF_ROWS = HALF * LEVELS
GROUP = 4
GROUPS = WLON // GROUP
GROUP_ROWS = GROUP * LEVELS
BLOCK = HEADS * GROUP_ROWS
STRIP = LONREL * LEVELS
PADDED = 16
OFFSETS = 24

EPSILON = 1e-05
SCALE = HEAD ** (-0.5)
HIGH = lax.Precision.HIGH
FULL = lax.Precision.HIGHEST


def dot(left, right, precision=HIGH):
    return lax.dot_general(
        left, right, (((1,), (0,)), ((), ())), precision=precision, preferred_element_type=jnp.float32
    )


def dot_right_transposed(left, right, precision=HIGH):
    return lax.dot_general(
        left, right, (((1,), (1,)), ((), ())), precision=precision, preferred_element_type=jnp.float32
    )


def dot_left_transposed(left, right, precision=HIGH):
    return lax.dot_general(
        left, right, (((0,), (0,)), ((), ())), precision=precision, preferred_element_type=jnp.float32
    )


def whole(count):
    return [pl.BlockSpec(memory_space=pltpu.VMEM)] * count


def hbm(*values):
    return [pltpu.with_memory_space_constraint(value, pltpu.HBM) for value in values]


def fetched(pairs, semaphores):
    copies = [pltpu.make_async_copy(*pair, semaphores.at[place]) for place, pair in enumerate(pairs)]
    for copy in copies:
        copy.start()
    return copies


def pack_kernel(features_ref, cotangent_ref, sent_ref, own_ref, band_ref, grad_ref, semaphores):
    for copy in fetched([(features_ref, band_ref), (cotangent_ref, grad_ref)], semaphores):
        copy.wait()
    for a in range(WLAT):
        for x in range(WLON):
            target_ref = own_ref if x < HALF else sent_ref
            band = band_ref[a, x]
            grad = grad_ref[a, x]
            tiles = (band[:, :128], jnp.concatenate([band[:, 128:], grad[:, 128:]], axis=1), grad[:, :128])
            for z in range(ZP):
                c, i = divmod((z + 1) % ZP, WZ)
                row = (x % HALF) * LEVELS + i * WLAT + a
                for tile in range(3):
                    target_ref[tile, c, row : row + 1, :] = tiles[tile][z : z + 1]


def unpack_kernel(own_ref, returned_ref, out_ref):
    for a in range(WLAT):
        for x in range(WLON):
            source_ref = own_ref if x < HALF else returned_ref
            for z in range(ZP):
                c, i = divmod((z + 1) % ZP, WZ)
                row = (x % HALF) * LEVELS + i * WLAT + a
                out_ref[a, x, z : z + 1, :128] = source_ref[c, row : row + 1, :]
                out_ref[a, x, z : z + 1, 128:] = source_ref[2, row : row + 1, c * 64 : (c + 1) * 64]


def pair_order():
    row = lax.broadcasted_iota(jnp.int32, (LEVELS * PADDED, 1), 0)
    key, query = row // PADDED, row % PADDED
    place = (query // WLAT) * 72 + (key // WLAT) * 36 + (query % WLAT) * WLAT + key % WLAT
    place = jnp.where(query < LEVELS, place, -1)
    return (place == lax.broadcasted_iota(jnp.int32, (LEVELS * PADDED, PAIRS), 1)).astype(jnp.bfloat16)


def offset_order():
    row = lax.broadcasted_iota(jnp.int32, (LEVELS * OFFSETS, 1), 0)
    place = (row % OFFSETS) * LEVELS + row // OFFSETS
    columns = lax.broadcasted_iota(jnp.int32, (LEVELS * OFFSETS, LEVELS * OFFSETS), 1)
    return (place == columns).astype(jnp.bfloat16)


def parts_of(value, count):
    parts = []
    for _ in range(count):
        parts.append(value.astype(jnp.bfloat16))
        value = value - parts[-1].astype(jnp.float32)
    return parts


def moved(value, order, dims, count):
    total = None
    for part in parts_of(value, count):
        product = lax.dot_general(part, order, (dims, ((), ())), preferred_element_type=jnp.float32)
        total = product if total is None else total + product
    return total


def normalized(band):
    average = jnp.mean(band, axis=-1, keepdims=True)
    centred = band - average
    inverse = lax.rsqrt(jnp.mean(centred * centred, axis=-1, keepdims=True) + EPSILON)
    return centred * inverse, inverse


def split_tiles(half_ref):
    tiles = [half_ref[tile].reshape(WIN, 128) for tile in range(3)]
    band = jnp.concatenate([tiles[0], tiles[1][:, : D - 128]], axis=1)
    grad = jnp.concatenate([tiles[2], tiles[1][:, D - 128 :]], axis=1)
    return band, grad


def projections(half_ref, out_ref, gain, shift, weight_q, weight_k, weight_v, out_weight):
    band, grad = split_tiles(half_ref)
    unit, inverse = normalized(band)
    tokens = unit * gain + shift
    out_ref[0] = unit
    out_ref[1] = jnp.broadcast_to(inverse, unit.shape)
    out_ref[2] = tokens
    out_ref[3] = grad
    out_ref[4] = dot(tokens, weight_q, FULL) * SCALE
    out_ref[5] = dot(tokens, weight_k, FULL)
    out_ref[6] = dot(tokens, weight_v)
    out_ref[7] = dot_right_transposed(grad, out_weight)


def prepare_kernel(
    bias_hbm, own_ref, gain_hbm, shift_hbm, qkv_hbm, out_w_hbm,
    table_ref, projected_ref, affine_ref, parts_ref,
    turned_ref, strip_ref, bias_ref, qkv_ref, semaphores,
):
    copies = fetched(
        [
            (bias_hbm, bias_ref),
            (gain_hbm, affine_ref.at[0:1]),
            (shift_hbm, affine_ref.at[1:2]),
            (qkv_hbm, qkv_ref),
            (out_w_hbm, parts_ref.at[3]),
        ],
        semaphores,
    )
    pairs, offsets = pair_order(), offset_order()
    for copy in copies:
        copy.wait()
    for part in range(3):
        parts_ref[part] = qkv_ref[:, part * D : (part + 1) * D]
    projections(own_ref, projected_ref, affine_ref[0:1], affine_ref[1:2], *(parts_ref[part] for part in range(4)))
    strip_ref[...] = jnp.zeros_like(strip_ref)
    rows = jnp.concatenate([bias_ref[h, :, c, :] for c in range(PW) for h in range(HEADS)], axis=0)
    turned = None
    for part in parts_of(rows, 3):
        product = lax.dot_general(pairs, part, (((1,), (1,)), ((), ())), preferred_element_type=jnp.float32)
        turned = product if turned is None else turned + product
    turned_ref[...] = turned
    for block in range(PW * HEADS):
        for key in range(LEVELS):
            strip_ref[block * PADDED : (block + 1) * PADDED, key * OFFSETS : key * OFFSETS + LONREL] = turned_ref[
                key * PADDED : (key + 1) * PADDED, block * LONREL : (block + 1) * LONREL
            ]
    strips = moved(strip_ref[...], offsets, ((1,), (0,)), 3)
    row = lax.broadcasted_iota(jnp.int32, strips.shape, 0)
    level = (row % PADDED) // WLAT
    key_level = (lax.broadcasted_iota(jnp.int32, strips.shape, 1) % LEVELS) // WLAT
    strips = jnp.where((row >= HEADS * PADDED) | (level == key_level), strips, -jnp.inf)
    for c in range(PW):
        for h in range(HEADS):
            first = (c * HEADS + h) * PADDED
            strip = strips[first : first + LEVELS, :STRIP]
            for g in range(GROUP):
                first = h * GROUP_ROWS + g * LEVELS
                table_ref[c, first : first + LEVELS, g * LEVELS : g * LEVELS + STRIP] = strip


def turn_kernel(strip_ref, rows_ref, turned_ref):
    pairs, offsets = pair_order(), offset_order()
    by_level = moved(strip_ref[...], offsets, ((1,), (1,)), 2)
    for block in range(PW * HEADS):
        for key in range(LEVELS):
            turned_ref[key * PADDED : (key + 1) * PADDED, block * OFFSETS : (block + 1) * OFFSETS] = by_level[
                block * PADDED : (block + 1) * PADDED, key * OFFSETS : (key + 1) * OFFSETS
            ]
    rows = moved(turned_ref[...], pairs, ((0,), (0,)), 2)
    half = HEADS * OFFSETS // 2
    for y in range(2):
        first, second = rows[y * half : (y + 1) * half], rows[(y + 2) * half : (y + 3) * half]
        rows_ref[y, :half] = second[:, :128]
        rows_ref[y, half:] = jnp.concatenate(
            [second[:, 128:], first[:, :36], first[:, 108:], jnp.zeros((half, 40), jnp.float32)], axis=1
        )


def finish_kernel(parity_ref, mine_ref, other_ref, weights_ref, norm_ref, bias_ref, weights_out_ref, norm_out_ref):
    low = parity_ref[0] == 0
    mine, other = mine_ref[...], other_ref[...]
    halves = (jnp.where(low, mine, other), jnp.where(low, other, mine))
    half = HEADS * OFFSETS // 2
    for h in range(HEADS):
        first = (h % 3) * OFFSETS
        left = halves[h // 3][first : first + LONREL]
        right = halves[h // 3][half + first : half + first + LONREL]
        bias_ref[h, :, 1, :] = jnp.concatenate([left, right[:, :16]], axis=1)
        bias_ref[h, :, 0, :] = jnp.concatenate(
            [right[:, 16:52], jnp.zeros((LONREL, 72), jnp.float32), right[:, 52:88]], axis=1
        )
    weights_out_ref[...] = unpacked_chunk(weights_ref[...])
    norm = norm_ref[:4] + norm_ref[4:]
    norm_out_ref[:, :128] = norm[:2]
    norm_out_ref[0:1, 128:] = norm[2:3, :64]
    norm_out_ref[1:2, 128:] = norm[2:3, 64:]


def packed_chunk(chunk):
    beside = jnp.concatenate([chunk[40:, 32 * piece : 32 * (piece + 1)] for piece in range(3)], axis=0)
    beside = jnp.concatenate([beside, jnp.zeros((16, 32), chunk.dtype)], axis=0)
    return jnp.concatenate([chunk[:40], beside], axis=1)


def unpacked_chunk(packed):
    last = jnp.concatenate([packed[8 * piece : 8 * (piece + 1), 96:] for piece in range(3)], axis=1)
    return jnp.concatenate([packed[:, :96], last], axis=0)


def block_kernel(
    factor, packed,
    borrowed_ref, projected_ref, affine_ref, parts_ref, table_ref,
    grad_own_ref, grad_borrowed_ref, weights_ref, strip_grad_ref, norm_ref,
    table_grad_ref, arrived_ref,
):
    gain, shift = affine_ref[0:1], affine_ref[1:2]
    projections(borrowed_ref, arrived_ref, gain, shift, *(parts_ref[part] for part in range(4)))

    def whole_window(index, c):
        rows = slice(c * HALF_ROWS, (c + 1) * HALF_ROWS)
        return jnp.concatenate([arrived_ref[index, rows], projected_ref[index, rows]], axis=0)

    head_of_lane = lax.broadcasted_iota(jnp.int32, (WIN, D), 1) // HEAD

    def stacked(value):
        return jnp.concatenate([jnp.where(head_of_lane == h, value, 0.0) for h in range(HEADS)], axis=0)

    def unstacked(value):
        total = None
        for h in range(HEADS):
            part = jnp.where(head_of_lane == h, value[h * WIN : (h + 1) * WIN], 0.0)
            total = part if total is None else total + part
        return total

    strip_grad_ref[...] = jnp.zeros_like(strip_grad_ref)
    mixtures, grads_q, grads_k, grads_v = [], [], [], []
    for c in range(PW):
        keys, values = whole_window(5, c), whole_window(6, c)
        query_stack = stacked(whole_window(4, c))
        grad_stack = stacked(whole_window(7, c))
        scores = dot_right_transposed(query_stack, keys, FULL)
        biased = []
        for h in range(HEADS):
            for g in range(GROUPS):
                first = h * WIN + g * GROUP_ROWS
                start = (WLON - 1 - GROUP * g) * LEVELS
                bias = table_ref[c, h * GROUP_ROWS : (h + 1) * GROUP_ROWS, start : start + WIN]
                biased.append(scores[first : first + GROUP_ROWS] + bias)
        scores = jnp.concatenate(biased, axis=0)
        exponent = jnp.exp(scores - jnp.max(scores, axis=-1, keepdims=True))
        attention = exponent * (1.0 / jnp.sum(exponent, axis=-1, keepdims=True))
        mixtures.append(unstacked(dot(attention, values)))
        grad_attention = dot_right_transposed(grad_stack, values)
        weighted = jnp.sum(attention * grad_attention, axis=-1, keepdims=True)
        grad_scores = attention * (grad_attention - weighted)
        grads_v.append(dot_left_transposed(attention, grad_stack))
        grads_q.append(unstacked(dot(grad_scores, keys)) * SCALE)
        grads_k.append(dot_left_transposed(grad_scores, query_stack))

        table_grad_ref[...] = jnp.zeros_like(table_grad_ref)
        for h in range(HEADS):
            for g in range(GROUPS):
                first = h * WIN + g * GROUP_ROWS
                start = (WLON - 1 - GROUP * g) * LEVELS
                table_grad_ref[h * GROUP_ROWS : (h + 1) * GROUP_ROWS, start : start + WIN] += grad_scores[
                    first : first + GROUP_ROWS
                ]
        for h in range(HEADS):
            total = None
            for g in range(GROUP):
                first = h * GROUP_ROWS + g * LEVELS
                part = table_grad_ref[first : first + LEVELS, g * LEVELS : g * LEVELS + STRIP]
                total = part if total is None else total + part
            first = (c * HEADS + h) * PADDED
            strip_grad_ref[first : first + LEVELS, :STRIP] = total

    grad_projected = jnp.concatenate(
        [jnp.concatenate(grads, axis=0) for grads in (grads_q, grads_k, grads_v)], axis=1
    )
    tokens, window_grad, unit, inverse = (
        jnp.concatenate([whole_window(index, c) for c in range(PW)], axis=0) for index in (2, 3, 0, 1)
    )
    grad_tokens = sum(
        dot_right_transposed(jnp.concatenate(grads, axis=0), parts_ref[part])
        for part, grads in enumerate((grads_q, grads_k, grads_v))
    )
    grad_unit = grad_tokens * gain
    result = window_grad + inverse * (
        grad_unit
        - jnp.mean(grad_unit, axis=-1, keepdims=True)
        - unit * jnp.mean(grad_unit * unit, axis=-1, keepdims=True)
    )
    for ref, offset in ((grad_borrowed_ref, 0), (grad_own_ref, HALF_ROWS)):
        halves = [result[c * WIN + offset : c * WIN + offset + HALF_ROWS] for c in range(PW)]
        for c in range(PW):
            ref[c] = halves[c][:, :128]
        ref[2] = jnp.concatenate([half[:, 128:] for half in halves], axis=1)
    gain_sum = jnp.sum(grad_tokens * unit, axis=0, keepdims=True) * factor
    shift_sum = jnp.sum(grad_tokens, axis=0, keepdims=True) * factor
    norm_ref[...] = jnp.zeros_like(norm_ref)
    norm_ref[:3] = jnp.concatenate(
        [gain_sum[:, :128], shift_sum[:, :128], jnp.concatenate([gain_sum[:, 128:], shift_sum[:, 128:]], axis=1)], axis=0
    )
    grad_qkv = dot_left_transposed(tokens, grad_projected) * factor
    grad_out = dot_left_transposed(jnp.concatenate(mixtures, axis=0), window_grad) * factor
    if not packed:
        weights_ref[:, : 3 * D] = grad_qkv
        weights_ref[:, 3 * D :] = grad_out
        return
    for block in range(4):
        for y in range(2):
            first = block * D + 96 * y
            column = grad_qkv[:, first : first + 96] if block < 3 else grad_out[:, 96 * y : 96 * (y + 1)]
            for lat in range(4):
                chunk = column[48 * lat : 48 * (lat + 1)]
                place = (y, block % 2, block // 2) if lat % 2 == 0 else (block % 2, block // 2, y)
                weights_ref[(lat % 2,) + place + (lat // 2,)] = packed_chunk(chunk)


def bits_of(count):
    return [1 << place for place in range(count.bit_length() - 1)]


def partners(first_bits, second_bits):
    lat_count, lon_count = lax.axis_size("lat"), lax.axis_size("lon")
    pairs = []
    for lat in range(lat_count):
        for lon in range(lon_count):
            lat_bit, lon_bit = first_bits if lat % 2 == 0 else second_bits
            pairs.append((lat * lon_count + lon, (lat ^ lat_bit) * lon_count + (lon ^ lon_bit)))
    return pairs


def side(first_bits, second_bits):
    lat, lon = lax.axis_index("lat"), lax.axis_index("lon")
    first, second = ((lat & lat_bit | lon & lon_bit) != 0 for lat_bit, lon_bit in (first_bits, second_bits))
    return jnp.where(lat & 1 == 0, first, second).astype(jnp.int32)


def exchanged(value, step):
    return lax.ppermute(value, ("lat", "lon"), partners(*step))


def kept_and_given(value, step):
    high = side(*step)
    return (
        lax.dynamic_index_in_dim(value, high, 0, keepdims=False),
        lax.dynamic_index_in_dim(value, 1 - high, 0, keepdims=False),
    )


def exchange_all(values, step):
    flat = [value.reshape(-1, 128) for value in values]
    arrived = exchanged(jnp.concatenate(flat, axis=0), step)
    results, first = [], 0
    for value, rows in zip(values, flat):
        results.append(arrived[first : first + rows.shape[0]].reshape(value.shape))
        first += rows.shape[0]
    return results


def halving_steps(lat_count, lon_count):
    lat_bits, lon_bits = bits_of(lat_count), bits_of(lon_count)
    lon_steps = [((0, first), (0, second)) for first, second in zip(lon_bits, lon_bits[1:] + lon_bits[:1])]
    lat_steps = [((bit, 0), (bit, 0)) for bit in lat_bits]
    return lat_steps[:1], lon_steps, lat_steps[1:]


def chunks_by_step(weights, lat_count, lon_count):
    rows, columns = weights.shape[0] // lat_count, weights.shape[1] // lon_count
    lat_places, lon_places = len(bits_of(lat_count)), len(bits_of(lon_count))
    split = weights.reshape((2,) * lat_places + (rows,) + (2,) * lon_places + (columns,))
    lat_dims = list(range(lat_places))[::-1]
    lon_dims = list(range(lat_places + 1, lat_places + 1 + lon_places))[::-1]
    halves = []
    for core, dims in enumerate((lon_dims, lon_dims[1:] + lon_dims[:1])):
        order = lat_dims[:1] + dims + lat_dims[1:] + [lat_places, lat_places + 1 + lon_places]
        halves.append(split.transpose(order)[core])
    places = lat_places + lon_places
    split = jnp.stack(halves).reshape((2,) * places + (rows * columns,))
    words = -(-rows * columns // 1024) * 1024
    split = jnp.pad(split, [(0, 0)] * places + [(0, words - rows * columns)])
    return split.reshape((2,) * places + (words // 128, 128))


def shards(features, cotangent, norm_gain, norm_shift, qkv_weight, out_weight, bias_table):
    lat_count, lon_count = lax.axis_size("lat"), lax.axis_size("lon")
    token_count = ZP * features.shape[1] * features.shape[2] * lat_count * lon_count
    factor = 1.0 / math.sqrt(token_count)
    packed = (lat_count, lon_count) == (4, 8)
    f32 = jnp.float32
    shape = jax.ShapeDtypeStruct
    params = pltpu.CompilerParams(vmem_limit_bytes=48 << 20)
    half_shape = shape((3, PW, HALF_ROWS, 128), f32)
    block_shape = (WLAT, WLON, ZP, D)
    sent, own = pl.pallas_call(
        pack_kernel,
        out_shape=(pltpu.VMEM(half_shape.shape, f32),) * 2,
        in_specs=[pl.BlockSpec(memory_space=pltpu.HBM)] * 2,
        out_specs=tuple(whole(2)),
        scratch_shapes=[pltpu.VMEM(block_shape, f32), pltpu.VMEM(block_shape, f32), pltpu.SemaphoreType.DMA((2,))],
        compiler_params=params,
    )(*hbm(features.transpose(1, 2, 0, 3), cotangent.transpose(1, 2, 0, 3)))
    borrowed = lax.ppermute(sent, "lon", [(s, (s + 1) % lon_count) for s in range(lon_count)])
    projected_shape = (8, WIN, D)
    in_hbm = pl.BlockSpec(memory_space=pltpu.HBM)
    bias, gain_row, shift_row, qkv_rows, out_rows = hbm(
        bias_table[0].transpose(1, 2, 0, 3), norm_gain[None], norm_shift[None], qkv_weight, out_weight
    )
    table, projected, affine, parts = pl.pallas_call(
        prepare_kernel,
        out_shape=(
            pltpu.VMEM((PW, GROUP_ROWS * HEADS, 384), f32),
            pltpu.VMEM(projected_shape, f32),
            pltpu.VMEM((2, D), f32),
            pltpu.VMEM((4, D, D), f32),
        ),
        in_specs=[in_hbm] + whole(1) + [in_hbm] * 4,
        out_specs=tuple(whole(4)),
        scratch_shapes=[
            pltpu.VMEM((LEVELS * PADDED, PW * HEADS * LONREL), f32),
            pltpu.VMEM((PW * HEADS * PADDED, LEVELS * OFFSETS), f32),
            pltpu.VMEM((HEADS, LONREL, PW, PAIRS), f32),
            pltpu.VMEM((D, 3 * D), f32),
            pltpu.SemaphoreType.DMA((5,)),
        ],
        compiler_params=params,
    )(bias, own, gain_row, shift_row, qkv_rows, out_rows)
    grad_half = shape((3, HALF_ROWS, 128), f32)
    grad_own, grad_borrowed, weights, strips, norm = pl.pallas_call(
        functools.partial(block_kernel, factor, packed),
        out_shape=(
            grad_half,
            grad_half,
            shape((2, 2, 2, 2, 2, 40, 128) if packed else (D, 4 * D), f32),
            shape((PW * HEADS * PADDED, LEVELS * OFFSETS), f32),
            shape((8, 128), f32),
        ),
        in_specs=whole(5),
        out_specs=tuple(whole(5)),
        scratch_shapes=[pltpu.VMEM((BLOCK, 384), f32), pltpu.VMEM(projected_shape, f32)],
        compiler_params=params,
    )(borrowed, projected, affine, parts, table)
    if not packed:
        weights = chunks_by_step(weights, lat_count, lon_count)
    rows_shape = shape((2, HEADS * OFFSETS, 128), f32)
    strip_grad = pl.pallas_call(
        turn_kernel,
        out_shape=rows_shape,
        in_specs=whole(1),
        out_specs=whole(1)[0],
        scratch_shapes=[pltpu.VMEM((LEVELS * PADDED, PW * HEADS * OFFSETS), f32)],
        compiler_params=params,
    )(strips)
    first_steps, lon_steps, last_steps = halving_steps(lat_count, lon_count)
    norm = jnp.where(lax.axis_index("lon") % 2 == 0, norm, jnp.roll(norm, 4, 0))
    returned = other_strip = None
    for step in first_steps + lon_steps + last_steps:
        kept, given = kept_and_given(weights, step)
        if step in lon_steps:
            given_strip = strip_grad
            if step == lon_steps[0]:
                strip_grad, given_strip = kept_and_given(strip_grad, step)
                given, grad_borrowed = lax.optimization_barrier((given, grad_borrowed))
                returned = lax.ppermute(grad_borrowed, "lon", [(s, (s - 1) % lon_count) for s in range(lon_count)])
            more, more_strip, more_norm = exchange_all([given, given_strip, norm], step)
            strip_grad = strip_grad + more_strip
        else:
            if step == last_steps[0]:
                other_strip = exchanged(strip_grad, lon_steps[0])
            more, more_norm = exchange_all([given, norm], step)
            if step == last_steps[-1]:
                more, returned = lax.optimization_barrier((more, returned))
        weights, norm = kept + more, norm + more_norm
    grad_features = pl.pallas_call(
        unpack_kernel,
        out_shape=shape(block_shape, f32),
        in_specs=whole(2),
        out_specs=whole(1)[0],
        compiler_params=params,
    )(grad_own, returned).transpose(2, 0, 1, 3)
    chunk = weights if packed else jnp.zeros((40, 128), f32)
    parity = side(*lon_steps[0])[None]
    grad_bias, grad_weights, grad_norm = pl.pallas_call(
        finish_kernel,
        out_shape=(shape((HEADS, LONREL, PW, PAIRS), f32), shape((48, 96), f32), shape((2, D), f32)),
        in_specs=[pl.BlockSpec(memory_space=pltpu.SMEM)] + whole(4),
        out_specs=tuple(whole(3)),
        compiler_params=params,
    )(parity, strip_grad, other_strip, chunk, norm)
    grad_bias = grad_bias.transpose(2, 0, 1, 3)[None]
    if not packed:
        rows, columns = D // lat_count, 4 * D // lon_count
        grad_weights = weights.reshape(-1)[: rows * columns].reshape(rows, columns)
    return (grad_features, grad_weights, grad_bias, grad_norm)


def solution(mesh):
    placed = (
        P(None, "lat", "lon", None),
        P(None, "lat", "lon", None),
        P(),
        P(),
        P(),
        P(),
        P("lat", None, None, None, None),
    )
    return jax.shard_map(
        shards,
        mesh=mesh,
        in_specs=placed,
        out_specs=(
            P(None, "lat", "lon", None),
            P("lat", "lon"),
            P("lat", None, None, None, None),
            P(),
        ),
        check_vma=False,
    )
```

time: 58.2 us -> 51.6 us (0.89)
  waiting for transfers between devices: 28.8 us -> 26.2 us
  local copies, waits for them, and re-layouts: 2.75 us -> 0.15 us
  starting transfers between devices: 7.95 us -> 6.66 us
    pallas_call x3 -> x4, Pallas kernels: 3.41 us -> 6.82 us  [the longest x1 3.31 us: shards(): pl.pallas_call(prepare_kernel, out_shape=(pltpu.VMEM((PW, GROUP_ROWS * HE...]
    ppermute x1, waiting for transfers between devices: 2.73 us -> 0.01 us  [shards(): lax.ppermute(grad_borrowed, 'lon', [(s, (s - 1) % lon_count) for s in ran...]
    pallas_call x1, Pallas kernels: 3.49 us -> 0.88 us  [shards(): pl.pallas_call(finish_kernel, out_shape=(shape((HEADS, LONREL, PW, PAIRS)...]
    unnamed x14 -> x0, local copies, waits for them, and re-layouts: 2.6 us -> none
    ppermute x6, waiting for transfers between devices: 19.8 us -> 21 us  [exchanged(): return lax.ppermute(value, ('lat', 'lon'), partners(*step))]
    ppermute x1, waiting for transfers between devices: 6.25 us -> 5.15 us  [shards(): lax.ppermute(sent, 'lon', [(s, (s + 1) % lon_count) for s in range(lon_co...]
    ppermute x6, starting transfers between devices: 2.92 us -> 1.91 us  [exchanged(): return lax.ppermute(value, ('lat', 'lon'), partners(*step))]
    pallas_call x1, Pallas kernels: 10.4 us -> 9.6 us  [shards(): pl.pallas_call(functools.partial(block_kernel, factor, packed), out_shape...]
  transfers between devices with their start and end apart: 8 -> 8, of which waited for: 8 -> 7; matrix products, arithmetic and copies ran while one was open for 0% -> 0% of each run, Pallas kernels for 5% -> 11%
where the time goes in v3:
time: 51.6 us; the launch traced here: 51.5 us
  waiting for transfers between devices  26.2 us (51%)
  Pallas kernels  17.3 us (34%)
  starting transfers between devices  6.66 us (13%)
  between operations  0.92 us (2%)
    ppermute x6, waiting for transfers between devices, exchanged(): return lax.ppermute(value, ('lat', 'lon'), partners(*step))  21 us
    pallas_call x1, Pallas kernels, shards(): pl.pallas_call(functools.partial(block_kernel, factor, packed), out_shape...  9.6 us
    ppermute x1, waiting for transfers between devices, shards(): lax.ppermute(sent, 'lon', [(s, (s + 1) % lon_count) for s in range(lon_co...  5.15 us
    pallas_call x1, Pallas kernels, shards(): pl.pallas_call(prepare_kernel, out_shape=(pltpu.VMEM((PW, GROUP_ROWS * HE...  3.31 us
    ppermute x1, starting transfers between devices, shards(): lax.ppermute(sent, 'lon', [(s, (s + 1) % lon_count) for s in range(lon_co...  3.02 us
    ppermute x6, starting transfers between devices, exchanged(): return lax.ppermute(value, ('lat', 'lon'), partners(*step))  1.91 us
    ppermute x1, starting transfers between devices, shards(): lax.ppermute(grad_borrowed, 'lon', [(s, (s - 1) % lon_count) for s in ran...  1.73 us
    pallas_call x1, Pallas kernels, shards(): pl.pallas_call(pack_kernel, out_shape=(pltpu.VMEM(half_shape.shape, f32),...  1.3 us
  transfers between devices with their start and end apart: 8, of which 7 were waited for; matrix products, arithmetic and copies ran while one was open for 0% of the time, Pallas kernels for 11%

profile of v3, /device:TPU:0, one launch (start us, length us, event | category | flops | bytes accessed | tf_op | source)
XLA Modules:
  0.0 51.5 jit_solution(6668607700577696032)
XLA Ops:
  0.6 1.3 %shard_map.102 = (f32[3,2,72,128]{3,2,1,0:T(8,128)S(1)}, f32[3,2,72,128]{3,2,1,0:T(8,128)S(1)}) custom-call(f32[6,12,4,192]{3,2,1,0:T(4,128)} %bitcast.44, f32[6,12,4,192]{3,2,1,0:T(4,128)} %bitcast.45), custom_call_target="tpu_custom_call" | custom-call | tf_op jit(solution)/shard_map/pallas_call | solution.py:440
  1.9 3.0 %collective-permute-start = (f32[3,2,72,128]{3,2,1,0:T(8,128)S(1)}, f32[3,2,72,128]{3,2,1,0:T(8,128)S(1)}, u32[]{:S(2)}, u32[]{:S(2)}) collective-permute-start(f32[3,2,72,128]{3,2,1,0:T(8,128)S(1)} %get-tuple-element.22), channel_id=1, source_target_pairs={{0,1},{1,2},{2,3},{3,4},{4,5},{5,6},{6,7},{7,0},{8,9},{9,10},{10,1... | collective-permute-start | bytes 663560 | tf_op jit(solution)/shard_map/ppermute | solution.py:448
  5.0 3.3 %shard_map.103 = (f32[2,288,384]{2,1,0:T(8,128)S(1)}, f32[8,144,192]{2,1,0:T(8,128)S(1)}, f32[2,192]{1,0:T(2,128)S(1)}, f32[4,192,192]{2,1,0:T(8,128)S(1)}) custom-call(f32[6,23,2,144]{3,2,1,0:T(2,128)} %bitcast.47, f32[3,2,72,128]{3,2,1,0:T(8,128)S(1)} %get-tuple-element.23.own_ref, f32[1,192]{1,0:T(1,128)} %bitcast.50, f32[1,192]{1,0:T(1,128)} %bitcast.51, ...), custom_call_target="tpu_custom_call" | custom-call | tf_op jit(solution)/shard_map/pallas_call | solution.py:454
  8.3 5.2 %collective-permute-done.borrowed_ref = f32[3,2,72,128]{3,2,1,0:T(8,128)S(1)} collective-permute-done((f32[3,2,72,128]{3,2,1,0:T(8,128)S(1)}, f32[3,2,72,128]{3,2,1,0:T(8,128)S(1)}, u32[]{:S(2)}, u32[]{:S(2)}) %collective-permute-start) | collective-permute-done | bytes 221216 | tf_op jit(solution)/shard_map/ppermute | solution.py:448
  13.4 9.6 %shard_map.104 = (f32[3,72,128]{2,1,0:T(8,128)S(1)}, f32[3,72,128]{2,1,0:T(8,128)S(1)}, f32[2,2,2,2,2,40,128]{6,5,4,3,2,1,0:T(8,128)S(1)}, f32[192,288]{1,0:T(8,128)S(1)}, f32[8,128]{1,0:T(8,128)S(1)}) custom-call(f32[3,2,72,128]{3,2,1,0:T(8,128)S(1)} %collective-permute-done.borrowed_ref, f32[8,144,192]{2,1,0:T(8,128)S(1)} %get-tuple-element.24.projected_ref, ...), custom_call_target="tpu_custom_call" | custom-call | tf_op jit(solution)/shard_map/pallas_call | solution.py:474
  23.1 0.1 collective-permute-start.1
  23.2 1.2 %shard_map.105 = f32[2,144,128]{2,1,0:T(8,128)S(1)} custom-call(f32[192,288]{1,0:T(8,128)S(1)} %get-tuple-element.33.strip_ref), custom_call_target="tpu_custom_call" | custom-call | tf_op jit(solution)/shard_map/pallas_call | solution.py:491
  24.4 0.4 collective-permute-done.1
  24.8 0.1 bitcast_add_fusion
  25.0 0.1 collective-permute-start.2
  25.1 6.1 %collective-permute-done.2 = f32[472,128]{1,0:T(8,128)S(1)} collective-permute-done((f32[472,128]{1,0:T(8,128)S(1)}, f32[472,128]{1,0:T(8,128)S(1)}, u32[]{:S(2)}, u32[]{:S(2)}) %collective-permute-start.2) | collective-permute-done | bytes 241696 | tf_op jit(solution)/shard_map/ppermute | solution.py:385
  31.3 0.1 collective-permute-start.3
  31.4 6.9 %collective-permute-done.3 = f32[312,128]{1,0:T(8,128)S(1)} collective-permute-done((f32[312,128]{1,0:T(8,128)S(1)}, f32[312,128]{1,0:T(8,128)S(1)}, u32[]{:S(2)}, u32[]{:S(2)}) %collective-permute-start.3) | collective-permute-done | bytes 159776 | tf_op jit(solution)/shard_map/ppermute | solution.py:385
  38.4 0.1 collective-permute-start.4
  38.5 1.7 %collective-permute-start.6 = (f32[3,72,128]{2,1,0:T(8,128)S(1)}, f32[3,72,128]{2,1,0:T(8,128)S(1)}, u32[]{:S(2)}, u32[]{:S(2)}) collective-permute-start(f32[3,72,128]{2,1,0:T(8,128)S(1)} %get-tuple-element.34), channel_id=1, source_target_pairs={{0,7},{1,0},{2,1},{3,2},{4,3},{5,4},{6,5},{7,6},{8,15},{9,8},{10,9... | collective-permute-start | bytes 331784 | tf_op jit(solution)/shard_map/ppermute | solution.py:509
  40.2 4.3 %collective-permute-done.4 = f32[232,128]{1,0:T(8,128)S(1)} collective-permute-done((f32[232,128]{1,0:T(8,128)S(1)}, f32[232,128]{1,0:T(8,128)S(1)}, u32[]{:S(2)}, u32[]{:S(2)}) %collective-permute-start.4) | collective-permute-done | bytes 118816 | tf_op jit(solution)/shard_map/ppermute | solution.py:385
  44.6 1.6 %collective-permute-start.5 = (f32[48,128]{1,0:T(8,128)S(1)}, f32[48,128]{1,0:T(8,128)S(1)}, u32[]{:S(2)}, u32[]{:S(2)}) collective-permute-start(f32[48,128]{1,0:T(8,128)S(1)} %pad_maximum_fusion.4), channel_id=1, source_target_pairs={{0,16},{1,17},{2,18},{3,19},{4,20},{5,21},{6,22},{7,23},{8,24},{9,... | collective-permute-start | bytes 73736 | tf_op jit(solution)/shard_map/ppermute | solution.py:385
  46.2 0.1 collective-permute-start.7
  46.2 2.2 %collective-permute-done.5 = f32[48,128]{1,0:T(8,128)S(1)} collective-permute-done((f32[48,128]{1,0:T(8,128)S(1)}, f32[48,128]{1,0:T(8,128)S(1)}, u32[]{:S(2)}, u32[]{:S(2)}) %collective-permute-start.5) | collective-permute-done | bytes 24608 | tf_op jit(solution)/shard_map/ppermute | solution.py:385
  48.5 0.0 collective-permute-done.6.returned_ref
  48.5 1.0 %shard_map.106 = f32[6,12,4,192]{3,2,1,0:T(4,128)} custom-call(f32[3,72,128]{2,1,0:T(8,128)S(1)} %get-tuple-element.28.own_ref, f32[3,72,128]{2,1,0:T(8,128)S(1)} %collective-permute-done.6.returned_ref), custom_call_target="tpu_custom_call" | custom-call | tf_op jit(solution)/shard_map/pallas_call | solution.py:519
  49.5 1.1 %collective-permute-done.7.other_ref = f32[144,128]{1,0:T(8,128)S(1)} collective-permute-done((f32[144,128]{1,0:T(8,128)S(1)}, f32[144,128]{1,0:T(8,128)S(1)}, u32[]{:S(2)}, u32[]{:S(2)}) %collective-permute-start.7) | collective-permute-done | bytes 73760 | tf_op jit(solution)/shard_map/ppermute | solution.py:385
  50.6 0.9 %shard_map.107 = (f32[6,23,2,144]{3,2,1,0:T(2,128)}, f32[48,96]{1,0:T(8,128)}, f32[2,192]{1,0:T(2,128)}) custom-call(s32[1]{0:T(128)} %bitcast.23.parity_ref, f32[144,128]{1,0:T(8,128)S(1)} %slice_add_fusion.mine_ref, f32[144,128]{1,0:T(8,128)S(1)} %collective-permute-done.7.other_ref, f32[40,128]{1,0:T(8,128)S(1)} %bitcast_add_fusion.4.weights_ref, ...), custom_call_target="tpu_custom_call" | custom-call | tf_op jit(solution)/shard_map/pallas_call | solution.py:528
  (30 shorter events, 0.3 us)
Async XLA Ops:
  1.9 11.5 %collective-permute-start = (f32[3,2,72,128]{3,2,1,0:T(8,128)S(1)}, f32[3,2,72,128]{3,2,1,0:T(8,128)S(1)}, u32[]{:S(2)}, u32[]{:S(2)}) collective-permute-start(f32[3,2,72,128]{3,2,1,0:T(8,128)S(1)} %get-tuple-element.22), channel_id=1, source_target_pairs={{0,1},{1,2},{2,3},{3,4},{4,5},{5,6},{6,7},{7,0},{8,9},{9,10},{10,1... | collective-permute-start | bytes 663560 | tf_op jit(solution)/shard_map/ppermute | solution.py:448
  23.1 1.7 %collective-permute-start.1 = (f32[648,128]{1,0:T(8,128)S(1)}, f32[648,128]{1,0:T(8,128)S(1)}, u32[]{:S(2)}, u32[]{:S(2)}) collective-permute-start(f32[648,128]{1,0:T(8,128)S(1)} %pad_maximum_fusion), channel_id=1, source_target_pairs={{0,8},{1,9},{2,10},{3,11},{4,12},{5,13},{6,14},{7,15},{8,0},{9,1},... | collective-permute-start | bytes 995336 | tf_op jit(solution)/shard_map/ppermute | solution.py:385
  25.0 6.2 %collective-permute-start.2 = (f32[472,128]{1,0:T(8,128)S(1)}, f32[472,128]{1,0:T(8,128)S(1)}, u32[]{:S(2)}, u32[]{:S(2)}) collective-permute-start(f32[472,128]{1,0:T(8,128)S(1)} %pad_maximum_fusion.1), channel_id=1, source_target_pairs={{0,1},{1,0},{2,3},{3,2},{4,5},{5,4},{6,7},{7,6},{8,10},{9,11},{10,... | collective-permute-start | bytes 725000 | tf_op jit(solution)/shard_map/ppermute | solution.py:385
  31.3 7.0 %collective-permute-start.3 = (f32[312,128]{1,0:T(8,128)S(1)}, f32[312,128]{1,0:T(8,128)S(1)}, u32[]{:S(2)}, u32[]{:S(2)}) collective-permute-start(f32[312,128]{1,0:T(8,128)S(1)} %pad_maximum_fusion.2), channel_id=1, source_target_pairs={{0,2},{1,3},{2,0},{3,1},{4,6},{5,7},{6,4},{7,5},{8,12},{9,13},{10,... | collective-permute-start | bytes 479240 | tf_op jit(solution)/shard_map/ppermute | solution.py:385
  38.4 6.2 %collective-permute-start.4 = (f32[232,128]{1,0:T(8,128)S(1)}, f32[232,128]{1,0:T(8,128)S(1)}, u32[]{:S(2)}, u32[]{:S(2)}) collective-permute-start(f32[232,128]{1,0:T(8,128)S(1)} %pad_maximum_fusion.3), channel_id=1, source_target_pairs={{0,4},{1,5},{2,6},{3,7},{4,0},{5,1},{6,2},{7,3},{8,9},{9,8},{10,11... | collective-permute-start | bytes 356360 | tf_op jit(solution)/shard_map/ppermute | solution.py:385
  38.5 10.0 %collective-permute-start.6 = (f32[3,72,128]{2,1,0:T(8,128)S(1)}, f32[3,72,128]{2,1,0:T(8,128)S(1)}, u32[]{:S(2)}, u32[]{:S(2)}) collective-permute-start(f32[3,72,128]{2,1,0:T(8,128)S(1)} %get-tuple-element.34), channel_id=1, source_target_pairs={{0,7},{1,0},{2,1},{3,2},{4,3},{5,4},{6,5},{7,6},{8,15},{9,8},{10,9... | collective-permute-start | bytes 331784 | tf_op jit(solution)/shard_map/ppermute | solution.py:509
  44.6 3.9 %collective-permute-start.5 = (f32[48,128]{1,0:T(8,128)S(1)}, f32[48,128]{1,0:T(8,128)S(1)}, u32[]{:S(2)}, u32[]{:S(2)}) collective-permute-start(f32[48,128]{1,0:T(8,128)S(1)} %pad_maximum_fusion.4), channel_id=1, source_target_pairs={{0,16},{1,17},{2,18},{3,19},{4,20},{5,21},{6,22},{7,23},{8,24},{9,... | collective-permute-start | bytes 73736 | tf_op jit(solution)/shard_map/ppermute | solution.py:385
  46.2 4.4 %collective-permute-start.7 = (f32[144,128]{1,0:T(8,128)S(1)}, f32[144,128]{1,0:T(8,128)S(1)}, u32[]{:S(2)}, u32[]{:S(2)}) collective-permute-start(f32[144,128]{1,0:T(8,128)S(1)} %slice_add_fusion.mine_ref), channel_id=1, source_target_pairs={{0,1},{1,0},{2,3},{3,2},{4,5},{5,4},{6,7},{7,6},{8,10},{9,11},{10,... | collective-permute-start | bytes 221192 | tf_op jit(solution)/shard_map/ppermute | solution.py:385

commit v4 on v3

--- a/solution.py
+++ b/solution.py
@@ -251,6 +251,39 @@
     return jnp.concatenate([packed[:, :96], last], axis=0)
 
 
+HEADS_AT_ONCE = 6
+DEPTH = 1
+
+
+def halves_of(value):
+    high = value.astype(jnp.bfloat16)
+    return high, (value - high.astype(jnp.float32)).astype(jnp.bfloat16)
+
+
+def product(left, right, dims):
+    dims = (dims, ((), ()))
+
+    def one(a, b):
+        return lax.dot_general(a, b, dims, preferred_element_type=jnp.float32)
+
+    return one(left[0], right[0]) + one(left[0], right[1]) + one(left[1], right[0])
+
+
+def full_product(left, right, dims):
+    dims = (dims, ((), ()))
+
+    def one(a, b):
+        return lax.dot_general(a, b, dims, preferred_element_type=jnp.float32)
+
+    low = one(left[0], right[2]) + one(left[2], right[0]) + one(left[1], right[1])
+    return low + one(left[0], right[1]) + one(left[1], right[0]) + one(left[0], right[0])
+
+
+NORMAL = ((1,), (0,))
+RIGHT = ((1,), (1,))
+LEFT = ((0,), (0,))
+
+
 def block_kernel(
     factor, packed,
     borrowed_ref, projected_ref, affine_ref, parts_ref, table_ref,
@@ -265,69 +298,94 @@
         return jnp.concatenate([arrived_ref[index, rows], projected_ref[index, rows]], axis=0)
 
     head_of_lane = lax.broadcasted_iota(jnp.int32, (WIN, D), 1) // HEAD
-
-    def stacked(value):
-        return jnp.concatenate([jnp.where(head_of_lane == h, value, 0.0) for h in range(HEADS)], axis=0)
-
-    def unstacked(value):
-        total = None
-        for h in range(HEADS):
-            part = jnp.where(head_of_lane == h, value[h * WIN : (h + 1) * WIN], 0.0)
-            total = part if total is None else total + part
-        return total
-
     strip_grad_ref[...] = jnp.zeros_like(strip_grad_ref)
-    mixtures, grads_q, grads_k, grads_v = [], [], [], []
+    table_grad_ref[...] = jnp.zeros_like(table_grad_ref)
+    windows = []
     for c in range(PW):
-        keys, values = whole_window(5, c), whole_window(6, c)
-        query_stack = stacked(whole_window(4, c))
-        grad_stack = stacked(whole_window(7, c))
-        scores = dot_right_transposed(query_stack, keys, FULL)
+        windows.append(
+            dict(
+                queries=whole_window(4, c),
+                grad=whole_window(7, c),
+                keys=parts_of(whole_window(5, c), 3),
+                values=halves_of(whole_window(6, c)),
+                mixture=None, grad_q=None, grad_k=None, grad_v=None,
+            )
+        )
+
+    def add(window, name, value):
+        window[name] = value if window[name] is None else window[name] + value
+
+    def masked(value, heads):
+        return jnp.concatenate([jnp.where(head_of_lane == h, value, 0.0) for h in heads], axis=0)
+
+    def joined(value, heads):
+        return sum(jnp.where(head_of_lane == h, value[n * WIN : (n + 1) * WIN], 0.0) for n, h in enumerate(heads))
+
+    def first_stage(c, heads):
+        window = windows[c]
+        stack = parts_of(masked(window["queries"], heads), 3)
+        scores = full_product(stack, window["keys"], RIGHT)
         biased = []
-        for h in range(HEADS):
+        for n, h in enumerate(heads):
             for g in range(GROUPS):
-                first = h * WIN + g * GROUP_ROWS
+                first = n * WIN + g * GROUP_ROWS
                 start = (WLON - 1 - GROUP * g) * LEVELS
                 bias = table_ref[c, h * GROUP_ROWS : (h + 1) * GROUP_ROWS, start : start + WIN]
                 biased.append(scores[first : first + GROUP_ROWS] + bias)
         scores = jnp.concatenate(biased, axis=0)
         exponent = jnp.exp(scores - jnp.max(scores, axis=-1, keepdims=True))
         attention = exponent * (1.0 / jnp.sum(exponent, axis=-1, keepdims=True))
-        mixtures.append(unstacked(dot(attention, values)))
-        grad_attention = dot_right_transposed(grad_stack, values)
+        return stack[:2], attention
+
+    def second_stage(c, heads, stack, attention):
+        window = windows[c]
+        halves = halves_of(attention)
+        add(window, "mixture", joined(product(halves, window["values"], NORMAL), heads))
+        grad_stack = halves_of(masked(window["grad"], heads))
+        grad_attention = product(grad_stack, window["values"], RIGHT)
         weighted = jnp.sum(attention * grad_attention, axis=-1, keepdims=True)
         grad_scores = attention * (grad_attention - weighted)
-        grads_v.append(dot_left_transposed(attention, grad_stack))
-        grads_q.append(unstacked(dot(grad_scores, keys)) * SCALE)
-        grads_k.append(dot_left_transposed(grad_scores, query_stack))
-
-        table_grad_ref[...] = jnp.zeros_like(table_grad_ref)
-        for h in range(HEADS):
+        add(window, "grad_v", product(halves, grad_stack, LEFT))
+        return stack, grad_scores
+
+    def third_stage(c, heads, stack, grad_scores):
+        window = windows[c]
+        halves = halves_of(grad_scores)
+        add(window, "grad_q", joined(product(halves, window["keys"][:2], NORMAL), heads))
+        add(window, "grad_k", product(halves, stack, LEFT))
+        for n, h in enumerate(heads):
+            table_rows = slice((c * HEADS + h) * GROUP_ROWS, (c * HEADS + h + 1) * GROUP_ROWS)
             for g in range(GROUPS):
-                first = h * WIN + g * GROUP_ROWS
+                first = n * WIN + g * GROUP_ROWS
                 start = (WLON - 1 - GROUP * g) * LEVELS
-                table_grad_ref[h * GROUP_ROWS : (h + 1) * GROUP_ROWS, start : start + WIN] += grad_scores[
-                    first : first + GROUP_ROWS
-                ]
-        for h in range(HEADS):
+                table_grad_ref[table_rows, start : start + WIN] += grad_scores[first : first + GROUP_ROWS]
             total = None
             for g in range(GROUP):
-                first = h * GROUP_ROWS + g * LEVELS
+                first = (c * HEADS + h) * GROUP_ROWS + g * LEVELS
                 part = table_grad_ref[first : first + LEVELS, g * LEVELS : g * LEVELS + STRIP]
                 total = part if total is None else total + part
             first = (c * HEADS + h) * PADDED
             strip_grad_ref[first : first + LEVELS, :STRIP] = total
 
-    grad_projected = jnp.concatenate(
-        [jnp.concatenate(grads, axis=0) for grads in (grads_q, grads_k, grads_v)], axis=1
-    )
+    chunks = [
+        (c, tuple(range(h, h + HEADS_AT_ONCE))) for h in range(0, HEADS, HEADS_AT_ONCE) for c in range(PW)
+    ]
+    stages = (first_stage, second_stage, third_stage)
+    state = {}
+    for tick in range(len(chunks) + DEPTH * (len(stages) - 1)):
+        for place in reversed(range(len(stages))):
+            index = tick - DEPTH * place
+            if 0 <= index < len(chunks):
+                state[index] = stages[place](*chunks[index], *(state[index] if place else ()))
+
+    def rows_of(name):
+        return jnp.concatenate([window[name] for window in windows], axis=0)
+
+    grads = [halves_of(value) for value in (rows_of("grad_q") * SCALE, rows_of("grad_k"), rows_of("grad_v"))]
     tokens, window_grad, unit, inverse = (
         jnp.concatenate([whole_window(index, c) for c in range(PW)], axis=0) for index in (2, 3, 0, 1)
     )
-    grad_tokens = sum(
-        dot_right_transposed(jnp.concatenate(grads, axis=0), parts_ref[part])
-        for part, grads in enumerate((grads_q, grads_k, grads_v))
-    )
+    grad_tokens = sum(product(grads[part], halves_of(parts_ref[part]), RIGHT) for part in range(3))
     grad_unit = grad_tokens * gain
     result = window_grad + inverse * (
         grad_unit
@@ -345,20 +403,18 @@
     norm_ref[:3] = jnp.concatenate(
         [gain_sum[:, :128], shift_sum[:, :128], jnp.concatenate([gain_sum[:, 128:], shift_sum[:, 128:]], axis=1)], axis=0
     )
-    grad_qkv = dot_left_transposed(tokens, grad_projected) * factor
-    grad_out = dot_left_transposed(jnp.concatenate(mixtures, axis=0), window_grad) * factor
-    if not packed:
-        weights_ref[:, : 3 * D] = grad_qkv
-        weights_ref[:, 3 * D :] = grad_out
-        return
-    for block in range(4):
+    token_halves = halves_of(tokens * factor)
+    sums = [product(token_halves, grad, LEFT) for grad in grads]
+    sums.append(product(halves_of(rows_of("mixture") * factor), halves_of(window_grad), LEFT))
+    for block, total in enumerate(sums):
+        if not packed:
+            weights_ref[:, block * D : (block + 1) * D] = total
+            continue
         for y in range(2):
-            first = block * D + 96 * y
-            column = grad_qkv[:, first : first + 96] if block < 3 else grad_out[:, 96 * y : 96 * (y + 1)]
             for lat in range(4):
-                chunk = column[48 * lat : 48 * (lat + 1)]
-                place = (y, block % 2, block // 2) if lat % 2 == 0 else (block % 2, block // 2, y)
-                weights_ref[(lat % 2,) + place + (lat // 2,)] = packed_chunk(chunk)
+                chunk = total[48 * lat : 48 * (lat + 1), 96 * y : 96 * (y + 1)]
+                place = (block % 2, block // 2, y) if lat % 2 == 0 else (block // 2, y, block % 2)
+                weights_ref[(lat % 2, lat // 2) + place] = packed_chunk(chunk)
 
 
 def bits_of(count):
@@ -403,11 +459,15 @@
     return results
 
 
-def halving_steps(lat_count, lon_count):
+def turned_by(items, count):
+    return items[count:] + items[:count]
+
+
+def summing_steps(lat_count, lon_count):
     lat_bits, lon_bits = bits_of(lat_count), bits_of(lon_count)
-    lon_steps = [((0, first), (0, second)) for first, second in zip(lon_bits, lon_bits[1:] + lon_bits[:1])]
     lat_steps = [((bit, 0), (bit, 0)) for bit in lat_bits]
-    return lat_steps[:1], lon_steps, lat_steps[1:]
+    lon_steps = [((0, first), (0, second)) for first, second in zip(turned_by(lon_bits, 1), turned_by(lon_bits, 2))]
+    return lat_steps, lon_steps, lon_steps[-1]
 
 
 def chunks_by_step(weights, lat_count, lon_count):
@@ -417,8 +477,8 @@
     lat_dims = list(range(lat_places))[::-1]
     lon_dims = list(range(lat_places + 1, lat_places + 1 + lon_places))[::-1]
     halves = []
-    for core, dims in enumerate((lon_dims, lon_dims[1:] + lon_dims[:1])):
-        order = lat_dims[:1] + dims + lat_dims[1:] + [lat_places, lat_places + 1 + lon_places]
+    for core, dims in enumerate((turned_by(lon_dims, 1), turned_by(lon_dims, 2))):
+        order = lat_dims + dims + [lat_places, lat_places + 1 + lon_places]
         halves.append(split.transpose(order)[core])
     places = lat_places + lon_places
     split = jnp.stack(halves).reshape((2,) * places + (rows * columns,))
@@ -482,7 +542,7 @@
         ),
         in_specs=whole(5),
         out_specs=tuple(whole(5)),
-        scratch_shapes=[pltpu.VMEM((BLOCK, 384), f32), pltpu.VMEM(projected_shape, f32)],
+        scratch_shapes=[pltpu.VMEM((PW * BLOCK, 384), f32), pltpu.VMEM(projected_shape, f32)],
         compiler_params=params,
     )(borrowed, projected, affine, parts, table)
     if not packed:
@@ -496,25 +556,25 @@
         scratch_shapes=[pltpu.VMEM((LEVELS * PADDED, PW * HEADS * OFFSETS), f32)],
         compiler_params=params,
     )(strips)
-    first_steps, lon_steps, last_steps = halving_steps(lat_count, lon_count)
-    norm = jnp.where(lax.axis_index("lon") % 2 == 0, norm, jnp.roll(norm, 4, 0))
-    returned = other_strip = None
-    for step in first_steps + lon_steps + last_steps:
+    lat_steps, lon_steps, strip_step = summing_steps(lat_count, lon_count)
+    apart = lon_steps[0][0][1]
+    norm = jnp.where(lax.axis_index("lon") & apart == 0, norm, jnp.roll(norm, 4, 0))
+    strip_grad, given_strip = kept_and_given(strip_grad, strip_step)
+    strip_grad = strip_grad + exchanged(given_strip, strip_step)
+    other_strip = None
+    for step in lat_steps + lon_steps:
         kept, given = kept_and_given(weights, step)
-        if step in lon_steps:
-            given_strip = strip_grad
+        if step in lat_steps:
+            more, more_norm = exchange_all([given, norm], step)
+        else:
             if step == lon_steps[0]:
-                strip_grad, given_strip = kept_and_given(strip_grad, step)
                 given, grad_borrowed = lax.optimization_barrier((given, grad_borrowed))
                 returned = lax.ppermute(grad_borrowed, "lon", [(s, (s - 1) % lon_count) for s in range(lon_count)])
-            more, more_strip, more_norm = exchange_all([given, given_strip, norm], step)
-            strip_grad = strip_grad + more_strip
-        else:
-            if step == last_steps[0]:
-                other_strip = exchanged(strip_grad, lon_steps[0])
-            more, more_norm = exchange_all([given, norm], step)
-            if step == last_steps[-1]:
-                more, returned = lax.optimization_barrier((more, returned))
+            more, more_strip, more_norm = exchange_all([given, strip_grad, norm], step)
+            if step == lon_steps[-1]:
+                other_strip = more_strip
+            else:
+                strip_grad = strip_grad + more_strip
         weights, norm = kept + more, norm + more_norm
     grad_features = pl.pallas_call(
         unpack_kernel,
@@ -524,7 +584,7 @@
         compiler_params=params,
     )(grad_own, returned).transpose(2, 0, 1, 3)
     chunk = weights if packed else jnp.zeros((40, 128), f32)
-    parity = side(*lon_steps[0])[None]
+    parity = side(*strip_step)[None]
     grad_bias, grad_weights, grad_norm = pl.pallas_call(
         finish_kernel,
         out_shape=(shape((HEADS, LONREL, PW, PAIRS), f32), shape((48, 96), f32), shape((2, D), f32)),

time: 51.6 us -> 49.9 us (0.967)
  waiting for transfers between devices: 26.2 us -> 23.8 us
  starting transfers between devices: 6.66 us -> 8.37 us
  Pallas kernels: 17.3 us -> 16.3 us
    ppermute x6, waiting for transfers between devices: 21 us -> 18.7 us  [exchanged(): return lax.ppermute(value, ('lat', 'lon'), partners(*step))]
    ppermute x6, starting transfers between devices: 1.91 us -> 3.74 us  [exchanged(): return lax.ppermute(value, ('lat', 'lon'), partners(*step))]
    pallas_call x1, Pallas kernels: 9.6 us -> 8.59 us  [shards(): pl.pallas_call(functools.partial(block_kernel, factor, packed), out_shape...]
where the time goes in v4:
time: 49.9 us; the launch traced here: 49.8 us
  waiting for transfers between devices  23.8 us (48%)
  Pallas kernels  16.3 us (33%)
  starting transfers between devices  8.37 us (17%)
  between operations  0.9 us (2%)
    ppermute x6, waiting for transfers between devices, exchanged(): return lax.ppermute(value, ('lat', 'lon'), partners(*step))  18.7 us
    pallas_call x1, Pallas kernels, shards(): pl.pallas_call(functools.partial(block_kernel, factor, packed), out_shape...  8.59 us
    ppermute x1, waiting for transfers between devices, shards(): lax.ppermute(sent, 'lon', [(s, (s + 1) % lon_count) for s in range(lon_co...  5.15 us
    ppermute x6, starting transfers between devices, exchanged(): return lax.ppermute(value, ('lat', 'lon'), partners(*step))  3.74 us
    pallas_call x1, Pallas kernels, shards(): pl.pallas_call(prepare_kernel, out_shape=(pltpu.VMEM((PW, GROUP_ROWS * HE...  3.31 us
    ppermute x1, starting transfers between devices, shards(): lax.ppermute(sent, 'lon', [(s, (s + 1) % lon_count) for s in range(lon_co...  3.02 us
    ppermute x1, starting transfers between devices, shards(): lax.ppermute(grad_borrowed, 'lon', [(s, (s - 1) % lon_count) for s in ran...  1.61 us
    pallas_call x1, Pallas kernels, shards(): pl.pallas_call(pack_kernel, out_shape=(pltpu.VMEM(half_shape.shape, f32),...  1.3 us
  transfers between devices with their start and end apart: 8, of which 7 were waited for; matrix products, arithmetic and copies ran while one was open for 0% of the time, Pallas kernels for 11%

profile of v4, /device:TPU:0, one launch (start us, length us, event | category | flops | bytes accessed | tf_op | source)
XLA Modules:
  0.0 49.8 jit_solution(6179240760487700227)
XLA Ops:
  0.6 1.3 %shard_map.102 = (f32[3,2,72,128]{3,2,1,0:T(8,128)S(1)}, f32[3,2,72,128]{3,2,1,0:T(8,128)S(1)}) custom-call(f32[6,12,4,192]{3,2,1,0:T(4,128)} %bitcast.44, f32[6,12,4,192]{3,2,1,0:T(4,128)} %bitcast.45), custom_call_target="tpu_custom_call" | custom-call | tf_op jit(solution)/shard_map/pallas_call | solution.py:500
  1.9 3.0 %collective-permute-start = (f32[3,2,72,128]{3,2,1,0:T(8,128)S(1)}, f32[3,2,72,128]{3,2,1,0:T(8,128)S(1)}, u32[]{:S(2)}, u32[]{:S(2)}) collective-permute-start(f32[3,2,72,128]{3,2,1,0:T(8,128)S(1)} %get-tuple-element.20), channel_id=1, source_target_pairs={{0,1},{1,2},{2,3},{3,4},{4,5},{5,6},{6,7},{7,0},{8,9},{9,10},{10,1... | collective-permute-start | bytes 663560 | tf_op jit(solution)/shard_map/ppermute | solution.py:508
  5.0 3.3 %shard_map.103 = (f32[2,288,384]{2,1,0:T(8,128)S(1)}, f32[8,144,192]{2,1,0:T(8,128)S(1)}, f32[2,192]{1,0:T(2,128)S(1)}, f32[4,192,192]{2,1,0:T(8,128)S(1)}) custom-call(f32[6,23,2,144]{3,2,1,0:T(2,128)} %bitcast.47, f32[3,2,72,128]{3,2,1,0:T(8,128)S(1)} %get-tuple-element.21.own_ref, f32[1,192]{1,0:T(1,128)} %bitcast.50, f32[1,192]{1,0:T(1,128)} %bitcast.51, ...), custom_call_target="tpu_custom_call" | custom-call | tf_op jit(solution)/shard_map/pallas_call | solution.py:514
  8.3 5.2 %collective-permute-done.borrowed_ref = f32[3,2,72,128]{3,2,1,0:T(8,128)S(1)} collective-permute-done((f32[3,2,72,128]{3,2,1,0:T(8,128)S(1)}, f32[3,2,72,128]{3,2,1,0:T(8,128)S(1)}, u32[]{:S(2)}, u32[]{:S(2)}) %collective-permute-start) | collective-permute-done | bytes 221216 | tf_op jit(solution)/shard_map/ppermute | solution.py:508
  13.4 8.6 %shard_map.104 = (f32[3,72,128]{2,1,0:T(8,128)S(1)}, f32[3,72,128]{2,1,0:T(8,128)S(1)}, f32[2,2,2,2,2,40,128]{6,5,4,3,2,1,0:T(8,128)S(1)}, f32[192,288]{1,0:T(8,128)S(1)}, f32[8,128]{1,0:T(8,128)S(1)}) custom-call(f32[3,2,72,128]{3,2,1,0:T(8,128)S(1)} %collective-permute-done.borrowed_ref, f32[8,144,192]{2,1,0:T(8,128)S(1)} %get-tuple-element.22.projected_ref, ...), custom_call_target="tpu_custom_call" | custom-call | tf_op jit(solution)/shard_map/pallas_call | solution.py:534
  22.1 0.1 collective-permute-start.1
  22.2 1.2 %shard_map.106 = f32[2,144,128]{2,1,0:T(8,128)S(1)} custom-call(f32[192,288]{1,0:T(8,128)S(1)} %get-tuple-element.31.strip_ref), custom_call_target="tpu_custom_call" | custom-call | tf_op jit(solution)/shard_map/pallas_call | solution.py:551
  23.5 0.1 collective-permute-start.4
  23.5 0.3 collective-permute-done.1
  23.9 1.6 %collective-permute-start.2 = (f32[328,128]{1,0:T(8,128)S(1)}, f32[328,128]{1,0:T(8,128)S(1)}, u32[]{:S(2)}, u32[]{:S(2)}) collective-permute-start(f32[328,128]{1,0:T(8,128)S(1)} %pad_maximum_fusion.1), channel_id=1, source_target_pairs={{0,16},{1,17},{2,18},{3,19},{4,20},{5,21},{6,22},{7,23},{8,24},{9,... | collective-permute-start | bytes 503816 | tf_op jit(solution)/shard_map/ppermute | solution.py:441
  25.5 2.4 %collective-permute-done.4 = f32[144,128]{1,0:T(8,128)S(1)} collective-permute-done((f32[144,128]{1,0:T(8,128)S(1)}, f32[144,128]{1,0:T(8,128)S(1)}, u32[]{:S(2)}, u32[]{:S(2)}) %collective-permute-start.4) | collective-permute-done | bytes 73760 | tf_op jit(solution)/shard_map/ppermute | solution.py:441
  27.9 2.5 %collective-permute-done.2 = f32[328,128]{1,0:T(8,128)S(1)} collective-permute-done((f32[328,128]{1,0:T(8,128)S(1)}, f32[328,128]{1,0:T(8,128)S(1)}, u32[]{:S(2)}, u32[]{:S(2)}) %collective-permute-start.2) | collective-permute-done | bytes 167968 | tf_op jit(solution)/shard_map/ppermute | solution.py:441
  30.5 0.1 collective-permute-start.5
  30.6 5.9 %collective-permute-done.5 = f32[312,128]{1,0:T(8,128)S(1)} collective-permute-done((f32[312,128]{1,0:T(8,128)S(1)}, f32[312,128]{1,0:T(8,128)S(1)}, u32[]{:S(2)}, u32[]{:S(2)}) %collective-permute-start.5) | collective-permute-done | bytes 159776 | tf_op jit(solution)/shard_map/ppermute | solution.py:441
  36.6 1.7 %collective-permute-start.6 = (f32[232,128]{1,0:T(8,128)S(1)}, f32[232,128]{1,0:T(8,128)S(1)}, u32[]{:S(2)}, u32[]{:S(2)}) collective-permute-start(f32[232,128]{1,0:T(8,128)S(1)} %pad_maximum_fusion.3), channel_id=1, source_target_pairs={{0,4},{1,5},{2,6},{3,7},{4,0},{5,1},{6,2},{7,3},{8,9},{9,8},{10,11... | collective-permute-start | bytes 356360 | tf_op jit(solution)/shard_map/ppermute | solution.py:441
  38.3 1.6 %collective-permute-start.3 = (f32[3,72,128]{2,1,0:T(8,128)S(1)}, f32[3,72,128]{2,1,0:T(8,128)S(1)}, u32[]{:S(2)}, u32[]{:S(2)}) collective-permute-start(f32[3,72,128]{2,1,0:T(8,128)S(1)} %get-tuple-element.30), channel_id=1, source_target_pairs={{0,7},{1,0},{2,1},{3,2},{4,3},{5,4},{6,5},{7,6},{8,15},{9,8},{10,9... | collective-permute-start | bytes 331784 | tf_op jit(solution)/shard_map/ppermute | solution.py:572
  39.9 4.2 %collective-permute-done.6 = f32[232,128]{1,0:T(8,128)S(1)} collective-permute-done((f32[232,128]{1,0:T(8,128)S(1)}, f32[232,128]{1,0:T(8,128)S(1)}, u32[]{:S(2)}, u32[]{:S(2)}) %collective-permute-start.6) | collective-permute-done | bytes 118816 | tf_op jit(solution)/shard_map/ppermute | solution.py:441
  44.2 0.3 collective-permute-start.7
  44.5 0.0 collective-permute-done.3.returned_ref
  44.5 1.0 %shard_map.105 = f32[6,12,4,192]{3,2,1,0:T(4,128)} custom-call(f32[3,72,128]{2,1,0:T(8,128)S(1)} %get-tuple-element.26.own_ref, f32[3,72,128]{2,1,0:T(8,128)S(1)} %collective-permute-done.3.returned_ref), custom_call_target="tpu_custom_call" | custom-call | tf_op jit(solution)/shard_map/pallas_call | solution.py:579
  45.5 3.4 %collective-permute-done.7 = f32[192,128]{1,0:T(8,128)S(1)} collective-permute-done((f32[192,128]{1,0:T(8,128)S(1)}, f32[192,128]{1,0:T(8,128)S(1)}, u32[]{:S(2)}, u32[]{:S(2)}) %collective-permute-start.7) | collective-permute-done | bytes 98336 | tf_op jit(solution)/shard_map/ppermute | solution.py:441
  48.9 0.9 %shard_map.107 = (f32[6,23,2,144]{3,2,1,0:T(2,128)}, f32[48,96]{1,0:T(8,128)}, f32[2,192]{1,0:T(2,128)}) custom-call(s32[1]{0:T(128)} %bitcast.14.parity_ref, f32[144,128]{1,0:T(8,128)S(1)} %slice_add_fusion.mine_ref, f32[144,128]{1,0:T(8,128)S(1)} %slice.72.other_ref, f32[40,128]{1,0:T(8,128)S(1)} %slice_add_fusion.2.weights_ref, ...), custom_call_target="tpu_custom_call" | custom-call | tf_op jit(solution)/shard_map/pallas_call | solution.py:588
  (31 shorter events, 0.4 us)
Async XLA Ops:
  1.9 11.5 %collective-permute-start = (f32[3,2,72,128]{3,2,1,0:T(8,128)S(1)}, f32[3,2,72,128]{3,2,1,0:T(8,128)S(1)}, u32[]{:S(2)}, u32[]{:S(2)}) collective-permute-start(f32[3,2,72,128]{3,2,1,0:T(8,128)S(1)} %get-tuple-element.20), channel_id=1, source_target_pairs={{0,1},{1,2},{2,3},{3,4},{4,5},{5,6},{6,7},{7,0},{8,9},{9,10},{10,1... | collective-permute-start | bytes 663560 | tf_op jit(solution)/shard_map/ppermute | solution.py:508
  22.1 1.7 %collective-permute-start.1 = (f32[648,128]{1,0:T(8,128)S(1)}, f32[648,128]{1,0:T(8,128)S(1)}, u32[]{:S(2)}, u32[]{:S(2)}) collective-permute-start(f32[648,128]{1,0:T(8,128)S(1)} %pad_maximum_fusion), channel_id=1, source_target_pairs={{0,8},{1,9},{2,10},{3,11},{4,12},{5,13},{6,14},{7,15},{8,0},{9,1},... | collective-permute-start | bytes 995336 | tf_op jit(solution)/shard_map/ppermute | solution.py:441
  23.5 4.4 %collective-permute-start.4 = (f32[144,128]{1,0:T(8,128)S(1)}, f32[144,128]{1,0:T(8,128)S(1)}, u32[]{:S(2)}, u32[]{:S(2)}) collective-permute-start(f32[144,128]{1,0:T(8,128)S(1)} %dynamic-slice_bitcast_fusion.1), channel_id=1, source_target_pairs={{0,1},{1,0},{2,3},{3,2},{4,5},{5,4},{6,7},{7,6},{8,10},{9,11},{10,... | collective-permute-start | bytes 221192 | tf_op jit(solution)/shard_map/ppermute | solution.py:441
  23.9 6.5 %collective-permute-start.2 = (f32[328,128]{1,0:T(8,128)S(1)}, f32[328,128]{1,0:T(8,128)S(1)}, u32[]{:S(2)}, u32[]{:S(2)}) collective-permute-start(f32[328,128]{1,0:T(8,128)S(1)} %pad_maximum_fusion.1), channel_id=1, source_target_pairs={{0,16},{1,17},{2,18},{3,19},{4,20},{5,21},{6,22},{7,23},{8,24},{9,... | collective-permute-start | bytes 503816 | tf_op jit(solution)/shard_map/ppermute | solution.py:441
  30.5 6.0 %collective-permute-start.5 = (f32[312,128]{1,0:T(8,128)S(1)}, f32[312,128]{1,0:T(8,128)S(1)}, u32[]{:S(2)}, u32[]{:S(2)}) collective-permute-start(f32[312,128]{1,0:T(8,128)S(1)} %pad_maximum_fusion.2), channel_id=1, source_target_pairs={{0,2},{1,3},{2,0},{3,1},{4,6},{5,7},{6,4},{7,5},{8,12},{9,13},{10,... | collective-permute-start | bytes 479240 | tf_op jit(solution)/shard_map/ppermute | solution.py:441
  36.6 7.5 %collective-permute-start.6 = (f32[232,128]{1,0:T(8,128)S(1)}, f32[232,128]{1,0:T(8,128)S(1)}, u32[]{:S(2)}, u32[]{:S(2)}) collective-permute-start(f32[232,128]{1,0:T(8,128)S(1)} %pad_maximum_fusion.3), channel_id=1, source_target_pairs={{0,4},{1,5},{2,6},{3,7},{4,0},{5,1},{6,2},{7,3},{8,9},{9,8},{10,11... | collective-permute-start | bytes 356360 | tf_op jit(solution)/shard_map/ppermute | solution.py:441
  38.3 6.2 %collective-permute-start.3 = (f32[3,72,128]{2,1,0:T(8,128)S(1)}, f32[3,72,128]{2,1,0:T(8,128)S(1)}, u32[]{:S(2)}, u32[]{:S(2)}) collective-permute-start(f32[3,72,128]{2,1,0:T(8,128)S(1)} %get-tuple-element.30), channel_id=1, source_target_pairs={{0,7},{1,0},{2,1},{3,2},{4,3},{5,4},{6,5},{7,6},{8,15},{9,8},{10,9... | collective-permute-start | bytes 331784 | tf_op jit(solution)/shard_map/ppermute | solution.py:572
  44.2 4.7 %collective-permute-start.7 = (f32[192,128]{1,0:T(8,128)S(1)}, f32[192,128]{1,0:T(8,128)S(1)}, u32[]{:S(2)}, u32[]{:S(2)}) collective-permute-start(f32[192,128]{1,0:T(8,128)S(1)} %pad_maximum_fusion.4), channel_id=1, source_target_pairs={{0,1},{1,0},{2,3},{3,2},{4,5},{5,4},{6,7},{7,6},{8,10},{9,11},{10,... | collective-permute-start | bytes 294920 | tf_op jit(solution)/shard_map/ppermute | solution.py:441

commit v5 on v4

--- a/solution.py
+++ b/solution.py
@@ -28,6 +28,7 @@
 BLOCK = HEADS * GROUP_ROWS
 STRIP = LONREL * LEVELS
 PADDED = 16
+TURNS = (0, 1)
 OFFSETS = 24
 
 EPSILON = 1e-05
@@ -251,8 +252,7 @@
     return jnp.concatenate([packed[:, :96], last], axis=0)
 
 
-HEADS_AT_ONCE = 6
-DEPTH = 1
+ORDER = "S0 D0 S1 P0 D1 M0 V0 P1 G0 M1 V1 G1 Q0 K0 T0 Q1 K1 T1".split()
 
 
 def halves_of(value):
@@ -297,68 +297,69 @@
         rows = slice(c * HALF_ROWS, (c + 1) * HALF_ROWS)
         return jnp.concatenate([arrived_ref[index, rows], projected_ref[index, rows]], axis=0)
 
+    lane = lax.broadcasted_iota(jnp.int32, (1, D), 1) // HEAD
+    head_masks = [(lane == h).astype(jnp.float32).astype(jnp.bfloat16) for h in range(HEADS)]
     head_of_lane = lax.broadcasted_iota(jnp.int32, (WIN, D), 1) // HEAD
     strip_grad_ref[...] = jnp.zeros_like(strip_grad_ref)
     table_grad_ref[...] = jnp.zeros_like(table_grad_ref)
-    windows = []
-    for c in range(PW):
-        windows.append(
-            dict(
-                queries=whole_window(4, c),
-                grad=whole_window(7, c),
-                keys=parts_of(whole_window(5, c), 3),
-                values=halves_of(whole_window(6, c)),
-                mixture=None, grad_q=None, grad_k=None, grad_v=None,
-            )
-        )
-
-    def add(window, name, value):
-        window[name] = value if window[name] is None else window[name] + value
-
-    def masked(value, heads):
-        return jnp.concatenate([jnp.where(head_of_lane == h, value, 0.0) for h in heads], axis=0)
-
-    def joined(value, heads):
-        return sum(jnp.where(head_of_lane == h, value[n * WIN : (n + 1) * WIN], 0.0) for n, h in enumerate(heads))
-
-    def first_stage(c, heads):
-        window = windows[c]
-        stack = parts_of(masked(window["queries"], heads), 3)
-        scores = full_product(stack, window["keys"], RIGHT)
+
+    def masked(parts):
+        return tuple(jnp.concatenate([part * mask for mask in head_masks], axis=0) for part in parts)
+
+    def joined(value):
+        total = value[:WIN]
+        for h in range(1, HEADS):
+            total = jnp.where(head_of_lane == h, value[h * WIN : (h + 1) * WIN], total)
+        return total
+
+    def score(window, c):
+        window["keys"] = parts_of(whole_window(5, c), 3)
+        window["queries"] = masked(parts_of(whole_window(4, c), 3))
+        window["scores"] = full_product(window["queries"], window["keys"], RIGHT)
+
+    def grad_attend(window, c):
+        window["values"] = halves_of(whole_window(6, c))
+        window["grads"] = masked(halves_of(whole_window(7, c)))
+        window["grad_attention"] = product(window["grads"], window["values"], RIGHT)
+
+    def softmax(window, c):
         biased = []
-        for n, h in enumerate(heads):
+        for h in range(HEADS):
             for g in range(GROUPS):
-                first = n * WIN + g * GROUP_ROWS
+                first = h * WIN + g * GROUP_ROWS
                 start = (WLON - 1 - GROUP * g) * LEVELS
                 bias = table_ref[c, h * GROUP_ROWS : (h + 1) * GROUP_ROWS, start : start + WIN]
-                biased.append(scores[first : first + GROUP_ROWS] + bias)
+                biased.append(window["scores"][first : first + GROUP_ROWS] + bias)
         scores = jnp.concatenate(biased, axis=0)
         exponent = jnp.exp(scores - jnp.max(scores, axis=-1, keepdims=True))
-        attention = exponent * (1.0 / jnp.sum(exponent, axis=-1, keepdims=True))
-        return stack[:2], attention
-
-    def second_stage(c, heads, stack, attention):
-        window = windows[c]
-        halves = halves_of(attention)
-        add(window, "mixture", joined(product(halves, window["values"], NORMAL), heads))
-        grad_stack = halves_of(masked(window["grad"], heads))
-        grad_attention = product(grad_stack, window["values"], RIGHT)
+        window["attention"] = exponent * (1.0 / jnp.sum(exponent, axis=-1, keepdims=True))
+        window["halves"] = halves_of(window["attention"])
+
+    def mix(window, c):
+        window["mixture"] = joined(product(window["halves"], window["values"], NORMAL))
+
+    def value_grad(window, c):
+        window["grad_v"] = product(window["halves"], window["grads"], LEFT)
+
+    def score_grad(window, c):
+        attention, grad_attention = window["attention"], window["grad_attention"]
         weighted = jnp.sum(attention * grad_attention, axis=-1, keepdims=True)
-        grad_scores = attention * (grad_attention - weighted)
-        add(window, "grad_v", product(halves, grad_stack, LEFT))
-        return stack, grad_scores
-
-    def third_stage(c, heads, stack, grad_scores):
-        window = windows[c]
-        halves = halves_of(grad_scores)
-        add(window, "grad_q", joined(product(halves, window["keys"][:2], NORMAL), heads))
-        add(window, "grad_k", product(halves, stack, LEFT))
-        for n, h in enumerate(heads):
+        window["grad_scores"] = attention * (grad_attention - weighted)
+        window["score_halves"] = halves_of(window["grad_scores"])
+
+    def query_grad(window, c):
+        window["grad_q"] = joined(product(window["score_halves"], window["keys"][:2], NORMAL))
+
+    def key_grad(window, c):
+        window["grad_k"] = product(window["score_halves"], window["queries"][:2], LEFT)
+
+    def strip_grad(window, c):
+        for h in range(HEADS):
             table_rows = slice((c * HEADS + h) * GROUP_ROWS, (c * HEADS + h + 1) * GROUP_ROWS)
             for g in range(GROUPS):
-                first = n * WIN + g * GROUP_ROWS
+                first = h * WIN + g * GROUP_ROWS
                 start = (WLON - 1 - GROUP * g) * LEVELS
-                table_grad_ref[table_rows, start : start + WIN] += grad_scores[first : first + GROUP_ROWS]
+                table_grad_ref[table_rows, start : start + WIN] += window["grad_scores"][first : first + GROUP_ROWS]
             total = None
             for g in range(GROUP):
                 first = (c * HEADS + h) * GROUP_ROWS + g * LEVELS
@@ -367,16 +368,12 @@
             first = (c * HEADS + h) * PADDED
             strip_grad_ref[first : first + LEVELS, :STRIP] = total
 
-    chunks = [
-        (c, tuple(range(h, h + HEADS_AT_ONCE))) for h in range(0, HEADS, HEADS_AT_ONCE) for c in range(PW)
-    ]
-    stages = (first_stage, second_stage, third_stage)
-    state = {}
-    for tick in range(len(chunks) + DEPTH * (len(stages) - 1)):
-        for place in reversed(range(len(stages))):
-            index = tick - DEPTH * place
-            if 0 <= index < len(chunks):
-                state[index] = stages[place](*chunks[index], *(state[index] if place else ()))
+    windows = [{}, {}]
+    stages = dict(
+        S=score, P=softmax, D=grad_attend, M=mix, V=value_grad, G=score_grad, Q=query_grad, K=key_grad, T=strip_grad
+    )
+    for name, c in ORDER:
+        stages[name](windows[int(c)], int(c))
 
     def rows_of(name):
         return jnp.concatenate([window[name] for window in windows], axis=0)
@@ -413,7 +410,7 @@
         for y in range(2):
             for lat in range(4):
                 chunk = total[48 * lat : 48 * (lat + 1), 96 * y : 96 * (y + 1)]
-                place = (block % 2, block // 2, y) if lat % 2 == 0 else (block // 2, y, block % 2)
+                place = turned_by((y, block % 2, block // 2), TURNS[lat % 2])
                 weights_ref[(lat % 2, lat // 2) + place] = packed_chunk(chunk)
 
 
@@ -466,7 +463,7 @@
 def summing_steps(lat_count, lon_count):
     lat_bits, lon_bits = bits_of(lat_count), bits_of(lon_count)
     lat_steps = [((bit, 0), (bit, 0)) for bit in lat_bits]
-    lon_steps = [((0, first), (0, second)) for first, second in zip(turned_by(lon_bits, 1), turned_by(lon_bits, 2))]
+    lon_steps = [((0, first), (0, second)) for first, second in zip(*(turned_by(lon_bits, turn) for turn in TURNS))]
     return lat_steps, lon_steps, lon_steps[-1]
 
 
@@ -477,7 +474,7 @@
     lat_dims = list(range(lat_places))[::-1]
     lon_dims = list(range(lat_places + 1, lat_places + 1 + lon_places))[::-1]
     halves = []
-    for core, dims in enumerate((turned_by(lon_dims, 1), turned_by(lon_dims, 2))):
+    for core, dims in enumerate(turned_by(lon_dims, turn) for turn in TURNS):
         order = lat_dims + dims + [lat_places, lat_places + 1 + lon_places]
         halves.append(split.transpose(order)[core])
     places = lat_places + lon_places
@@ -557,7 +554,7 @@
         compiler_params=params,
     )(strips)
     lat_steps, lon_steps, strip_step = summing_steps(lat_count, lon_count)
-    apart = lon_steps[0][0][1]
+    apart = lon_steps[0][0][1] if (TURNS[1] - TURNS[0]) % len(lon_steps) == 1 else lon_steps[0][1][1]
     norm = jnp.where(lax.axis_index("lon") & apart == 0, norm, jnp.roll(norm, 4, 0))
     strip_grad, given_strip = kept_and_given(strip_grad, strip_step)
     strip_grad = strip_grad + exchanged(given_strip, strip_step)

time: 49.9 us -> 47.7 us (0.956)
  waiting for transfers between devices: 23.8 us -> 20.6 us
  starting transfers between devices: 8.37 us -> 11.1 us
  Pallas kernels: 16.3 us -> 14.5 us
    ppermute x6, waiting for transfers between devices: 18.7 us -> 15.5 us  [exchanged(): return lax.ppermute(value, ('lat', 'lon'), partners(*step))]
    ppermute x6, starting transfers between devices: 3.74 us -> 6.3 us  [exchanged(): return lax.ppermute(value, ('lat', 'lon'), partners(*step))]
    pallas_call x1, Pallas kernels: 8.59 us -> 6.83 us  [shards(): pl.pallas_call(functools.partial(block_kernel, factor, packed), out_shape...]
  transfers between devices with their start and end apart: 8 -> 8, of which waited for: 7 -> 6; matrix products, arithmetic and copies ran while one was open for 0% -> 0% of each run, Pallas kernels for 11% -> 12%
where the time goes in v5:
time: 47.7 us; the launch traced here: 47.6 us
  waiting for transfers between devices  20.6 us (43%)
  Pallas kernels  14.5 us (30%)
  starting transfers between devices  11.1 us (23%)
  between operations  0.88 us (2%)
    ppermute x6, waiting for transfers between devices, exchanged(): return lax.ppermute(value, ('lat', 'lon'), partners(*step))  15.5 us
    pallas_call x1, Pallas kernels, shards(): pl.pallas_call(functools.partial(block_kernel, factor, packed), out_shape...  6.83 us
    ppermute x6, starting transfers between devices, exchanged(): return lax.ppermute(value, ('lat', 'lon'), partners(*step))  6.3 us
    ppermute x1, waiting for transfers between devices, shards(): lax.ppermute(sent, 'lon', [(s, (s + 1) % lon_count) for s in range(lon_co...  5.15 us
    pallas_call x1, Pallas kernels, shards(): pl.pallas_call(prepare_kernel, out_shape=(pltpu.VMEM((PW, GROUP_ROWS * HE...  3.31 us
    ppermute x1, starting transfers between devices, shards(): lax.ppermute(sent, 'lon', [(s, (s + 1) % lon_count) for s in range(lon_co...  3.02 us
    ppermute x1, starting transfers between devices, shards(): lax.ppermute(grad_borrowed, 'lon', [(s, (s - 1) % lon_count) for s in ran...  1.8 us
    pallas_call x1, Pallas kernels, shards(): pl.pallas_call(pack_kernel, out_shape=(pltpu.VMEM(half_shape.shape, f32),...  1.3 us
  transfers between devices with their start and end apart: 8, of which 6 were waited for; matrix products, arithmetic and copies ran while one was open for 0% of the time, Pallas kernels for 12%

profile of v5, /device:TPU:0, one launch (start us, length us, event | category | flops | bytes accessed | tf_op | source)
XLA Modules:
  0.0 47.6 jit_solution(17975070429675269012)
XLA Ops:
  0.6 1.3 %shard_map.102 = (f32[3,2,72,128]{3,2,1,0:T(8,128)S(1)}, f32[3,2,72,128]{3,2,1,0:T(8,128)S(1)}) custom-call(f32[6,12,4,192]{3,2,1,0:T(4,128)} %bitcast.44, f32[6,12,4,192]{3,2,1,0:T(4,128)} %bitcast.45), custom_call_target="tpu_custom_call" | custom-call | tf_op jit(solution)/shard_map/pallas_call | solution.py:497
  1.9 3.0 %collective-permute-start = (f32[3,2,72,128]{3,2,1,0:T(8,128)S(1)}, f32[3,2,72,128]{3,2,1,0:T(8,128)S(1)}, u32[]{:S(2)}, u32[]{:S(2)}) collective-permute-start(f32[3,2,72,128]{3,2,1,0:T(8,128)S(1)} %get-tuple-element.20), channel_id=1, source_target_pairs={{0,1},{1,2},{2,3},{3,4},{4,5},{5,6},{6,7},{7,0},{8,9},{9,10},{10,1... | collective-permute-start | bytes 663560 | tf_op jit(solution)/shard_map/ppermute | solution.py:505
  5.0 3.3 %shard_map.103 = (f32[2,288,384]{2,1,0:T(8,128)S(1)}, f32[8,144,192]{2,1,0:T(8,128)S(1)}, f32[2,192]{1,0:T(2,128)S(1)}, f32[4,192,192]{2,1,0:T(8,128)S(1)}) custom-call(f32[6,23,2,144]{3,2,1,0:T(2,128)} %bitcast.47, f32[3,2,72,128]{3,2,1,0:T(8,128)S(1)} %get-tuple-element.21.own_ref, f32[1,192]{1,0:T(1,128)} %bitcast.50, f32[1,192]{1,0:T(1,128)} %bitcast.51, ...), custom_call_target="tpu_custom_call" | custom-call | tf_op jit(solution)/shard_map/pallas_call | solution.py:511
  8.3 5.2 %collective-permute-done.borrowed_ref = f32[3,2,72,128]{3,2,1,0:T(8,128)S(1)} collective-permute-done((f32[3,2,72,128]{3,2,1,0:T(8,128)S(1)}, f32[3,2,72,128]{3,2,1,0:T(8,128)S(1)}, u32[]{:S(2)}, u32[]{:S(2)}) %collective-permute-start) | collective-permute-done | bytes 221216 | tf_op jit(solution)/shard_map/ppermute | solution.py:505
  13.4 6.8 %shard_map.104 = (f32[3,72,128]{2,1,0:T(8,128)S(1)}, f32[3,72,128]{2,1,0:T(8,128)S(1)}, f32[2,2,2,2,2,40,128]{6,5,4,3,2,1,0:T(8,128)S(1)}, f32[192,288]{1,0:T(8,128)S(1)}, f32[8,128]{1,0:T(8,128)S(1)}) custom-call(f32[3,2,72,128]{3,2,1,0:T(8,128)S(1)} %collective-permute-done.borrowed_ref, f32[8,144,192]{2,1,0:T(8,128)S(1)} %get-tuple-element.22.projected_ref, ...), custom_call_target="tpu_custom_call" | custom-call | tf_op jit(solution)/shard_map/pallas_call | solution.py:531
  20.3 0.1 collective-permute-start.1
  20.5 1.2 %shard_map.106 = f32[2,144,128]{2,1,0:T(8,128)S(1)} custom-call(f32[192,288]{1,0:T(8,128)S(1)} %get-tuple-element.31.strip_ref), custom_call_target="tpu_custom_call" | custom-call | tf_op jit(solution)/shard_map/pallas_call | solution.py:548
  21.7 0.7 %collective-permute-start.4 = (f32[144,128]{1,0:T(8,128)S(1)}, f32[144,128]{1,0:T(8,128)S(1)}, u32[]{:S(2)}, u32[]{:S(2)}) collective-permute-start(f32[144,128]{1,0:T(8,128)S(1)} %dynamic-slice_bitcast_fusion.1), channel_id=1, source_target_pairs={{0,4},{1,5},{2,6},{3,7},{4,0},{5,1},{6,2},{7,3},{8,9},{9,8},{10,11... | collective-permute-start | bytes 221192 | tf_op jit(solution)/shard_map/ppermute | solution.py:438
  22.4 0.0 collective-permute-done.1
  22.6 1.6 %collective-permute-start.2 = (f32[328,128]{1,0:T(8,128)S(1)}, f32[328,128]{1,0:T(8,128)S(1)}, u32[]{:S(2)}, u32[]{:S(2)}) collective-permute-start(f32[328,128]{1,0:T(8,128)S(1)} %pad_maximum_fusion.1), channel_id=1, source_target_pairs={{0,16},{1,17},{2,18},{3,19},{4,20},{5,21},{6,22},{7,23},{8,24},{9,... | collective-permute-start | bytes 503816 | tf_op jit(solution)/shard_map/ppermute | solution.py:438
  24.1 2.9 %collective-permute-done.4 = f32[144,128]{1,0:T(8,128)S(1)} collective-permute-done((f32[144,128]{1,0:T(8,128)S(1)}, f32[144,128]{1,0:T(8,128)S(1)}, u32[]{:S(2)}, u32[]{:S(2)}) %collective-permute-start.4) | collective-permute-done | bytes 73760 | tf_op jit(solution)/shard_map/ppermute | solution.py:438
  27.0 1.6 %collective-permute-done.2 = f32[328,128]{1,0:T(8,128)S(1)} collective-permute-done((f32[328,128]{1,0:T(8,128)S(1)}, f32[328,128]{1,0:T(8,128)S(1)}, u32[]{:S(2)}, u32[]{:S(2)}) %collective-permute-start.2) | collective-permute-done | bytes 167968 | tf_op jit(solution)/shard_map/ppermute | solution.py:438
  28.8 1.8 %collective-permute-start.5 = (f32[312,128]{1,0:T(8,128)S(1)}, f32[312,128]{1,0:T(8,128)S(1)}, u32[]{:S(2)}, u32[]{:S(2)}) collective-permute-start(f32[312,128]{1,0:T(8,128)S(1)} %pad_maximum_fusion.2), channel_id=1, source_target_pairs={{0,1},{1,0},{2,3},{3,2},{4,5},{5,4},{6,7},{7,6},{8,10},{9,11},{10,... | collective-permute-start | bytes 479240 | tf_op jit(solution)/shard_map/ppermute | solution.py:438
  30.6 3.6 %collective-permute-done.5 = f32[312,128]{1,0:T(8,128)S(1)} collective-permute-done((f32[312,128]{1,0:T(8,128)S(1)}, f32[312,128]{1,0:T(8,128)S(1)}, u32[]{:S(2)}, u32[]{:S(2)}) %collective-permute-start.5) | collective-permute-done | bytes 159776 | tf_op jit(solution)/shard_map/ppermute | solution.py:438
  34.2 1.0 %collective-permute-start.6 = (f32[232,128]{1,0:T(8,128)S(1)}, f32[232,128]{1,0:T(8,128)S(1)}, u32[]{:S(2)}, u32[]{:S(2)}) collective-permute-start(f32[232,128]{1,0:T(8,128)S(1)} %pad_maximum_fusion.3), channel_id=1, source_target_pairs={{0,2},{1,3},{2,0},{3,1},{4,6},{5,7},{6,4},{7,5},{8,12},{9,13},{10,... | collective-permute-start | bytes 356360 | tf_op jit(solution)/shard_map/ppermute | solution.py:438
  35.2 1.8 %collective-permute-start.3 = (f32[3,72,128]{2,1,0:T(8,128)S(1)}, f32[3,72,128]{2,1,0:T(8,128)S(1)}, u32[]{:S(2)}, u32[]{:S(2)}) collective-permute-start(f32[3,72,128]{2,1,0:T(8,128)S(1)} %get-tuple-element.30), channel_id=1, source_target_pairs={{0,7},{1,0},{2,1},{3,2},{4,3},{5,4},{6,5},{7,6},{8,15},{9,8},{10,9... | collective-permute-start | bytes 331784 | tf_op jit(solution)/shard_map/ppermute | solution.py:569
  37.0 3.5 %collective-permute-done.6 = f32[232,128]{1,0:T(8,128)S(1)} collective-permute-done((f32[232,128]{1,0:T(8,128)S(1)}, f32[232,128]{1,0:T(8,128)S(1)}, u32[]{:S(2)}, u32[]{:S(2)}) %collective-permute-start.6) | collective-permute-done | bytes 118816 | tf_op jit(solution)/shard_map/ppermute | solution.py:438
  40.6 1.2 %collective-permute-start.7 = (f32[192,128]{1,0:T(8,128)S(1)}, f32[192,128]{1,0:T(8,128)S(1)}, u32[]{:S(2)}, u32[]{:S(2)}) collective-permute-start(f32[192,128]{1,0:T(8,128)S(1)} %pad_maximum_fusion.4), channel_id=1, source_target_pairs={{0,4},{1,5},{2,6},{3,7},{4,0},{5,1},{6,2},{7,3},{8,9},{9,8},{10,11... | collective-permute-start | bytes 294920 | tf_op jit(solution)/shard_map/ppermute | solution.py:438
  41.8 0.0 collective-permute-done.3.returned_ref
  41.8 1.0 %shard_map.105 = f32[6,12,4,192]{3,2,1,0:T(4,128)} custom-call(f32[3,72,128]{2,1,0:T(8,128)S(1)} %get-tuple-element.26.own_ref, f32[3,72,128]{2,1,0:T(8,128)S(1)} %collective-permute-done.3.returned_ref), custom_call_target="tpu_custom_call" | custom-call | tf_op jit(solution)/shard_map/pallas_call | solution.py:576
  42.8 3.9 %collective-permute-done.7 = f32[192,128]{1,0:T(8,128)S(1)} collective-permute-done((f32[192,128]{1,0:T(8,128)S(1)}, f32[192,128]{1,0:T(8,128)S(1)}, u32[]{:S(2)}, u32[]{:S(2)}) %collective-permute-start.7) | collective-permute-done | bytes 98336 | tf_op jit(solution)/shard_map/ppermute | solution.py:438
  46.7 0.9 %shard_map.107 = (f32[6,23,2,144]{3,2,1,0:T(2,128)}, f32[48,96]{1,0:T(8,128)}, f32[2,192]{1,0:T(2,128)}) custom-call(s32[1]{0:T(128)} %bitcast.14.parity_ref, f32[144,128]{1,0:T(8,128)S(1)} %slice_add_fusion.mine_ref, f32[144,128]{1,0:T(8,128)S(1)} %slice.72.other_ref, f32[40,128]{1,0:T(8,128)S(1)} %slice_add_fusion.2.weights_ref, ...), custom_call_target="tpu_custom_call" | custom-call | tf_op jit(solution)/shard_map/pallas_call | solution.py:585
  (31 shorter events, 0.4 us)
Async XLA Ops:
  1.9 11.5 %collective-permute-start = (f32[3,2,72,128]{3,2,1,0:T(8,128)S(1)}, f32[3,2,72,128]{3,2,1,0:T(8,128)S(1)}, u32[]{:S(2)}, u32[]{:S(2)}) collective-permute-start(f32[3,2,72,128]{3,2,1,0:T(8,128)S(1)} %get-tuple-element.20), channel_id=1, source_target_pairs={{0,1},{1,2},{2,3},{3,4},{4,5},{5,6},{6,7},{7,0},{8,9},{9,10},{10,1... | collective-permute-start | bytes 663560 | tf_op jit(solution)/shard_map/ppermute | solution.py:505
  20.3 2.1 %collective-permute-start.1 = (f32[648,128]{1,0:T(8,128)S(1)}, f32[648,128]{1,0:T(8,128)S(1)}, u32[]{:S(2)}, u32[]{:S(2)}) collective-permute-start(f32[648,128]{1,0:T(8,128)S(1)} %pad_maximum_fusion), channel_id=1, source_target_pairs={{0,8},{1,9},{2,10},{3,11},{4,12},{5,13},{6,14},{7,15},{8,0},{9,1},... | collective-permute-start | bytes 995336 | tf_op jit(solution)/shard_map/ppermute | solution.py:438
  21.7 5.3 %collective-permute-start.4 = (f32[144,128]{1,0:T(8,128)S(1)}, f32[144,128]{1,0:T(8,128)S(1)}, u32[]{:S(2)}, u32[]{:S(2)}) collective-permute-start(f32[144,128]{1,0:T(8,128)S(1)} %dynamic-slice_bitcast_fusion.1), channel_id=1, source_target_pairs={{0,4},{1,5},{2,6},{3,7},{4,0},{5,1},{6,2},{7,3},{8,9},{9,8},{10,11... | collective-permute-start | bytes 221192 | tf_op jit(solution)/shard_map/ppermute | solution.py:438
  22.6 6.1 %collective-permute-start.2 = (f32[328,128]{1,0:T(8,128)S(1)}, f32[328,128]{1,0:T(8,128)S(1)}, u32[]{:S(2)}, u32[]{:S(2)}) collective-permute-start(f32[328,128]{1,0:T(8,128)S(1)} %pad_maximum_fusion.1), channel_id=1, source_target_pairs={{0,16},{1,17},{2,18},{3,19},{4,20},{5,21},{6,22},{7,23},{8,24},{9,... | collective-permute-start | bytes 503816 | tf_op jit(solution)/shard_map/ppermute | solution.py:438
  28.8 5.3 %collective-permute-start.5 = (f32[312,128]{1,0:T(8,128)S(1)}, f32[312,128]{1,0:T(8,128)S(1)}, u32[]{:S(2)}, u32[]{:S(2)}) collective-permute-start(f32[312,128]{1,0:T(8,128)S(1)} %pad_maximum_fusion.2), channel_id=1, source_target_pairs={{0,1},{1,0},{2,3},{3,2},{4,5},{5,4},{6,7},{7,6},{8,10},{9,11},{10,... | collective-permute-start | bytes 479240 | tf_op jit(solution)/shard_map/ppermute | solution.py:438
  34.2 6.3 %collective-permute-start.6 = (f32[232,128]{1,0:T(8,128)S(1)}, f32[232,128]{1,0:T(8,128)S(1)}, u32[]{:S(2)}, u32[]{:S(2)}) collective-permute-start(f32[232,128]{1,0:T(8,128)S(1)} %pad_maximum_fusion.3), channel_id=1, source_target_pairs={{0,2},{1,3},{2,0},{3,1},{4,6},{5,7},{6,4},{7,5},{8,12},{9,13},{10,... | collective-permute-start | bytes 356360 | tf_op jit(solution)/shard_map/ppermute | solution.py:438
  35.2 6.6 %collective-permute-start.3 = (f32[3,72,128]{2,1,0:T(8,128)S(1)}, f32[3,72,128]{2,1,0:T(8,128)S(1)}, u32[]{:S(2)}, u32[]{:S(2)}) collective-permute-start(f32[3,72,128]{2,1,0:T(8,128)S(1)} %get-tuple-element.30), channel_id=1, source_target_pairs={{0,7},{1,0},{2,1},{3,2},{4,3},{5,4},{6,5},{7,6},{8,15},{9,8},{10,9... | collective-permute-start | bytes 331784 | tf_op jit(solution)/shard_map/ppermute | solution.py:569
  40.6 6.0 %collective-permute-start.7 = (f32[192,128]{1,0:T(8,128)S(1)}, f32[192,128]{1,0:T(8,128)S(1)}, u32[]{:S(2)}, u32[]{:S(2)}) collective-permute-start(f32[192,128]{1,0:T(8,128)S(1)} %pad_maximum_fusion.4), channel_id=1, source_target_pairs={{0,4},{1,5},{2,6},{3,7},{4,0},{5,1},{6,2},{7,3},{8,9},{9,8},{10,11... | collective-permute-start | bytes 294920 | tf_op jit(solution)/shard_map/ppermute | solution.py:438

commit v6 on v5

--- a/solution.py
+++ b/solution.py
@@ -28,7 +28,7 @@
 BLOCK = HEADS * GROUP_ROWS
 STRIP = LONREL * LEVELS
 PADDED = 16
-TURNS = (0, 1)
+TURN = 0
 OFFSETS = 24
 
 EPSILON = 1e-05
@@ -70,20 +70,24 @@
     return copies
 
 
-def pack_kernel(features_ref, cotangent_ref, sent_ref, own_ref, band_ref, grad_ref, semaphores):
-    for copy in fetched([(features_ref, band_ref), (cotangent_ref, grad_ref)], semaphores):
-        copy.wait()
+def pack_half(band_ref, grad_ref, target_ref):
     for a in range(WLAT):
-        for x in range(WLON):
-            target_ref = own_ref if x < HALF else sent_ref
+        for x in range(HALF):
             band = band_ref[a, x]
             grad = grad_ref[a, x]
             tiles = (band[:, :128], jnp.concatenate([band[:, 128:], grad[:, 128:]], axis=1), grad[:, :128])
             for z in range(ZP):
                 c, i = divmod((z + 1) % ZP, WZ)
-                row = (x % HALF) * LEVELS + i * WLAT + a
+                row = x * LEVELS + i * WLAT + a
                 for tile in range(3):
                     target_ref[tile, c, row : row + 1, :] = tiles[tile][z : z + 1]
+
+
+def pack_kernel(features_ref, cotangent_ref, sent_ref, band_ref, grad_ref, semaphores):
+    pairs = [(features_ref.at[:, HALF:], band_ref), (cotangent_ref.at[:, HALF:], grad_ref)]
+    for copy in fetched(pairs, semaphores):
+        copy.wait()
+    pack_half(band_ref, grad_ref, sent_ref)
 
 
 def unpack_kernel(own_ref, returned_ref, out_ref):
@@ -157,13 +161,15 @@
 
 
 def prepare_kernel(
-    bias_hbm, own_ref, gain_hbm, shift_hbm, qkv_hbm, out_w_hbm,
+    bias_hbm, features_hbm, cotangent_hbm, gain_hbm, shift_hbm, qkv_hbm, out_w_hbm,
     table_ref, projected_ref, affine_ref, parts_ref,
-    turned_ref, strip_ref, bias_ref, qkv_ref, semaphores,
+    turned_ref, strip_ref, bias_ref, qkv_ref, band_ref, grad_ref, own_ref, semaphores,
 ):
     copies = fetched(
         [
             (bias_hbm, bias_ref),
+            (features_hbm.at[:, :HALF], band_ref),
+            (cotangent_hbm.at[:, :HALF], grad_ref),
             (gain_hbm, affine_ref.at[0:1]),
             (shift_hbm, affine_ref.at[1:2]),
             (qkv_hbm, qkv_ref),
@@ -174,11 +180,14 @@
     pairs, offsets = pair_order(), offset_order()
     for copy in copies:
         copy.wait()
+    pack_half(band_ref, grad_ref, own_ref)
     for part in range(3):
         parts_ref[part] = qkv_ref[:, part * D : (part + 1) * D]
     projections(own_ref, projected_ref, affine_ref[0:1], affine_ref[1:2], *(parts_ref[part] for part in range(4)))
-    strip_ref[...] = jnp.zeros_like(strip_ref)
-    rows = jnp.concatenate([bias_ref[h, :, c, :] for c in range(PW) for h in range(HEADS)], axis=0)
+    spare = jnp.zeros((OFFSETS - LONREL, PAIRS), jnp.float32)
+    rows = jnp.concatenate(
+        [part for c in range(PW) for h in range(HEADS) for part in (bias_ref[h, :, c, :], spare)], axis=0
+    )
     turned = None
     for part in parts_of(rows, 3):
         product = lax.dot_general(pairs, part, (((1,), (1,)), ((), ())), preferred_element_type=jnp.float32)
@@ -186,8 +195,8 @@
     turned_ref[...] = turned
     for block in range(PW * HEADS):
         for key in range(LEVELS):
-            strip_ref[block * PADDED : (block + 1) * PADDED, key * OFFSETS : key * OFFSETS + LONREL] = turned_ref[
-                key * PADDED : (key + 1) * PADDED, block * LONREL : (block + 1) * LONREL
+            strip_ref[block * PADDED : (block + 1) * PADDED, key * OFFSETS : (key + 1) * OFFSETS] = turned_ref[
+                key * PADDED : (key + 1) * PADDED, block * OFFSETS : (block + 1) * OFFSETS
             ]
     strips = moved(strip_ref[...], offsets, ((1,), (0,)), 3)
     row = lax.broadcasted_iota(jnp.int32, strips.shape, 0)
@@ -410,8 +419,9 @@
         for y in range(2):
             for lat in range(4):
                 chunk = total[48 * lat : 48 * (lat + 1), 96 * y : 96 * (y + 1)]
-                place = turned_by((y, block % 2, block // 2), TURNS[lat % 2])
-                weights_ref[(lat % 2, lat // 2) + place] = packed_chunk(chunk)
+                place = turned_by((y, block % 2, block // 2), TURN)
+                place = (lat // 2,) + place if lat % 2 == 0 else place + (lat // 2,)
+                weights_ref[(lat % 2,) + place] = packed_chunk(chunk)
 
 
 def bits_of(count):
@@ -461,22 +471,24 @@
 
 
 def summing_steps(lat_count, lon_count):
-    lat_bits, lon_bits = bits_of(lat_count), bits_of(lon_count)
-    lat_steps = [((bit, 0), (bit, 0)) for bit in lat_bits]
-    lon_steps = [((0, first), (0, second)) for first, second in zip(*(turned_by(lon_bits, turn) for turn in TURNS))]
-    return lat_steps, lon_steps, lon_steps[-1]
+    lat_bits, lon_bits = bits_of(lat_count), turned_by(bits_of(lon_count), TURN)
+    core, second, *others = [(bit, 0) for bit in lat_bits]
+    lons = [(0, bit) for bit in lon_bits]
+    first_order = [second] + others + lons
+    second_order = lons[:1] + others + lons[1:] + [second]
+    return (core, core), list(zip(first_order, second_order)), (lons[-1], lons[0])
 
 
 def chunks_by_step(weights, lat_count, lon_count):
     rows, columns = weights.shape[0] // lat_count, weights.shape[1] // lon_count
     lat_places, lon_places = len(bits_of(lat_count)), len(bits_of(lon_count))
     split = weights.reshape((2,) * lat_places + (rows,) + (2,) * lon_places + (columns,))
-    lat_dims = list(range(lat_places))[::-1]
-    lon_dims = list(range(lat_places + 1, lat_places + 1 + lon_places))[::-1]
+    core, second, *others = list(range(lat_places))[::-1]
+    lons = turned_by(list(range(lat_places + 1, lat_places + 1 + lon_places))[::-1], TURN)
     halves = []
-    for core, dims in enumerate(turned_by(lon_dims, turn) for turn in TURNS):
-        order = lat_dims + dims + [lat_places, lat_places + 1 + lon_places]
-        halves.append(split.transpose(order)[core])
+    for place, dims in enumerate(([second] + others + lons, lons[:1] + others + lons[1:] + [second])):
+        order = [core] + dims + [lat_places, lat_places + 1 + lon_places]
+        halves.append(split.transpose(order)[place])
     places = lat_places + lon_places
     split = jnp.stack(halves).reshape((2,) * places + (rows * columns,))
     words = -(-rows * columns // 1024) * 1024
@@ -494,14 +506,16 @@
     params = pltpu.CompilerParams(vmem_limit_bytes=48 << 20)
     half_shape = shape((3, PW, HALF_ROWS, 128), f32)
     block_shape = (WLAT, WLON, ZP, D)
-    sent, own = pl.pallas_call(
+    features, cotangent = hbm(features.transpose(1, 2, 0, 3), cotangent.transpose(1, 2, 0, 3))
+    half_block = pltpu.VMEM((WLAT, HALF, ZP, D), f32)
+    sent = pl.pallas_call(
         pack_kernel,
-        out_shape=(pltpu.VMEM(half_shape.shape, f32),) * 2,
+        out_shape=pltpu.VMEM(half_shape.shape, f32),
         in_specs=[pl.BlockSpec(memory_space=pltpu.HBM)] * 2,
-        out_specs=tuple(whole(2)),
-        scratch_shapes=[pltpu.VMEM(block_shape, f32), pltpu.VMEM(block_shape, f32), pltpu.SemaphoreType.DMA((2,))],
+        out_specs=whole(1)[0],
+        scratch_shapes=[half_block, half_block, pltpu.SemaphoreType.DMA((2,))],
         compiler_params=params,
-    )(*hbm(features.transpose(1, 2, 0, 3), cotangent.transpose(1, 2, 0, 3)))
+    )(features, cotangent)
     borrowed = lax.ppermute(sent, "lon", [(s, (s + 1) % lon_count) for s in range(lon_count)])
     projected_shape = (8, WIN, D)
     in_hbm = pl.BlockSpec(memory_space=pltpu.HBM)
@@ -516,17 +530,20 @@
             pltpu.VMEM((2, D), f32),
             pltpu.VMEM((4, D, D), f32),
         ),
-        in_specs=[in_hbm] + whole(1) + [in_hbm] * 4,
+        in_specs=[in_hbm] * 7,
         out_specs=tuple(whole(4)),
         scratch_shapes=[
-            pltpu.VMEM((LEVELS * PADDED, PW * HEADS * LONREL), f32),
+            pltpu.VMEM((LEVELS * PADDED, PW * HEADS * OFFSETS), f32),
             pltpu.VMEM((PW * HEADS * PADDED, LEVELS * OFFSETS), f32),
             pltpu.VMEM((HEADS, LONREL, PW, PAIRS), f32),
             pltpu.VMEM((D, 3 * D), f32),
-            pltpu.SemaphoreType.DMA((5,)),
+            half_block,
+            half_block,
+            pltpu.VMEM(half_shape.shape, f32),
+            pltpu.SemaphoreType.DMA((7,)),
         ],
         compiler_params=params,
-    )(bias, own, gain_row, shift_row, qkv_rows, out_rows)
+    )(bias, features, cotangent, gain_row, shift_row, qkv_rows, out_rows)
     grad_half = shape((3, HALF_ROWS, 128), f32)
     grad_own, grad_borrowed, weights, strips, norm = pl.pallas_call(
         functools.partial(block_kernel, factor, packed),
@@ -553,26 +570,26 @@
         scratch_shapes=[pltpu.VMEM((LEVELS * PADDED, PW * HEADS * OFFSETS), f32)],
         compiler_params=params,
     )(strips)
-    lat_steps, lon_steps, strip_step = summing_steps(lat_count, lon_count)
-    apart = lon_steps[0][0][1] if (TURNS[1] - TURNS[0]) % len(lon_steps) == 1 else lon_steps[0][1][1]
-    norm = jnp.where(lax.axis_index("lon") & apart == 0, norm, jnp.roll(norm, 4, 0))
+    core_step, steps, strip_step = summing_steps(lat_count, lon_count)
+    norm = jnp.where(lax.axis_index("lat") & 2 == 0, norm, jnp.roll(norm, 4, 0))
     strip_grad, given_strip = kept_and_given(strip_grad, strip_step)
     strip_grad = strip_grad + exchanged(given_strip, strip_step)
-    other_strip = None
-    for step in lat_steps + lon_steps:
+    shared = steps[-(len(bits_of(lon_count)) - 1) - 1 : -1]
+    for step in [core_step] + steps[:-1]:
         kept, given = kept_and_given(weights, step)
-        if step in lat_steps:
-            more, more_norm = exchange_all([given, norm], step)
-        else:
-            if step == lon_steps[0]:
-                given, grad_borrowed = lax.optimization_barrier((given, grad_borrowed))
+        if step in shared:
+            if step == shared[0]:
                 returned = lax.ppermute(grad_borrowed, "lon", [(s, (s - 1) % lon_count) for s in range(lon_count)])
             more, more_strip, more_norm = exchange_all([given, strip_grad, norm], step)
-            if step == lon_steps[-1]:
-                other_strip = more_strip
-            else:
-                strip_grad = strip_grad + more_strip
+            strip_grad = strip_grad + more_strip
+        else:
+            more, more_norm = exchange_all([given, norm], step)
         weights, norm = kept + more, norm + more_norm
+    other_strip = exchanged(strip_grad, strip_step)
+    kept, given = kept_and_given(weights, steps[-1])
+    more, more_norm = exchange_all([given, norm], steps[-1])
+    more, returned = lax.optimization_barrier((more, returned))
+    weights, norm = kept + more, norm + more_norm
     grad_features = pl.pallas_call(
         unpack_kernel,
         out_shape=shape(block_shape, f32),

time: 47.7 us -> 47 us (0.985)
  waiting for transfers between devices: 20.6 us -> 18.6 us
  starting transfers between devices: 11.1 us -> 12.3 us
    ppermute x6 -> x7, waiting for transfers between devices: 15.5 us -> 13.7 us  [exchanged(): return lax.ppermute(value, ('lat', 'lon'), partners(*step))]
    ppermute x6 -> x7, starting transfers between devices: 6.3 us -> 7.74 us  [exchanged(): return lax.ppermute(value, ('lat', 'lon'), partners(*step))]
  transfers between devices with their start and end apart: 8 -> 9, of which waited for: 6 -> 7; matrix products, arithmetic and copies ran while one was open for 0% -> 0% of each run, Pallas kernels for 12% -> 12%
where the time goes in v6:
time: 47 us; the launch traced here: 46.8 us
  waiting for transfers between devices  18.6 us (40%)
  Pallas kernels  14.6 us (31%)
  starting transfers between devices  12.3 us (26%)
  between operations  0.88 us (2%)
    ppermute x7, waiting for transfers between devices, exchanged(): return lax.ppermute(value, ('lat', 'lon'), partners(*step))  13.7 us
    ppermute x7, starting transfers between devices, exchanged(): return lax.ppermute(value, ('lat', 'lon'), partners(*step))  7.74 us
    pallas_call x1, Pallas kernels, shards(): pl.pallas_call(functools.partial(block_kernel, factor, packed), out_shape...  6.81 us
    ppermute x1, waiting for transfers between devices, shards(): lax.ppermute(sent, 'lon', [(s, (s + 1) % lon_count) for s in range(lon_co...  4.88 us
    pallas_call x1, Pallas kernels, shards(): pl.pallas_call(prepare_kernel, out_shape=(pltpu.VMEM((PW, GROUP_ROWS * HE...  3.58 us
    ppermute x1, starting transfers between devices, shards(): lax.ppermute(sent, 'lon', [(s, (s + 1) % lon_count) for s in range(lon_co...  3.02 us
    ppermute x1, starting transfers between devices, shards(): lax.ppermute(grad_borrowed, 'lon', [(s, (s - 1) % lon_count) for s in ran...  1.58 us
    pallas_call x1, Pallas kernels, shards(): pl.pallas_call(turn_kernel, out_shape=rows_shape, in_specs=whole(1), out_...  1.21 us
  transfers between devices with their start and end apart: 9, of which 7 were waited for; matrix products, arithmetic and copies ran while one was open for 0% of the time, Pallas kernels for 12%

profile of v6, /device:TPU:0, one launch (start us, length us, event | category | flops | bytes accessed | tf_op | source)
XLA Modules:
  0.0 46.8 jit_solution(8874437042111832811)
XLA Ops:
  0.6 1.1 %shard_map.102 = f32[3,2,72,128]{3,2,1,0:T(8,128)S(1)} custom-call(f32[6,12,4,192]{3,2,1,0:T(4,128)} %bitcast.38, f32[6,12,4,192]{3,2,1,0:T(4,128)} %bitcast.40), custom_call_target="tpu_custom_call" | custom-call | tf_op jit(solution)/shard_map/pallas_call | solution.py:511
  1.8 3.0 %collective-permute-start = (f32[3,2,72,128]{3,2,1,0:T(8,128)S(1)}, f32[3,2,72,128]{3,2,1,0:T(8,128)S(1)}, u32[]{:S(2)}, u32[]{:S(2)}) collective-permute-start(f32[3,2,72,128]{3,2,1,0:T(8,128)S(1)} %shard_map.102), channel_id=1, source_target_pairs={{0,1},{1,2},{2,3},{3,4},{4,5},{5,6},{6,7},{7,0},{8,9},{9,10},{10,1... | collective-permute-start | bytes 663560 | tf_op jit(solution)/shard_map/ppermute | solution.py:519
  4.8 3.6 %shard_map.103 = (f32[2,288,384]{2,1,0:T(8,128)S(1)}, f32[8,144,192]{2,1,0:T(8,128)S(1)}, f32[2,192]{1,0:T(2,128)S(1)}, f32[4,192,192]{2,1,0:T(8,128)S(1)}) custom-call(f32[6,23,2,144]{3,2,1,0:T(2,128)} %bitcast.47, f32[6,12,4,192]{3,2,1,0:T(4,128)} %bitcast.39, f32[6,12,4,192]{3,2,1,0:T(4,128)} %bitcast.41, f32[1,192]{1,0:T(1,128)} %bitcast.50, ...), custom_call_target="tpu_custom_call" | custom-call | tf_op jit(solution)/shard_map/pallas_call | solution.py:525
  8.4 4.9 %collective-permute-done.borrowed_ref = f32[3,2,72,128]{3,2,1,0:T(8,128)S(1)} collective-permute-done((f32[3,2,72,128]{3,2,1,0:T(8,128)S(1)}, f32[3,2,72,128]{3,2,1,0:T(8,128)S(1)}, u32[]{:S(2)}, u32[]{:S(2)}) %collective-permute-start) | collective-permute-done | bytes 221216 | tf_op jit(solution)/shard_map/ppermute | solution.py:519
  13.2 6.8 %shard_map.104 = (f32[3,72,128]{2,1,0:T(8,128)S(1)}, f32[3,72,128]{2,1,0:T(8,128)S(1)}, f32[2,2,2,2,2,40,128]{6,5,4,3,2,1,0:T(8,128)S(1)}, f32[192,288]{1,0:T(8,128)S(1)}, f32[8,128]{1,0:T(8,128)S(1)}) custom-call(f32[3,2,72,128]{3,2,1,0:T(8,128)S(1)} %collective-permute-done.borrowed_ref, f32[8,144,192]{2,1,0:T(8,128)S(1)} %get-tuple-element.18.projected_ref, ...), custom_call_target="tpu_custom_call" | custom-call | tf_op jit(solution)/shard_map/pallas_call | solution.py:548
  20.1 0.1 collective-permute-start.1
  20.3 1.2 %shard_map.105 = f32[2,144,128]{2,1,0:T(8,128)S(1)} custom-call(f32[192,288]{1,0:T(8,128)S(1)} %get-tuple-element.25.strip_ref), custom_call_target="tpu_custom_call" | custom-call | tf_op jit(solution)/shard_map/pallas_call | solution.py:565
  21.5 0.7 %collective-permute-start.3 = (f32[144,128]{1,0:T(8,128)S(1)}, f32[144,128]{1,0:T(8,128)S(1)}, u32[]{:S(2)}, u32[]{:S(2)}) collective-permute-start(f32[144,128]{1,0:T(8,128)S(1)} %dynamic-slice_bitcast_fusion), channel_id=1, source_target_pairs={{0,4},{1,5},{2,6},{3,7},{4,0},{5,1},{6,2},{7,3},{8,9},{9,8},{10,11... | collective-permute-start | bytes 221192 | tf_op jit(solution)/shard_map/ppermute | solution.py:448
  22.2 0.0 collective-permute-done.1
  22.4 1.6 %collective-permute-start.2 = (f32[328,128]{1,0:T(8,128)S(1)}, f32[328,128]{1,0:T(8,128)S(1)}, u32[]{:S(2)}, u32[]{:S(2)}) collective-permute-start(f32[328,128]{1,0:T(8,128)S(1)} %pad_maximum_fusion.1), channel_id=1, source_target_pairs={{0,16},{1,17},{2,18},{3,19},{4,20},{5,21},{6,22},{7,23},{8,9},{9,8... | collective-permute-start | bytes 503816 | tf_op jit(solution)/shard_map/ppermute | solution.py:448
  23.9 2.9 %collective-permute-done.3 = f32[144,128]{1,0:T(8,128)S(1)} collective-permute-done((f32[144,128]{1,0:T(8,128)S(1)}, f32[144,128]{1,0:T(8,128)S(1)}, u32[]{:S(2)}, u32[]{:S(2)}) %collective-permute-start.3) | collective-permute-done | bytes 73760 | tf_op jit(solution)/shard_map/ppermute | solution.py:448
  26.8 1.0 %collective-permute-done.2 = f32[328,128]{1,0:T(8,128)S(1)} collective-permute-done((f32[328,128]{1,0:T(8,128)S(1)}, f32[328,128]{1,0:T(8,128)S(1)}, u32[]{:S(2)}, u32[]{:S(2)}) %collective-permute-start.2) | collective-permute-done | bytes 167968 | tf_op jit(solution)/shard_map/ppermute | solution.py:448
  27.9 0.7 %collective-permute-start.4 = (f32[312,128]{1,0:T(8,128)S(1)}, f32[312,128]{1,0:T(8,128)S(1)}, u32[]{:S(2)}, u32[]{:S(2)}) collective-permute-start(f32[312,128]{1,0:T(8,128)S(1)} %pad_maximum_fusion.2), channel_id=1, source_target_pairs={{0,1},{1,0},{2,3},{3,2},{4,5},{5,4},{6,7},{7,6},{8,10},{9,11},{10,... | collective-permute-start | bytes 479240 | tf_op jit(solution)/shard_map/ppermute | solution.py:448
  28.6 4.7 %collective-permute-done.4 = f32[312,128]{1,0:T(8,128)S(1)} collective-permute-done((f32[312,128]{1,0:T(8,128)S(1)}, f32[312,128]{1,0:T(8,128)S(1)}, u32[]{:S(2)}, u32[]{:S(2)}) %collective-permute-start.4) | collective-permute-done | bytes 159776 | tf_op jit(solution)/shard_map/ppermute | solution.py:448
  33.3 1.6 %collective-permute-start.5 = (f32[232,128]{1,0:T(8,128)S(1)}, f32[232,128]{1,0:T(8,128)S(1)}, u32[]{:S(2)}, u32[]{:S(2)}) collective-permute-start(f32[232,128]{1,0:T(8,128)S(1)} %pad_maximum_fusion.3), channel_id=1, source_target_pairs={{0,2},{1,3},{2,0},{3,1},{4,6},{5,7},{6,4},{7,5},{8,12},{9,13},{10,... | collective-permute-start | bytes 356360 | tf_op jit(solution)/shard_map/ppermute | solution.py:448
  35.0 1.6 %collective-permute-start.7 = (f32[3,72,128]{2,1,0:T(8,128)S(1)}, f32[3,72,128]{2,1,0:T(8,128)S(1)}, u32[]{:S(2)}, u32[]{:S(2)}) collective-permute-start(f32[3,72,128]{2,1,0:T(8,128)S(1)} %get-tuple-element.26), channel_id=1, source_target_pairs={{0,7},{1,0},{2,1},{3,2},{4,3},{5,4},{6,5},{7,6},{8,15},{9,8},{10,9... | collective-permute-start | bytes 331784 | tf_op jit(solution)/shard_map/ppermute | solution.py:582
  36.6 2.5 %collective-permute-done.5 = f32[232,128]{1,0:T(8,128)S(1)} collective-permute-done((f32[232,128]{1,0:T(8,128)S(1)}, f32[232,128]{1,0:T(8,128)S(1)}, u32[]{:S(2)}, u32[]{:S(2)}) %collective-permute-start.5) | collective-permute-done | bytes 118816 | tf_op jit(solution)/shard_map/ppermute | solution.py:448
  39.1 1.5 %collective-permute-start.6 = (f32[48,128]{1,0:T(8,128)S(1)}, f32[48,128]{1,0:T(8,128)S(1)}, u32[]{:S(2)}, u32[]{:S(2)}) collective-permute-start(f32[48,128]{1,0:T(8,128)S(1)} %pad_maximum_fusion.4), channel_id=1, source_target_pairs={{0,4},{1,5},{2,6},{3,7},{4,0},{5,1},{6,2},{7,3},{8,24},{9,25},{10,... | collective-permute-start | bytes 73736 | tf_op jit(solution)/shard_map/ppermute | solution.py:448
  40.6 1.6 %collective-permute-start.8 = (f32[144,128]{1,0:T(8,128)S(1)}, f32[144,128]{1,0:T(8,128)S(1)}, u32[]{:S(2)}, u32[]{:S(2)}) collective-permute-start(f32[144,128]{1,0:T(8,128)S(1)} %slice_add_fusion.mine_ref), channel_id=1, source_target_pairs={{0,4},{1,5},{2,6},{3,7},{4,0},{5,1},{6,2},{7,3},{8,9},{9,8},{10,11... | collective-permute-start | bytes 221192 | tf_op jit(solution)/shard_map/ppermute | solution.py:448
  42.2 1.7 %collective-permute-done.6 = f32[48,128]{1,0:T(8,128)S(1)} collective-permute-done((f32[48,128]{1,0:T(8,128)S(1)}, f32[48,128]{1,0:T(8,128)S(1)}, u32[]{:S(2)}, u32[]{:S(2)}) %collective-permute-start.6) | collective-permute-done | bytes 24608 | tf_op jit(solution)/shard_map/ppermute | solution.py:448
  43.9 0.0 collective-permute-done.7.returned_ref
  44.0 1.0 %shard_map.106 = f32[6,12,4,192]{3,2,1,0:T(4,128)} custom-call(f32[3,72,128]{2,1,0:T(8,128)S(1)} %get-tuple-element.22.own_ref, f32[3,72,128]{2,1,0:T(8,128)S(1)} %collective-permute-done.7.returned_ref), custom_call_target="tpu_custom_call" | custom-call | tf_op jit(solution)/shard_map/pallas_call | solution.py:593
  45.0 1.0 %collective-permute-done.8.other_ref = f32[144,128]{1,0:T(8,128)S(1)} collective-permute-done((f32[144,128]{1,0:T(8,128)S(1)}, f32[144,128]{1,0:T(8,128)S(1)}, u32[]{:S(2)}, u32[]{:S(2)}) %collective-permute-start.8) | collective-permute-done | bytes 73760 | tf_op jit(solution)/shard_map/ppermute | solution.py:448
  46.0 0.9 %shard_map.107 = (f32[6,23,2,144]{3,2,1,0:T(2,128)}, f32[48,96]{1,0:T(8,128)}, f32[2,192]{1,0:T(2,128)}) custom-call(s32[1]{0:T(128)} %bitcast.22.parity_ref, f32[144,128]{1,0:T(8,128)S(1)} %slice_add_fusion.mine_ref, f32[144,128]{1,0:T(8,128)S(1)} %collective-permute-done.8.other_ref, f32[40,128]{1,0:T(8,128)S(1)} %bitcast_add_fusion.5.weights_ref, ...), custom_call_target="tpu_custom_call" | custom-call | tf_op jit(solution)/shard_map/pallas_call | solution.py:602
  (31 shorter events, 0.4 us)
Async XLA Ops:
  1.8 11.5 %collective-permute-start = (f32[3,2,72,128]{3,2,1,0:T(8,128)S(1)}, f32[3,2,72,128]{3,2,1,0:T(8,128)S(1)}, u32[]{:S(2)}, u32[]{:S(2)}) collective-permute-start(f32[3,2,72,128]{3,2,1,0:T(8,128)S(1)} %shard_map.102), channel_id=1, source_target_pairs={{0,1},{1,2},{2,3},{3,4},{4,5},{5,6},{6,7},{7,0},{8,9},{9,10},{10,1... | collective-permute-start | bytes 663560 | tf_op jit(solution)/shard_map/ppermute | solution.py:519
  20.1 2.1 %collective-permute-start.1 = (f32[648,128]{1,0:T(8,128)S(1)}, f32[648,128]{1,0:T(8,128)S(1)}, u32[]{:S(2)}, u32[]{:S(2)}) collective-permute-start(f32[648,128]{1,0:T(8,128)S(1)} %pad_maximum_fusion), channel_id=1, source_target_pairs={{0,8},{1,9},{2,10},{3,11},{4,12},{5,13},{6,14},{7,15},{8,0},{9,1},... | collective-permute-start | bytes 995336 | tf_op jit(solution)/shard_map/ppermute | solution.py:448
  21.5 5.3 %collective-permute-start.3 = (f32[144,128]{1,0:T(8,128)S(1)}, f32[144,128]{1,0:T(8,128)S(1)}, u32[]{:S(2)}, u32[]{:S(2)}) collective-permute-start(f32[144,128]{1,0:T(8,128)S(1)} %dynamic-slice_bitcast_fusion), channel_id=1, source_target_pairs={{0,4},{1,5},{2,6},{3,7},{4,0},{5,1},{6,2},{7,3},{8,9},{9,8},{10,11... | collective-permute-start | bytes 221192 | tf_op jit(solution)/shard_map/ppermute | solution.py:448
  22.4 5.4 %collective-permute-start.2 = (f32[328,128]{1,0:T(8,128)S(1)}, f32[328,128]{1,0:T(8,128)S(1)}, u32[]{:S(2)}, u32[]{:S(2)}) collective-permute-start(f32[328,128]{1,0:T(8,128)S(1)} %pad_maximum_fusion.1), channel_id=1, source_target_pairs={{0,16},{1,17},{2,18},{3,19},{4,20},{5,21},{6,22},{7,23},{8,9},{9,8... | collective-permute-start | bytes 503816 | tf_op jit(solution)/shard_map/ppermute | solution.py:448
  27.9 5.3 %collective-permute-start.4 = (f32[312,128]{1,0:T(8,128)S(1)}, f32[312,128]{1,0:T(8,128)S(1)}, u32[]{:S(2)}, u32[]{:S(2)}) collective-permute-start(f32[312,128]{1,0:T(8,128)S(1)} %pad_maximum_fusion.2), channel_id=1, source_target_pairs={{0,1},{1,0},{2,3},{3,2},{4,5},{5,4},{6,7},{7,6},{8,10},{9,11},{10,... | collective-permute-start | bytes 479240 | tf_op jit(solution)/shard_map/ppermute | solution.py:448
  33.3 5.7 %collective-permute-start.5 = (f32[232,128]{1,0:T(8,128)S(1)}, f32[232,128]{1,0:T(8,128)S(1)}, u32[]{:S(2)}, u32[]{:S(2)}) collective-permute-start(f32[232,128]{1,0:T(8,128)S(1)} %pad_maximum_fusion.3), channel_id=1, source_target_pairs={{0,2},{1,3},{2,0},{3,1},{4,6},{5,7},{6,4},{7,5},{8,12},{9,13},{10,... | collective-permute-start | bytes 356360 | tf_op jit(solution)/shard_map/ppermute | solution.py:448
  35.0 9.0 %collective-permute-start.7 = (f32[3,72,128]{2,1,0:T(8,128)S(1)}, f32[3,72,128]{2,1,0:T(8,128)S(1)}, u32[]{:S(2)}, u32[]{:S(2)}) collective-permute-start(f32[3,72,128]{2,1,0:T(8,128)S(1)} %get-tuple-element.26), channel_id=1, source_target_pairs={{0,7},{1,0},{2,1},{3,2},{4,3},{5,4},{6,5},{7,6},{8,15},{9,8},{10,9... | collective-permute-start | bytes 331784 | tf_op jit(solution)/shard_map/ppermute | solution.py:582
  39.1 4.8 %collective-permute-start.6 = (f32[48,128]{1,0:T(8,128)S(1)}, f32[48,128]{1,0:T(8,128)S(1)}, u32[]{:S(2)}, u32[]{:S(2)}) collective-permute-start(f32[48,128]{1,0:T(8,128)S(1)} %pad_maximum_fusion.4), channel_id=1, source_target_pairs={{0,4},{1,5},{2,6},{3,7},{4,0},{5,1},{6,2},{7,3},{8,24},{9,25},{10,... | collective-permute-start | bytes 73736 | tf_op jit(solution)/shard_map/ppermute | solution.py:448
  40.6 5.3 %collective-permute-start.8 = (f32[144,128]{1,0:T(8,128)S(1)}, f32[144,128]{1,0:T(8,128)S(1)}, u32[]{:S(2)}, u32[]{:S(2)}) collective-permute-start(f32[144,128]{1,0:T(8,128)S(1)} %slice_add_fusion.mine_ref), channel_id=1, source_target_pairs={{0,4},{1,5},{2,6},{3,7},{4,0},{5,1},{6,2},{7,3},{8,9},{9,8},{10,11... | collective-permute-start | bytes 221192 | tf_op jit(solution)/shard_map/ppermute | solution.py:448

commit v7 on v6

--- a/solution.py
+++ b/solution.py
@@ -162,7 +162,7 @@
 
 def prepare_kernel(
     bias_hbm, features_hbm, cotangent_hbm, gain_hbm, shift_hbm, qkv_hbm, out_w_hbm,
-    table_ref, projected_ref, affine_ref, parts_ref,
+    table_ref, projected_ref, affine_ref, parts_ref, pairs_ref, offsets_ref,
     turned_ref, strip_ref, bias_ref, qkv_ref, band_ref, grad_ref, own_ref, semaphores,
 ):
     copies = fetched(
@@ -178,6 +178,7 @@
         semaphores,
     )
     pairs, offsets = pair_order(), offset_order()
+    pairs_ref[...], offsets_ref[...] = pairs, offsets
     for copy in copies:
         copy.wait()
     pack_half(band_ref, grad_ref, own_ref)
@@ -212,8 +213,8 @@
                 table_ref[c, first : first + LEVELS, g * LEVELS : g * LEVELS + STRIP] = strip
 
 
-def turn_kernel(strip_ref, rows_ref, turned_ref):
-    pairs, offsets = pair_order(), offset_order()
+def turn_kernel(strip_ref, pairs_ref, offsets_ref, rows_ref, turned_ref):
+    pairs, offsets = pairs_ref[...], offsets_ref[...]
     by_level = moved(strip_ref[...], offsets, ((1,), (1,)), 2)
     for block in range(PW * HEADS):
         for key in range(LEVELS):
@@ -261,7 +262,10 @@
     return jnp.concatenate([packed[:, :96], last], axis=0)
 
 
-ORDER = "S0 D0 S1 P0 D1 M0 V0 P1 G0 M1 V1 G1 Q0 K0 T0 Q1 K1 T1".split()
+ORDER = (
+    "S0", "D0", "S1", "P0", "D1", "M0", "V0", "P1", "G0",
+    "M1", "V1", "G1", "Q0", "K0", "T0", "Q1", "K1", "T1",
+)
 
 
 def halves_of(value):
@@ -522,16 +526,18 @@
     bias, gain_row, shift_row, qkv_rows, out_rows = hbm(
         bias_table[0].transpose(1, 2, 0, 3), norm_gain[None], norm_shift[None], qkv_weight, out_weight
     )
-    table, projected, affine, parts = pl.pallas_call(
+    table, projected, affine, parts, pairs, offsets = pl.pallas_call(
         prepare_kernel,
         out_shape=(
             pltpu.VMEM((PW, GROUP_ROWS * HEADS, 384), f32),
             pltpu.VMEM(projected_shape, f32),
             pltpu.VMEM((2, D), f32),
             pltpu.VMEM((4, D, D), f32),
+            pltpu.VMEM((LEVELS * PADDED, PAIRS), jnp.bfloat16),
+            pltpu.VMEM((LEVELS * OFFSETS, LEVELS * OFFSETS), jnp.bfloat16),
         ),
         in_specs=[in_hbm] * 7,
-        out_specs=tuple(whole(4)),
+        out_specs=tuple(whole(6)),
         scratch_shapes=[
             pltpu.VMEM((LEVELS * PADDED, PW * HEADS * OFFSETS), f32),
             pltpu.VMEM((PW * HEADS * PADDED, LEVELS * OFFSETS), f32),
@@ -565,11 +571,11 @@
     strip_grad = pl.pallas_call(
         turn_kernel,
         out_shape=rows_shape,
-        in_specs=whole(1),
+        in_specs=whole(3),
         out_specs=whole(1)[0],
         scratch_shapes=[pltpu.VMEM((LEVELS * PADDED, PW * HEADS * OFFSETS), f32)],
         compiler_params=params,
-    )(strips)
+    )(strips, pairs, offsets)
     core_step, steps, strip_step = summing_steps(lat_count, lon_count)
     norm = jnp.where(lax.axis_index("lat") & 2 == 0, norm, jnp.roll(norm, 4, 0))
     strip_grad, given_strip = kept_and_given(strip_grad, strip_step)

time: 47 us -> 46.9 us (level)
  no operation moved by 1% of the time
where the time goes in v7:
time: 46.9 us; the launch traced here: 46.7 us
  waiting for transfers between devices  18.6 us (40%)
  Pallas kernels  14.5 us (31%)
  starting transfers between devices  12.4 us (26%)
  between operations  0.88 us (2%)
    ppermute x7, waiting for transfers between devices, exchanged(): return lax.ppermute(value, ('lat', 'lon'), partners(*step))  13.7 us
    ppermute x7, starting transfers between devices, exchanged(): return lax.ppermute(value, ('lat', 'lon'), partners(*step))  7.75 us
    pallas_call x1, Pallas kernels, shards(): pl.pallas_call(functools.partial(block_kernel, factor, packed), out_shape...  6.81 us
    ppermute x1, waiting for transfers between devices, shards(): lax.ppermute(sent, 'lon', [(s, (s + 1) % lon_count) for s in range(lon_co...  4.88 us
    pallas_call x1, Pallas kernels, shards(): pl.pallas_call(prepare_kernel, out_shape=(pltpu.VMEM((PW, GROUP_ROWS * HE...  3.58 us
    ppermute x1, starting transfers between devices, shards(): lax.ppermute(sent, 'lon', [(s, (s + 1) % lon_count) for s in range(lon_co...  3.02 us
    ppermute x1, starting transfers between devices, shards(): lax.ppermute(grad_borrowed, 'lon', [(s, (s - 1) % lon_count) for s in ran...  1.58 us
    pallas_call x1, Pallas kernels, shards(): pl.pallas_call(turn_kernel, out_shape=rows_shape, in_specs=whole(3), out_...  1.12 us
  transfers between devices with their start and end apart: 9, of which 7 were waited for; matrix products, arithmetic and copies ran while one was open for 0% of the time, Pallas kernels for 12%

profile of v7, /device:TPU:0, one launch (start us, length us, event | category | flops | bytes accessed | tf_op | source)
XLA Modules:
  0.0 46.7 jit_solution(5127360749145520387)
XLA Ops:
  0.6 1.1 %shard_map.102 = f32[3,2,72,128]{3,2,1,0:T(8,128)S(1)} custom-call(f32[6,12,4,192]{3,2,1,0:T(4,128)} %bitcast.38, f32[6,12,4,192]{3,2,1,0:T(4,128)} %bitcast.40), custom_call_target="tpu_custom_call" | custom-call | tf_op jit(solution)/shard_map/pallas_call | solution.py:515
  1.8 3.0 %collective-permute-start = (f32[3,2,72,128]{3,2,1,0:T(8,128)S(1)}, f32[3,2,72,128]{3,2,1,0:T(8,128)S(1)}, u32[]{:S(2)}, u32[]{:S(2)}) collective-permute-start(f32[3,2,72,128]{3,2,1,0:T(8,128)S(1)} %shard_map.102), channel_id=1, source_target_pairs={{0,1},{1,2},{2,3},{3,4},{4,5},{5,6},{6,7},{7,0},{8,9},{9,10},{10,1... | collective-permute-start | bytes 663560 | tf_op jit(solution)/shard_map/ppermute | solution.py:523
  4.8 3.6 %shard_map.103 = (f32[2,288,384]{2,1,0:T(8,128)S(1)}, f32[8,144,192]{2,1,0:T(8,128)S(1)}, f32[2,192]{1,0:T(2,128)S(1)}, f32[4,192,192]{2,1,0:T(8,128)S(1)}, bf16...) custom-call(f32[6,23,2,144]{3,2,1,0:T(2,128)} %bitcast.47, f32[6,12,4,192]{3,2,1,0:T(4,128)} %bitcast.39, ...), custom_call_target="tpu_custom_call" | custom-call | tf_op jit(solution)/shard_map/pallas_call | solution.py:529
  8.4 4.9 %collective-permute-done.borrowed_ref = f32[3,2,72,128]{3,2,1,0:T(8,128)S(1)} collective-permute-done((f32[3,2,72,128]{3,2,1,0:T(8,128)S(1)}, f32[3,2,72,128]{3,2,1,0:T(8,128)S(1)}, u32[]{:S(2)}, u32[]{:S(2)}) %collective-permute-start) | collective-permute-done | bytes 221216 | tf_op jit(solution)/shard_map/ppermute | solution.py:523
  13.2 6.8 %shard_map.104 = (f32[3,72,128]{2,1,0:T(8,128)S(1)}, f32[3,72,128]{2,1,0:T(8,128)S(1)}, f32[2,2,2,2,2,40,128]{6,5,4,3,2,1,0:T(8,128)S(1)}, f32[192,288]{1,0:T(8,128)S(1)}, f32[8,128]{1,0:T(8,128)S(1)}) custom-call(f32[3,2,72,128]{3,2,1,0:T(8,128)S(1)} %collective-permute-done.borrowed_ref, f32[8,144,192]{2,1,0:T(8,128)S(1)} %get-tuple-element.20.projected_ref, ...), custom_call_target="tpu_custom_call" | custom-call | tf_op jit(solution)/shard_map/pallas_call | solution.py:554
  20.1 0.1 collective-permute-start.1
  20.3 1.1 %shard_map.105 = f32[2,144,128]{2,1,0:T(8,128)S(1)} custom-call(f32[192,288]{1,0:T(8,128)S(1)} %get-tuple-element.27.strip_ref, bf16[192,144]{1,0:T(8,128)(2,1)S(1)} %get-tuple-element.28.pairs_ref, bf16[288,288]{1,0:T(8,128)(2,1)S(1)} %get-tuple-element.29.offsets_ref), custom_call_target="tpu_custom_call" | custom-call | tf_op jit(solution)/shard_map/pallas_call | solution.py:571
  21.4 0.7 %collective-permute-start.3 = (f32[144,128]{1,0:T(8,128)S(1)}, f32[144,128]{1,0:T(8,128)S(1)}, u32[]{:S(2)}, u32[]{:S(2)}) collective-permute-start(f32[144,128]{1,0:T(8,128)S(1)} %dynamic-slice_bitcast_fusion), channel_id=1, source_target_pairs={{0,4},{1,5},{2,6},{3,7},{4,0},{5,1},{6,2},{7,3},{8,9},{9,8},{10,11... | collective-permute-start | bytes 221192 | tf_op jit(solution)/shard_map/ppermute | solution.py:452
  22.1 0.0 collective-permute-done.1
  22.3 1.6 %collective-permute-start.2 = (f32[328,128]{1,0:T(8,128)S(1)}, f32[328,128]{1,0:T(8,128)S(1)}, u32[]{:S(2)}, u32[]{:S(2)}) collective-permute-start(f32[328,128]{1,0:T(8,128)S(1)} %pad_maximum_fusion.1), channel_id=1, source_target_pairs={{0,16},{1,17},{2,18},{3,19},{4,20},{5,21},{6,22},{7,23},{8,9},{9,8... | collective-permute-start | bytes 503816 | tf_op jit(solution)/shard_map/ppermute | solution.py:452
  23.8 2.9 %collective-permute-done.3 = f32[144,128]{1,0:T(8,128)S(1)} collective-permute-done((f32[144,128]{1,0:T(8,128)S(1)}, f32[144,128]{1,0:T(8,128)S(1)}, u32[]{:S(2)}, u32[]{:S(2)}) %collective-permute-start.3) | collective-permute-done | bytes 73760 | tf_op jit(solution)/shard_map/ppermute | solution.py:452
  26.7 1.0 %collective-permute-done.2 = f32[328,128]{1,0:T(8,128)S(1)} collective-permute-done((f32[328,128]{1,0:T(8,128)S(1)}, f32[328,128]{1,0:T(8,128)S(1)}, u32[]{:S(2)}, u32[]{:S(2)}) %collective-permute-start.2) | collective-permute-done | bytes 167968 | tf_op jit(solution)/shard_map/ppermute | solution.py:452
  27.8 0.7 %collective-permute-start.4 = (f32[312,128]{1,0:T(8,128)S(1)}, f32[312,128]{1,0:T(8,128)S(1)}, u32[]{:S(2)}, u32[]{:S(2)}) collective-permute-start(f32[312,128]{1,0:T(8,128)S(1)} %pad_maximum_fusion.2), channel_id=1, source_target_pairs={{0,1},{1,0},{2,3},{3,2},{4,5},{5,4},{6,7},{7,6},{8,10},{9,11},{10,... | collective-permute-start | bytes 479240 | tf_op jit(solution)/shard_map/ppermute | solution.py:452
  28.5 4.6 %collective-permute-done.4 = f32[312,128]{1,0:T(8,128)S(1)} collective-permute-done((f32[312,128]{1,0:T(8,128)S(1)}, f32[312,128]{1,0:T(8,128)S(1)}, u32[]{:S(2)}, u32[]{:S(2)}) %collective-permute-start.4) | collective-permute-done | bytes 159776 | tf_op jit(solution)/shard_map/ppermute | solution.py:452
  33.3 1.6 %collective-permute-start.5 = (f32[232,128]{1,0:T(8,128)S(1)}, f32[232,128]{1,0:T(8,128)S(1)}, u32[]{:S(2)}, u32[]{:S(2)}) collective-permute-start(f32[232,128]{1,0:T(8,128)S(1)} %pad_maximum_fusion.3), channel_id=1, source_target_pairs={{0,2},{1,3},{2,0},{3,1},{4,6},{5,7},{6,4},{7,5},{8,12},{9,13},{10,... | collective-permute-start | bytes 356360 | tf_op jit(solution)/shard_map/ppermute | solution.py:452
  34.9 1.6 %collective-permute-start.7 = (f32[3,72,128]{2,1,0:T(8,128)S(1)}, f32[3,72,128]{2,1,0:T(8,128)S(1)}, u32[]{:S(2)}, u32[]{:S(2)}) collective-permute-start(f32[3,72,128]{2,1,0:T(8,128)S(1)} %get-tuple-element.30), channel_id=1, source_target_pairs={{0,7},{1,0},{2,1},{3,2},{4,3},{5,4},{6,5},{7,6},{8,15},{9,8},{10,9... | collective-permute-start | bytes 331784 | tf_op jit(solution)/shard_map/ppermute | solution.py:588
  36.5 2.5 %collective-permute-done.5 = f32[232,128]{1,0:T(8,128)S(1)} collective-permute-done((f32[232,128]{1,0:T(8,128)S(1)}, f32[232,128]{1,0:T(8,128)S(1)}, u32[]{:S(2)}, u32[]{:S(2)}) %collective-permute-start.5) | collective-permute-done | bytes 118816 | tf_op jit(solution)/shard_map/ppermute | solution.py:452
  39.0 1.5 %collective-permute-start.6 = (f32[48,128]{1,0:T(8,128)S(1)}, f32[48,128]{1,0:T(8,128)S(1)}, u32[]{:S(2)}, u32[]{:S(2)}) collective-permute-start(f32[48,128]{1,0:T(8,128)S(1)} %pad_maximum_fusion.4), channel_id=1, source_target_pairs={{0,4},{1,5},{2,6},{3,7},{4,0},{5,1},{6,2},{7,3},{8,24},{9,25},{10,... | collective-permute-start | bytes 73736 | tf_op jit(solution)/shard_map/ppermute | solution.py:452
  40.5 1.6 %collective-permute-start.8 = (f32[144,128]{1,0:T(8,128)S(1)}, f32[144,128]{1,0:T(8,128)S(1)}, u32[]{:S(2)}, u32[]{:S(2)}) collective-permute-start(f32[144,128]{1,0:T(8,128)S(1)} %slice_add_fusion.mine_ref), channel_id=1, source_target_pairs={{0,4},{1,5},{2,6},{3,7},{4,0},{5,1},{6,2},{7,3},{8,9},{9,8},{10,11... | collective-permute-start | bytes 221192 | tf_op jit(solution)/shard_map/ppermute | solution.py:452
  42.1 1.7 %collective-permute-done.6 = f32[48,128]{1,0:T(8,128)S(1)} collective-permute-done((f32[48,128]{1,0:T(8,128)S(1)}, f32[48,128]{1,0:T(8,128)S(1)}, u32[]{:S(2)}, u32[]{:S(2)}) %collective-permute-start.6) | collective-permute-done | bytes 24608 | tf_op jit(solution)/shard_map/ppermute | solution.py:452
  43.8 0.0 collective-permute-done.7.returned_ref
  43.9 1.0 %shard_map.106 = f32[6,12,4,192]{3,2,1,0:T(4,128)} custom-call(f32[3,72,128]{2,1,0:T(8,128)S(1)} %get-tuple-element.24.own_ref, f32[3,72,128]{2,1,0:T(8,128)S(1)} %collective-permute-done.7.returned_ref), custom_call_target="tpu_custom_call" | custom-call | tf_op jit(solution)/shard_map/pallas_call | solution.py:599
  44.9 1.0 %collective-permute-done.8.other_ref = f32[144,128]{1,0:T(8,128)S(1)} collective-permute-done((f32[144,128]{1,0:T(8,128)S(1)}, f32[144,128]{1,0:T(8,128)S(1)}, u32[]{:S(2)}, u32[]{:S(2)}) %collective-permute-start.8) | collective-permute-done | bytes 73760 | tf_op jit(solution)/shard_map/ppermute | solution.py:452
  45.9 0.9 %shard_map.107 = (f32[6,23,2,144]{3,2,1,0:T(2,128)}, f32[48,96]{1,0:T(8,128)}, f32[2,192]{1,0:T(2,128)}) custom-call(s32[1]{0:T(128)} %bitcast.22.parity_ref, f32[144,128]{1,0:T(8,128)S(1)} %slice_add_fusion.mine_ref, f32[144,128]{1,0:T(8,128)S(1)} %collective-permute-done.8.other_ref, f32[40,128]{1,0:T(8,128)S(1)} %bitcast_add_fusion.5.weights_ref, ...), custom_call_target="tpu_custom_call" | custom-call | tf_op jit(solution)/shard_map/pallas_call | solution.py:608
  (31 shorter events, 0.4 us)
Async XLA Ops:
  1.8 11.5 %collective-permute-start = (f32[3,2,72,128]{3,2,1,0:T(8,128)S(1)}, f32[3,2,72,128]{3,2,1,0:T(8,128)S(1)}, u32[]{:S(2)}, u32[]{:S(2)}) collective-permute-start(f32[3,2,72,128]{3,2,1,0:T(8,128)S(1)} %shard_map.102), channel_id=1, source_target_pairs={{0,1},{1,2},{2,3},{3,4},{4,5},{5,6},{6,7},{7,0},{8,9},{9,10},{10,1... | collective-permute-start | bytes 663560 | tf_op jit(solution)/shard_map/ppermute | solution.py:523
  20.1 2.0 %collective-permute-start.1 = (f32[648,128]{1,0:T(8,128)S(1)}, f32[648,128]{1,0:T(8,128)S(1)}, u32[]{:S(2)}, u32[]{:S(2)}) collective-permute-start(f32[648,128]{1,0:T(8,128)S(1)} %pad_maximum_fusion), channel_id=1, source_target_pairs={{0,8},{1,9},{2,10},{3,11},{4,12},{5,13},{6,14},{7,15},{8,0},{9,1},... | collective-permute-start | bytes 995336 | tf_op jit(solution)/shard_map/ppermute | solution.py:452
  21.4 5.3 %collective-permute-start.3 = (f32[144,128]{1,0:T(8,128)S(1)}, f32[144,128]{1,0:T(8,128)S(1)}, u32[]{:S(2)}, u32[]{:S(2)}) collective-permute-start(f32[144,128]{1,0:T(8,128)S(1)} %dynamic-slice_bitcast_fusion), channel_id=1, source_target_pairs={{0,4},{1,5},{2,6},{3,7},{4,0},{5,1},{6,2},{7,3},{8,9},{9,8},{10,11... | collective-permute-start | bytes 221192 | tf_op jit(solution)/shard_map/ppermute | solution.py:452
  22.3 5.4 %collective-permute-start.2 = (f32[328,128]{1,0:T(8,128)S(1)}, f32[328,128]{1,0:T(8,128)S(1)}, u32[]{:S(2)}, u32[]{:S(2)}) collective-permute-start(f32[328,128]{1,0:T(8,128)S(1)} %pad_maximum_fusion.1), channel_id=1, source_target_pairs={{0,16},{1,17},{2,18},{3,19},{4,20},{5,21},{6,22},{7,23},{8,9},{9,8... | collective-permute-start | bytes 503816 | tf_op jit(solution)/shard_map/ppermute | solution.py:452
  27.8 5.3 %collective-permute-start.4 = (f32[312,128]{1,0:T(8,128)S(1)}, f32[312,128]{1,0:T(8,128)S(1)}, u32[]{:S(2)}, u32[]{:S(2)}) collective-permute-start(f32[312,128]{1,0:T(8,128)S(1)} %pad_maximum_fusion.2), channel_id=1, source_target_pairs={{0,1},{1,0},{2,3},{3,2},{4,5},{5,4},{6,7},{7,6},{8,10},{9,11},{10,... | collective-permute-start | bytes 479240 | tf_op jit(solution)/shard_map/ppermute | solution.py:452
  33.3 5.7 %collective-permute-start.5 = (f32[232,128]{1,0:T(8,128)S(1)}, f32[232,128]{1,0:T(8,128)S(1)}, u32[]{:S(2)}, u32[]{:S(2)}) collective-permute-start(f32[232,128]{1,0:T(8,128)S(1)} %pad_maximum_fusion.3), channel_id=1, source_target_pairs={{0,2},{1,3},{2,0},{3,1},{4,6},{5,7},{6,4},{7,5},{8,12},{9,13},{10,... | collective-permute-start | bytes 356360 | tf_op jit(solution)/shard_map/ppermute | solution.py:452
  34.9 9.0 %collective-permute-start.7 = (f32[3,72,128]{2,1,0:T(8,128)S(1)}, f32[3,72,128]{2,1,0:T(8,128)S(1)}, u32[]{:S(2)}, u32[]{:S(2)}) collective-permute-start(f32[3,72,128]{2,1,0:T(8,128)S(1)} %get-tuple-element.30), channel_id=1, source_target_pairs={{0,7},{1,0},{2,1},{3,2},{4,3},{5,4},{6,5},{7,6},{8,15},{9,8},{10,9... | collective-permute-start | bytes 331784 | tf_op jit(solution)/shard_map/ppermute | solution.py:588
  39.0 4.8 %collective-permute-start.6 = (f32[48,128]{1,0:T(8,128)S(1)}, f32[48,128]{1,0:T(8,128)S(1)}, u32[]{:S(2)}, u32[]{:S(2)}) collective-permute-start(f32[48,128]{1,0:T(8,128)S(1)} %pad_maximum_fusion.4), channel_id=1, source_target_pairs={{0,4},{1,5},{2,6},{3,7},{4,0},{5,1},{6,2},{7,3},{8,24},{9,25},{10,... | collective-permute-start | bytes 73736 | tf_op jit(solution)/shard_map/ppermute | solution.py:452
  40.5 5.3 %collective-permute-start.8 = (f32[144,128]{1,0:T(8,128)S(1)}, f32[144,128]{1,0:T(8,128)S(1)}, u32[]{:S(2)}, u32[]{:S(2)}) collective-permute-start(f32[144,128]{1,0:T(8,128)S(1)} %slice_add_fusion.mine_ref), channel_id=1, source_target_pairs={{0,4},{1,5},{2,6},{3,7},{4,0},{5,1},{6,2},{7,3},{8,9},{9,8},{10,11... | collective-permute-start | bytes 221192 | tf_op jit(solution)/shard_map/ppermute | solution.py:452

commit v8 on v7

--- a/solution.py
+++ b/solution.py
@@ -575,6 +575,7 @@
         out_specs=whole(1)[0],
         scratch_shapes=[pltpu.VMEM((LEVELS * PADDED, PW * HEADS * OFFSETS), f32)],
         compiler_params=params,
+        cost_estimate=pl.CostEstimate(flops=1_300_000_000, bytes_accessed=400_000, transcendentals=0),
     )(strips, pairs, offsets)
     core_step, steps, strip_step = summing_steps(lat_count, lon_count)
     norm = jnp.where(lax.axis_index("lat") & 2 == 0, norm, jnp.roll(norm, 4, 0))
@@ -602,6 +603,7 @@
         in_specs=whole(2),
         out_specs=whole(1)[0],
         compiler_params=params,
+        cost_estimate=pl.CostEstimate(flops=0, bytes_accessed=3_600_000, transcendentals=0),
     )(grad_own, returned).transpose(2, 0, 1, 3)
     chunk = weights if packed else jnp.zeros((40, 128), f32)
     parity = side(*strip_step)[None]

time: 46.9 us -> 46.9 us (level)
  no operation moved by 1% of the time
where the time goes in v8:
time: 46.9 us; the launch traced here: 46.8 us
  waiting for transfers between devices  18.6 us (40%)
  Pallas kernels  14.5 us (31%)
  starting transfers between devices  12.3 us (26%)
  between operations  0.88 us (2%)
    ppermute x7, waiting for transfers between devices, exchanged(): return lax.ppermute(value, ('lat', 'lon'), partners(*step))  13.8 us
    ppermute x7, starting transfers between devices, exchanged(): return lax.ppermute(value, ('lat', 'lon'), partners(*step))  7.73 us
    pallas_call x1, Pallas kernels, shards(): pl.pallas_call(functools.partial(block_kernel, factor, packed), out_shape...  6.81 us
    ppermute x1, waiting for transfers between devices, shards(): lax.ppermute(sent, 'lon', [(s, (s + 1) % lon_count) for s in range(lon_co...  4.88 us
    pallas_call x1, Pallas kernels, shards(): pl.pallas_call(prepare_kernel, out_shape=(pltpu.VMEM((PW, GROUP_ROWS * HE...  3.58 us
    ppermute x1, starting transfers between devices, shards(): lax.ppermute(sent, 'lon', [(s, (s + 1) % lon_count) for s in range(lon_co...  3.02 us
    ppermute x1, starting transfers between devices, shards(): lax.ppermute(grad_borrowed, 'lon', [(s, (s - 1) % lon_count) for s in ran...  1.58 us
    pallas_call x1, Pallas kernels, shards(): pl.pallas_call(turn_kernel, out_shape=rows_shape, in_specs=whole(3), out_...  1.13 us
  transfers between devices with their start and end apart: 9, of which 7 were waited for; matrix products, arithmetic and copies ran while one was open for 0% of the time, Pallas kernels for 12%

profile of v8, /device:TPU:0, one launch (start us, length us, event | category | flops | bytes accessed | tf_op | source)
XLA Modules:
  0.0 46.8 jit_solution(16266936487949143152)
XLA Ops:
  0.6 1.1 %shard_map.102 = f32[3,2,72,128]{3,2,1,0:T(8,128)S(1)} custom-call(f32[6,12,4,192]{3,2,1,0:T(4,128)} %bitcast.38, f32[6,12,4,192]{3,2,1,0:T(4,128)} %bitcast.40), custom_call_target="tpu_custom_call" | custom-call | tf_op jit(solution)/shard_map/pallas_call | solution.py:515
  1.8 3.0 %collective-permute-start = (f32[3,2,72,128]{3,2,1,0:T(8,128)S(1)}, f32[3,2,72,128]{3,2,1,0:T(8,128)S(1)}, u32[]{:S(2)}, u32[]{:S(2)}) collective-permute-start(f32[3,2,72,128]{3,2,1,0:T(8,128)S(1)} %shard_map.102), channel_id=1, source_target_pairs={{0,1},{1,2},{2,3},{3,4},{4,5},{5,6},{6,7},{7,0},{8,9},{9,10},{10,1... | collective-permute-start | bytes 663560 | tf_op jit(solution)/shard_map/ppermute | solution.py:523
  4.8 3.6 %shard_map.103 = (f32[2,288,384]{2,1,0:T(8,128)S(1)}, f32[8,144,192]{2,1,0:T(8,128)S(1)}, f32[2,192]{1,0:T(2,128)S(1)}, f32[4,192,192]{2,1,0:T(8,128)S(1)}, bf16...) custom-call(f32[6,23,2,144]{3,2,1,0:T(2,128)} %bitcast.47, f32[6,12,4,192]{3,2,1,0:T(4,128)} %bitcast.39, ...), custom_call_target="tpu_custom_call" | custom-call | tf_op jit(solution)/shard_map/pallas_call | solution.py:529
  8.4 4.9 %collective-permute-done.borrowed_ref = f32[3,2,72,128]{3,2,1,0:T(8,128)S(1)} collective-permute-done((f32[3,2,72,128]{3,2,1,0:T(8,128)S(1)}, f32[3,2,72,128]{3,2,1,0:T(8,128)S(1)}, u32[]{:S(2)}, u32[]{:S(2)}) %collective-permute-start) | collective-permute-done | bytes 221216 | tf_op jit(solution)/shard_map/ppermute | solution.py:523
  13.2 6.8 %shard_map.104 = (f32[3,72,128]{2,1,0:T(8,128)S(1)}, f32[3,72,128]{2,1,0:T(8,128)S(1)}, f32[2,2,2,2,2,40,128]{6,5,4,3,2,1,0:T(8,128)S(1)}, f32[192,288]{1,0:T(8,128)S(1)}, f32[8,128]{1,0:T(8,128)S(1)}) custom-call(f32[3,2,72,128]{3,2,1,0:T(8,128)S(1)} %collective-permute-done.borrowed_ref, f32[8,144,192]{2,1,0:T(8,128)S(1)} %get-tuple-element.20.projected_ref, ...), custom_call_target="tpu_custom_call" | custom-call | tf_op jit(solution)/shard_map/pallas_call | solution.py:554
  20.1 0.1 collective-permute-start.1
  20.3 1.1 %shard_map.105 = f32[2,144,128]{2,1,0:T(8,128)S(1)} custom-call(f32[192,288]{1,0:T(8,128)S(1)} %get-tuple-element.27.strip_ref, bf16[192,144]{1,0:T(8,128)(2,1)S(1)} %get-tuple-element.28.pairs_ref, bf16[288,288]{1,0:T(8,128)(2,1)S(1)} %get-tuple-element.29.offsets_ref), custom_call_target="tpu_custom_call" | custom-call | flops 1300000000 | bytes 400000 | tf_op jit(solution)/shard_map/pallas_call | solution.py:571
  21.4 0.7 %collective-permute-start.3 = (f32[144,128]{1,0:T(8,128)S(1)}, f32[144,128]{1,0:T(8,128)S(1)}, u32[]{:S(2)}, u32[]{:S(2)}) collective-permute-start(f32[144,128]{1,0:T(8,128)S(1)} %dynamic-slice_bitcast_fusion), channel_id=1, source_target_pairs={{0,4},{1,5},{2,6},{3,7},{4,0},{5,1},{6,2},{7,3},{8,9},{9,8},{10,11... | collective-permute-start | bytes 221192 | tf_op jit(solution)/shard_map/ppermute | solution.py:452
  22.2 0.0 collective-permute-done.1
  22.3 1.6 %collective-permute-start.2 = (f32[328,128]{1,0:T(8,128)S(1)}, f32[328,128]{1,0:T(8,128)S(1)}, u32[]{:S(2)}, u32[]{:S(2)}) collective-permute-start(f32[328,128]{1,0:T(8,128)S(1)} %pad_maximum_fusion.1), channel_id=1, source_target_pairs={{0,16},{1,17},{2,18},{3,19},{4,20},{5,21},{6,22},{7,23},{8,9},{9,8... | collective-permute-start | bytes 503816 | tf_op jit(solution)/shard_map/ppermute | solution.py:452
  23.8 2.9 %collective-permute-done.3 = f32[144,128]{1,0:T(8,128)S(1)} collective-permute-done((f32[144,128]{1,0:T(8,128)S(1)}, f32[144,128]{1,0:T(8,128)S(1)}, u32[]{:S(2)}, u32[]{:S(2)}) %collective-permute-start.3) | collective-permute-done | bytes 73760 | tf_op jit(solution)/shard_map/ppermute | solution.py:452
  26.7 1.0 %collective-permute-done.2 = f32[328,128]{1,0:T(8,128)S(1)} collective-permute-done((f32[328,128]{1,0:T(8,128)S(1)}, f32[328,128]{1,0:T(8,128)S(1)}, u32[]{:S(2)}, u32[]{:S(2)}) %collective-permute-start.2) | collective-permute-done | bytes 167968 | tf_op jit(solution)/shard_map/ppermute | solution.py:452
  27.8 0.7 %collective-permute-start.4 = (f32[312,128]{1,0:T(8,128)S(1)}, f32[312,128]{1,0:T(8,128)S(1)}, u32[]{:S(2)}, u32[]{:S(2)}) collective-permute-start(f32[312,128]{1,0:T(8,128)S(1)} %pad_maximum_fusion.2), channel_id=1, source_target_pairs={{0,1},{1,0},{2,3},{3,2},{4,5},{5,4},{6,7},{7,6},{8,10},{9,11},{10,... | collective-permute-start | bytes 479240 | tf_op jit(solution)/shard_map/ppermute | solution.py:452
  28.5 4.7 %collective-permute-done.4 = f32[312,128]{1,0:T(8,128)S(1)} collective-permute-done((f32[312,128]{1,0:T(8,128)S(1)}, f32[312,128]{1,0:T(8,128)S(1)}, u32[]{:S(2)}, u32[]{:S(2)}) %collective-permute-start.4) | collective-permute-done | bytes 159776 | tf_op jit(solution)/shard_map/ppermute | solution.py:452
  33.3 1.6 %collective-permute-start.5 = (f32[232,128]{1,0:T(8,128)S(1)}, f32[232,128]{1,0:T(8,128)S(1)}, u32[]{:S(2)}, u32[]{:S(2)}) collective-permute-start(f32[232,128]{1,0:T(8,128)S(1)} %pad_maximum_fusion.3), channel_id=1, source_target_pairs={{0,2},{1,3},{2,0},{3,1},{4,6},{5,7},{6,4},{7,5},{8,12},{9,13},{10,... | collective-permute-start | bytes 356360 | tf_op jit(solution)/shard_map/ppermute | solution.py:452
  34.9 1.6 %collective-permute-start.7 = (f32[3,72,128]{2,1,0:T(8,128)S(1)}, f32[3,72,128]{2,1,0:T(8,128)S(1)}, u32[]{:S(2)}, u32[]{:S(2)}) collective-permute-start(f32[3,72,128]{2,1,0:T(8,128)S(1)} %get-tuple-element.30), channel_id=1, source_target_pairs={{0,7},{1,0},{2,1},{3,2},{4,3},{5,4},{6,5},{7,6},{8,15},{9,8},{10,9... | collective-permute-start | bytes 331784 | tf_op jit(solution)/shard_map/ppermute | solution.py:589
  36.5 2.5 %collective-permute-done.5 = f32[232,128]{1,0:T(8,128)S(1)} collective-permute-done((f32[232,128]{1,0:T(8,128)S(1)}, f32[232,128]{1,0:T(8,128)S(1)}, u32[]{:S(2)}, u32[]{:S(2)}) %collective-permute-start.5) | collective-permute-done | bytes 118816 | tf_op jit(solution)/shard_map/ppermute | solution.py:452
  39.1 1.5 %collective-permute-start.6 = (f32[48,128]{1,0:T(8,128)S(1)}, f32[48,128]{1,0:T(8,128)S(1)}, u32[]{:S(2)}, u32[]{:S(2)}) collective-permute-start(f32[48,128]{1,0:T(8,128)S(1)} %pad_maximum_fusion.4), channel_id=1, source_target_pairs={{0,4},{1,5},{2,6},{3,7},{4,0},{5,1},{6,2},{7,3},{8,24},{9,25},{10,... | collective-permute-start | bytes 73736 | tf_op jit(solution)/shard_map/ppermute | solution.py:452
  40.6 1.6 %collective-permute-start.8 = (f32[144,128]{1,0:T(8,128)S(1)}, f32[144,128]{1,0:T(8,128)S(1)}, u32[]{:S(2)}, u32[]{:S(2)}) collective-permute-start(f32[144,128]{1,0:T(8,128)S(1)} %slice_add_fusion.mine_ref), channel_id=1, source_target_pairs={{0,4},{1,5},{2,6},{3,7},{4,0},{5,1},{6,2},{7,3},{8,9},{9,8},{10,11... | collective-permute-start | bytes 221192 | tf_op jit(solution)/shard_map/ppermute | solution.py:452
  42.1 1.7 %collective-permute-done.6 = f32[48,128]{1,0:T(8,128)S(1)} collective-permute-done((f32[48,128]{1,0:T(8,128)S(1)}, f32[48,128]{1,0:T(8,128)S(1)}, u32[]{:S(2)}, u32[]{:S(2)}) %collective-permute-start.6) | collective-permute-done | bytes 24608 | tf_op jit(solution)/shard_map/ppermute | solution.py:452
  43.9 0.0 collective-permute-done.7.returned_ref
  43.9 1.0 %shard_map.106 = f32[6,12,4,192]{3,2,1,0:T(4,128)} custom-call(f32[3,72,128]{2,1,0:T(8,128)S(1)} %get-tuple-element.24.own_ref, f32[3,72,128]{2,1,0:T(8,128)S(1)} %collective-permute-done.7.returned_ref), custom_call_target="tpu_custom_call" | custom-call | bytes 3600000 | tf_op jit(solution)/shard_map/pallas_call | solution.py:600
  44.9 1.0 %collective-permute-done.8.other_ref = f32[144,128]{1,0:T(8,128)S(1)} collective-permute-done((f32[144,128]{1,0:T(8,128)S(1)}, f32[144,128]{1,0:T(8,128)S(1)}, u32[]{:S(2)}, u32[]{:S(2)}) %collective-permute-start.8) | collective-permute-done | bytes 73760 | tf_op jit(solution)/shard_map/ppermute | solution.py:452
  45.9 0.9 %shard_map.107 = (f32[6,23,2,144]{3,2,1,0:T(2,128)}, f32[48,96]{1,0:T(8,128)}, f32[2,192]{1,0:T(2,128)}) custom-call(s32[1]{0:T(128)} %bitcast.22.parity_ref, f32[144,128]{1,0:T(8,128)S(1)} %slice_add_fusion.mine_ref, f32[144,128]{1,0:T(8,128)S(1)} %collective-permute-done.8.other_ref, f32[40,128]{1,0:T(8,128)S(1)} %bitcast_add_fusion.5.weights_ref, ...), custom_call_target="tpu_custom_call" | custom-call | tf_op jit(solution)/shard_map/pallas_call | solution.py:610
  (31 shorter events, 0.4 us)
Async XLA Ops:
  1.8 11.5 %collective-permute-start = (f32[3,2,72,128]{3,2,1,0:T(8,128)S(1)}, f32[3,2,72,128]{3,2,1,0:T(8,128)S(1)}, u32[]{:S(2)}, u32[]{:S(2)}) collective-permute-start(f32[3,2,72,128]{3,2,1,0:T(8,128)S(1)} %shard_map.102), channel_id=1, source_target_pairs={{0,1},{1,2},{2,3},{3,4},{4,5},{5,6},{6,7},{7,0},{8,9},{9,10},{10,1... | collective-permute-start | bytes 663560 | tf_op jit(solution)/shard_map/ppermute | solution.py:523
  20.1 2.0 %collective-permute-start.1 = (f32[648,128]{1,0:T(8,128)S(1)}, f32[648,128]{1,0:T(8,128)S(1)}, u32[]{:S(2)}, u32[]{:S(2)}) collective-permute-start(f32[648,128]{1,0:T(8,128)S(1)} %pad_maximum_fusion), channel_id=1, source_target_pairs={{0,8},{1,9},{2,10},{3,11},{4,12},{5,13},{6,14},{7,15},{8,0},{9,1},... | collective-permute-start | bytes 995336 | tf_op jit(solution)/shard_map/ppermute | solution.py:452
  21.4 5.3 %collective-permute-start.3 = (f32[144,128]{1,0:T(8,128)S(1)}, f32[144,128]{1,0:T(8,128)S(1)}, u32[]{:S(2)}, u32[]{:S(2)}) collective-permute-start(f32[144,128]{1,0:T(8,128)S(1)} %dynamic-slice_bitcast_fusion), channel_id=1, source_target_pairs={{0,4},{1,5},{2,6},{3,7},{4,0},{5,1},{6,2},{7,3},{8,9},{9,8},{10,11... | collective-permute-start | bytes 221192 | tf_op jit(solution)/shard_map/ppermute | solution.py:452
  22.3 5.4 %collective-permute-start.2 = (f32[328,128]{1,0:T(8,128)S(1)}, f32[328,128]{1,0:T(8,128)S(1)}, u32[]{:S(2)}, u32[]{:S(2)}) collective-permute-start(f32[328,128]{1,0:T(8,128)S(1)} %pad_maximum_fusion.1), channel_id=1, source_target_pairs={{0,16},{1,17},{2,18},{3,19},{4,20},{5,21},{6,22},{7,23},{8,9},{9,8... | collective-permute-start | bytes 503816 | tf_op jit(solution)/shard_map/ppermute | solution.py:452
  27.8 5.3 %collective-permute-start.4 = (f32[312,128]{1,0:T(8,128)S(1)}, f32[312,128]{1,0:T(8,128)S(1)}, u32[]{:S(2)}, u32[]{:S(2)}) collective-permute-start(f32[312,128]{1,0:T(8,128)S(1)} %pad_maximum_fusion.2), channel_id=1, source_target_pairs={{0,1},{1,0},{2,3},{3,2},{4,5},{5,4},{6,7},{7,6},{8,10},{9,11},{10,... | collective-permute-start | bytes 479240 | tf_op jit(solution)/shard_map/ppermute | solution.py:452
  33.3 5.7 %collective-permute-start.5 = (f32[232,128]{1,0:T(8,128)S(1)}, f32[232,128]{1,0:T(8,128)S(1)}, u32[]{:S(2)}, u32[]{:S(2)}) collective-permute-start(f32[232,128]{1,0:T(8,128)S(1)} %pad_maximum_fusion.3), channel_id=1, source_target_pairs={{0,2},{1,3},{2,0},{3,1},{4,6},{5,7},{6,4},{7,5},{8,12},{9,13},{10,... | collective-permute-start | bytes 356360 | tf_op jit(solution)/shard_map/ppermute | solution.py:452
  34.9 9.0 %collective-permute-start.7 = (f32[3,72,128]{2,1,0:T(8,128)S(1)}, f32[3,72,128]{2,1,0:T(8,128)S(1)}, u32[]{:S(2)}, u32[]{:S(2)}) collective-permute-start(f32[3,72,128]{2,1,0:T(8,128)S(1)} %get-tuple-element.30), channel_id=1, source_target_pairs={{0,7},{1,0},{2,1},{3,2},{4,3},{5,4},{6,5},{7,6},{8,15},{9,8},{10,9... | collective-permute-start | bytes 331784 | tf_op jit(solution)/shard_map/ppermute | solution.py:589
  39.1 4.8 %collective-permute-start.6 = (f32[48,128]{1,0:T(8,128)S(1)}, f32[48,128]{1,0:T(8,128)S(1)}, u32[]{:S(2)}, u32[]{:S(2)}) collective-permute-start(f32[48,128]{1,0:T(8,128)S(1)} %pad_maximum_fusion.4), channel_id=1, source_target_pairs={{0,4},{1,5},{2,6},{3,7},{4,0},{5,1},{6,2},{7,3},{8,24},{9,25},{10,... | collective-permute-start | bytes 73736 | tf_op jit(solution)/shard_map/ppermute | solution.py:452
  40.6 5.3 %collective-permute-start.8 = (f32[144,128]{1,0:T(8,128)S(1)}, f32[144,128]{1,0:T(8,128)S(1)}, u32[]{:S(2)}, u32[]{:S(2)}) collective-permute-start(f32[144,128]{1,0:T(8,128)S(1)} %slice_add_fusion.mine_ref), channel_id=1, source_target_pairs={{0,4},{1,5},{2,6},{3,7},{4,0},{5,1},{6,2},{7,3},{8,9},{9,8},{10,11... | collective-permute-start | bytes 221192 | tf_op jit(solution)/shard_map/ppermute | solution.py:452
